TPU v7x, 256 devices: a whole 4x4x8 slice. The times are simulated.
256 devices in a mesh: dp: 8 (over z), seq: 32 (over x, y, core).
Axes of the slice: x: 4, y: 4, z: 8, core: 2. Of those that a mesh axis runs over, the one named last changes fastest.
Arguments:
- inputs: bfloat16 [8, 4096, 2048], P('dp', 'seq'), may hold values from -20 to 20
- queries: bfloat16 [8, 4096, 1024], P('dp', 'seq'), may hold values from -0.5 to 0.5
- values: bfloat16 [8, 4096, 1024], P('dp', 'seq'), may hold values from -6 to 6
- out_grad: bfloat16 [8, 4096, 1024], P('dp', 'seq'), may hold values from -0.09375 to 0.09375
- key_weight: bfloat16 [2048, 1024], P(('dp', 'seq')), may hold values from -0.125 to 0.125
- gate_down: bfloat16 [16, 2048], replicated, may hold values from -1 to 1
- gate_up: bfloat16 [16, 1024], replicated, may hold values from -1.5 to 1.5
- gate_bias: float32 [1024], replicated, may hold values from -1 to 14
Outputs:
- input_grad: bfloat16 [8, 4096, 2048], P('dp', 'seq')
- gate_grad: bfloat16 [8, 4096, 1024], P('dp', 'seq')
- key_weight_grad: float32 [2048, 1024], P(('dp', 'seq'))
- down_grad: float32 [16, 2048], replicated
- up_grad: float32 [16, 1024], replicated
All inputs are finite; a program needn't handle non-finite values.
Results may differ from a plain program's by a relative error of at most 0.017.
Values may be sent and summed in bfloat16 or wider, within the bound.
No kernel may reach another device: no remote copies, remote signals or barrier semaphores. Data moves between devices by JAX's collectives and lax.ppermute only.
A program may use at most 128 MiB of HBM per device.

v0:
```python
import jax
import jax.numpy as jnp
from jax import lax
from jax.sharding import PartitionSpec as P

HEADS = 8
DK = 128
GROUP = 64


PRECISION_LEVEL = lax.Precision.HIGHEST


def carried_in(part, axis, combine, identity, reverse):
    count = lax.axis_size(axis)
    place = lax.axis_index(axis)
    ahead = count - 1 - place if reverse else place
    gathered = jax.tree.map(lambda a: lax.all_gather(a, axis), part)
    state = jax.tree.map(lambda a, e: jnp.zeros_like(a) + jnp.asarray(e, a.dtype), part, identity)

    def one(step, state):
        source = count - 1 - step if reverse else step
        return combine(
            state, jax.tree.map(lambda a: lax.dynamic_index_in_dim(a, source, 0, False), gathered)
        )

    return lax.fori_loop(0, ahead, one, state)


def link_states(earlier, later):
    return (earlier[0] * later[0], later[0][..., None] * earlier[1] + later[1])


def add_totals(earlier, later):
    return earlier + later


def local(inputs, queries, values, out_grad, key_weight, gate_down, gate_up, gate_bias):
    tokens = inputs[0]
    count = tokens.shape[0]
    width = key_weight.shape[1]
    blocks = count // GROUP
    shape = (blocks, GROUP, HEADS, DK)
    whole_keyw = lax.all_gather(key_weight, ("dp", "seq"), axis=0, tiled=True)
    keys_f32 = jnp.dot(tokens, whole_keyw, preferred_element_type=jnp.float32)
    keys = keys_f32.astype(jnp.bfloat16)
    latent = lax.dot_general(
        tokens, gate_down, (((1,), (1,)), ((), ())), preferred_element_type=jnp.float32
    ).astype(jnp.bfloat16)
    logits = jnp.dot(latent, gate_up, preferred_element_type=jnp.float32) + gate_bias
    gamma = jax.nn.log_sigmoid(logits) / 16.0
    rows_idx = lax.broadcasted_iota(jnp.int32, (GROUP, GROUP), 0)
    cols_idx = lax.broadcasted_iota(jnp.int32, (GROUP, GROUP), 1)
    lower = (rows_idx >= cols_idx).astype(jnp.float32)
    query_f = queries[0].reshape(shape).astype(jnp.float32)
    key_f = keys.reshape(shape).astype(jnp.float32)
    value_f = values[0].reshape(shape).astype(jnp.float32)
    grad_f = out_grad[0].reshape(shape).astype(jnp.float32)
    beta = jnp.einsum("ij,njhk->nihk", lower, gamma.reshape(shape), precision=PRECISION_LEVEL)
    span = beta[:, -1]
    before = jnp.cumsum(span, axis=0) - span
    total_log = jnp.sum(span, axis=0)
    after = total_log[None] - before - span
    query_scaled = query_f * jnp.exp(beta)
    key_scaled = key_f * jnp.exp(-beta)
    key_tail = key_f * jnp.exp(span[:, None] - beta)
    zeros = jnp.zeros((HEADS, DK, DK), jnp.float32)

    def forward(carried_state, item):
        tail_rows, value_rows, step_index = item
        next_piece = jnp.exp(step_index)[..., None] * carried_state + jnp.einsum(
            "qex,qen->exn", tail_rows, value_rows, precision=PRECISION_LEVEL
        )
        return (next_piece, carried_state)

    end_state, states_local = lax.scan(forward, zeros, (key_tail, value_f, span))

    def backward(gradient_term, item):
        scaled_rows, output_gradient, step_index = item
        current_piece = jnp.exp(step_index)[..., None] * gradient_term + jnp.einsum(
            "qex,qen->exn", scaled_rows, output_gradient, precision=PRECISION_LEVEL
        )
        return (current_piece, gradient_term)

    start_grad, grads_local = lax.scan(backward, zeros, (query_scaled, grad_f, span), reverse=True)
    decay = jnp.exp(total_log)
    identity = (jnp.ones_like(decay), jnp.zeros_like(end_state))
    incoming = carried_in((decay, end_state), "seq", link_states, identity, False)[1]
    outgoing = carried_in((decay, start_grad), "seq", link_states, identity, True)[1]
    states = states_local + jnp.exp(before)[..., None] * incoming[None]
    grads = grads_local + jnp.exp(after)[..., None] * outgoing[None]
    upper = jnp.transpose(lower)
    pairs = (
        jnp.einsum("nihv,njhv->nhij", grad_f, value_f, precision=PRECISION_LEVEL)
        * lower[None, None]
    )
    query_delta = jnp.exp(beta) * (
        jnp.einsum("nhkv,nihv->nihk", states, grad_f, precision=PRECISION_LEVEL)
        + jnp.einsum("nhij,njhk->nihk", pairs, key_scaled, precision=PRECISION_LEVEL)
    )
    key_delta = jnp.exp(span[:, None] - beta) * jnp.einsum(
        "nhkv,njhv->njhk", grads, value_f, precision=PRECISION_LEVEL
    ) + jnp.exp(-beta) * jnp.einsum(
        "nhij,nihk->njhk", pairs, query_scaled, precision=PRECISION_LEVEL
    )
    gate_delta = query_f * query_delta - key_f * key_delta
    within = jnp.einsum("ij,njhk->nihk", upper, gate_delta, precision=PRECISION_LEVEL)
    group_sums = within[:, 0]
    later = jnp.cumsum(group_sums[::-1], axis=0)[::-1] - group_sums
    own_total = jnp.sum(group_sums, axis=0).reshape(width)
    beyond = carried_in(own_total, "seq", add_totals, jnp.zeros_like(own_total), True)
    suffix = within + later[:, None] + beyond.reshape(HEADS, DK)[None, None]
    gate_grad = (suffix.reshape(count, width) * jax.nn.sigmoid(-logits) / 16.0).astype(jnp.bfloat16)
    key_bf = key_delta.reshape(count, width).astype(jnp.bfloat16)
    key_weight_grad = lax.psum_scatter(
        lax.dot_general(
            tokens, key_bf, (((0,), (0,)), ((), ())), preferred_element_type=jnp.float32
        ),
        ("dp", "seq"),
        scatter_dimension=0,
        tiled=True,
    )
    up_part = lax.dot_general(
        latent, gate_grad, (((0,), (0,)), ((), ())), preferred_element_type=jnp.float32
    )
    latent_delta = lax.dot_general(
        gate_grad, gate_up, (((1,), (1,)), ((), ())), preferred_element_type=jnp.float32
    ).astype(jnp.bfloat16)
    down_part = lax.dot_general(
        latent_delta, tokens, (((0,), (0,)), ((), ())), preferred_element_type=jnp.float32
    )
    down_grad, up_grad = lax.psum((down_part, up_part), ("dp", "seq"))
    through_gate = jnp.dot(latent_delta, gate_down, preferred_element_type=jnp.float32)
    through_keys = lax.dot_general(
        key_bf, whole_keyw, (((1,), (1,)), ((), ())), preferred_element_type=jnp.float32
    )
    input_grad = (through_keys + through_gate).astype(jnp.bfloat16)
    return (input_grad[None], gate_grad[None], key_weight_grad, down_grad, up_grad)


def solution(mesh):
    in_specs = (
        P("dp", "seq", None),
        P("dp", "seq", None),
        P("dp", "seq", None),
        P("dp", "seq", None),
        P(("dp", "seq"), None),
        P(),
        P(),
        P(),
    )
    out_specs = (P("dp", "seq", None), P("dp", "seq", None), P(("dp", "seq"), None), P(), P())
    return jax.shard_map(local, mesh=mesh, in_specs=in_specs, out_specs=out_specs, check_vma=False)
```

profile of v0, /device:TPU:1, one launch (start us, length us, event | category | flops | bytes accessed | tf_op | source)
XLA Modules:
  0.0 1904.1 jit_solution(16890864303596063495)
XLA Ops:
  8.2 1.1 convolution_convert_fusion.2
  9.3 1.0 convolution_add_fusion.4
  14.2 116.9 %all-gather.8.cloned.1.call-done = bf16[2048,1024]{1,0:T(8,128)(2,1)} async-done(((bf16[8,1024]{1,0:T(8,128)(2,1)}), bf16[2048,1024]{1,0:T(8,128)(2,1)}) %all-gather.8.cloned.1.call-update) | async-done | bytes 4194320 | tf_op jit(solution)/shard_map/all_gather | solution.py:44
  131.2 2.9 fusion.16
  134.2 2.1 fusion.38
  136.2 1.1 broadcast.25.clone
  137.3 4.1 while.71
  138.3 1.2 convolution_add_fusion.7
  140.3 1.2 convolution_add_fusion.7
  143.4 1.1 broadcast.25.clone.1
  144.5 6.0 while.72
  145.4 2.1 convolution_add_fusion.8
  148.4 2.1 convolution_add_fusion.8
  151.5 24.1 %all-gather = f32[256,128]{1,0:T(8,128)S(1)} all-gather(f32[8,128]{1,0:T(8,128)S(1)} %exp.77), channel_id=2, replica_groups=mesh['dp'=8,'seq'=32] {'seq'}, dimensions={0}, use_global_device_ids=true | all-gather | bytes 135168 | tf_op jit(solution)/shard_map/all_gather | solution.py:18
  176.2 1.2 convolution_multiply_fusion
  177.4 1.8 fusion.14
  179.2 1.6 fusion.32
  180.7 36.6 %all-gather.10.cloned.1.call-done = f32[256,128,128]{2,1,0:T(8,128)} async-done(((f32[8,128,128]{2,1,0:T(8,128)}), f32[256,128,128]{2,1,0:T(8,128)}) %all-gather.10.cloned.1.call-update) | async-done | bytes 16777232 | tf_op jit(solution)/shard_map/all_gather | solution.py:18
  217.4 41.1 %while.68 = (s32[]{:T(128)}, f32[8,128,128]{2,1,0:T(8,128)S(1)}, s32[]{:T(128)}, f32[32,8,128]{2,1,0:T(8,128)S(1)}, f32[32,8,128,128]{3,2,1,0:T(8,128)}, /*index=5*/s32[]{:T(128)}, s32[]{:T(128)}, s32[]{:T(128)}, s32[]{:T(128)}) while((s32[]{:T(128)}, f32[8,128,128]{2,1,0:T(8,128)S(1)}, s32[]{:T(128)}, f32[32,8,128]{2,1,0:T(8,128)S(1)}, ...), condition=%wide.region_5.6_spmd, body=%wide.region_4.5_spmd.sunk | while | flops 262150 | bytes 1585299 | solution.py:27
  217.4 1.4 bitcast_add_fusion.4
  218.8 1.3 bitcast_add_fusion.4
  220.2 1.3 bitcast_add_fusion.4
  221.5 1.3 bitcast_add_fusion.4
  222.9 1.3 bitcast_add_fusion.4
  224.2 1.3 bitcast_add_fusion.4
  225.6 1.3 bitcast_add_fusion.4
  227.0 1.3 bitcast_add_fusion.4
  228.3 1.3 bitcast_add_fusion.4
  229.7 1.3 bitcast_add_fusion.4
  231.0 1.4 bitcast_add_fusion.4
  232.4 1.4 bitcast_add_fusion.4
  233.9 1.3 bitcast_add_fusion.4
  235.2 1.3 bitcast_add_fusion.4
  236.6 1.3 bitcast_add_fusion.4
  237.9 1.3 bitcast_add_fusion.4
  239.3 1.3 bitcast_add_fusion.4
  240.7 1.3 bitcast_add_fusion.4
  242.1 1.3 bitcast_add_fusion.4
  243.4 1.3 bitcast_add_fusion.4
  244.8 1.3 bitcast_add_fusion.4
  246.1 1.3 bitcast_add_fusion.4
  247.5 1.3 bitcast_add_fusion.4
  248.9 1.3 bitcast_add_fusion.4
  250.2 1.3 bitcast_add_fusion.4
  251.6 1.3 bitcast_add_fusion.4
  252.9 1.3 bitcast_add_fusion.4
  254.3 1.3 bitcast_add_fusion.4
  255.7 1.3 bitcast_add_fusion.4
  257.0 1.5 bitcast_add_fusion.4
  258.5 38.4 %all-gather.12.cloned.1.call-done = f32[256,128,128]{2,1,0:T(8,128)} async-done(((f32[8,128,128]{2,1,0:T(8,128)}), f32[256,128,128]{2,1,0:T(8,128)}) %all-gather.12.cloned.1.call-update) | async-done | bytes 16777232 | tf_op jit(solution)/shard_map/all_gather | solution.py:18
  297.0 1.4 while.69
  297.0 1.3 bitcast_add_fusion.5
  298.4 3.3 fusion.55
  301.7 2.9 fusion.13
  305.1 63.1 %all-gather.3 = f32[32,1,1024]{2,1,0:T(1,128)S(1)} all-gather(f32[1,1,1024]{2,1,0:T(1,128)S(1)} %bitcast.195), channel_id=1, replica_groups=mesh['dp'=8,'seq'=32] {'seq'}, dimensions={0}, use_global_device_ids=true | all-gather | bytes 135168 | tf_op jit(solution)/shard_map/all_gather | solution.py:18
  368.3 1.7 while.70
  372.6 4.5 convolution_bitcast_fusion
  377.1 9.3 copy.58
  386.4 3.7 fusion.41
  390.2 1.1 fusion.7
  391.3 224.6 %all-reduce.3.cloned.1.call-done = (f32[16,2048]{1,0:T(8,128)}, f32[16,1024]{1,0:T(8,128)}) async-done(((f32[16,2048]{1,0:T(8,128)}, f32[16,1024]{1,0:T(8,128)}), (f32[16,2048]{1,0:T(8,128)}, f32[16,1024]{1,0:T(8,128)})) %all-reduce.3.cloned.1.call-update) | async-done | bytes 196624 | tf_op jit(solution)/shard_map/psum | solution.py:132
  615.9 1278.6 %reduce-scatter.4.cloned.1.call-done = f32[8,1024]{1,0:T(8,128)} async-done(((f32[2048,1024]{1,0:T(8,128)}), f32[8,1024]{1,0:T(8,128)}) %reduce-scatter.4.cloned.1.call-update) | async-done | bytes 32784
  1894.5 1.6 copy.149
  1896.1 1.5 copy.150
  (168 shorter events, 15.8 us)
Async XLA Ops:
  7.2 1.0 copy-start
  7.2 124.0 %all-gather.8.cloned.1.call-start = ((), (), s32[]{:S(2)}) async-start(), calls=%async_computation.1 | async-start | bytes 4210688 | tf_op jit(solution)/shard_map/all_gather | solution.py:44
  7.9 209.4 %all-gather.10.cloned.1.call-start = ((), (), s32[]{:S(2)}) async-start(), calls=%async_computation.2 | async-start | bytes 17301504 | tf_op jit(solution)/shard_map/all_gather | solution.py:18
  10.3 3.3 copy-start.4
  13.6 117.5 %copy-start.6 = (bf16[16,8,8,128]{3,2,1,0:T(8,128)(2,1)}, bf16[16,8,8,128]{3,2,1,0:T(8,128)(2,1)S(1)}, u32[]{:S(2)}) copy-start(bf16[16,8,8,128]{3,2,1,0:T(8,128)(2,1)S(1)} %copy.65) | copy-start | bytes 786436
  141.5 0.8 copy-start.1
  142.3 154.6 %all-gather.12.cloned.1.call-start = ((), (), s32[]{:S(2)}) async-start(), calls=%async_computation.3 | async-start | bytes 17301504 | tf_op jit(solution)/shard_map/all_gather | solution.py:18
  150.5 0.8 copy-start.2
  151.3 464.6 %all-reduce.3.cloned.1.call-start = ((), (), s32[]{:S(2)}) async-start(), calls=%async_computation.5 | async-start | bytes 393216 | tf_op jit(solution)/shard_map/psum | solution.py:132
  217.3 84.4 %copy-start.3 = (f32[16,8,8,128]{3,2,1,0:T(8,128)S(1)}, f32[16,8,8,128]{3,2,1,0:T(8,128)}, u32[]{:S(2)}) copy-start(f32[16,8,8,128]{3,2,1,0:T(8,128)} %copy.64) | copy-start | bytes 1572868
  298.4 72.1 %copy-start.10 = (bf16[16,1024]{1,0:T(8,128)(2,1)S(1)}, bf16[16,1024]{1,0:T(8,128)(2,1)}, u32[]{:S(2)}) copy-start(bf16[16,1024]{1,0:T(8,128)(2,1)} %param.24) | copy-start | bytes 98308
  301.7 68.6 %copy-start.5 = (f32[128,1024]{1,0:T(8,128)S(1)}, f32[128,1024]{1,0:T(8,128)}, u32[]{:S(2)}) copy-start(f32[128,1024]{1,0:T(8,128)} %copy-done.4) | copy-start | bytes 1572868
  301.7 70.7 %copy-start.8 = (bf16[2,64,8,128]{3,1,2,0:T(8,128)(2,1)S(1)}, bf16[2,64,8,128]{3,1,2,0:T(8,128)(2,1)}, u32[]{:S(2)}) copy-start(bf16[2,64,8,128]{3,1,2,0:T(8,128)(2,1)} %get-tuple-element.495) | copy-start | bytes 786436
  370.5 15.9 copy-start.7
  372.5 1522.0 %reduce-scatter.4.cloned.1.call-start = ((), (), s32[]{:S(2)}) async-start(), calls=%async_computation.4 | async-start | bytes 8421376
  386.4 3.8 copy-start.9
Sparse Core Ops, SparseCore 0:
  11.7 119.3 all-gather.7
  142.5 74.8 all-gather.9
  219.9 77.0 all-gather.11
  372.7 243.2 all-reduce.2
  618.8 1275.6 reduce-scatter.3
where the time goes:
time: 1910 us; the launch traced here: 1900 us
  waiting for transfers between devices  1700 us (89%)
  blocking collectives  87.2 us (5%)
  other arithmetic  48.9 us (3%)
  matrix products  34.3 us (2%)
  local copies, waits for them, and re-layouts  20.8 us (1%)
    unnamed x6, waiting for transfers between devices  1280 us
    psum x1, waiting for transfers between devices, local(): down_grad, up_grad = lax.psum((down_part, up_part), ('dp', 'seq'))  225 us
    all_gather x1, waiting for transfers between devices, local(): whole_keyw = lax.all_gather(key_weight, ('dp', 'seq'), axis=0, tiled=True)  117 us
    all_gather x2, blocking collectives, carried_in(): gathered = jax.tree.map(lambda a: lax.all_gather(a, axis), part)  87.2 us
    all_gather x2, waiting for transfers between devices, carried_in(): gathered = jax.tree.map(lambda a: lax.all_gather(a, axis), part)  75 us
    add x31, other arithmetic, link_states(): return (earlier[0] * later[0], later[0][..., None] * earlier[1] + later[1])  41 us
  transfers between devices with their start and end apart: 5, of which 5 were waited for; matrix products, arithmetic and copies ran while one was open for 4% of the time, Pallas kernels for 0%

commit v1 on v0

v1 whole, which is shorter than its diff:
```python
import jax
import jax.numpy as jnp
from jax import lax
from jax.sharding import Mesh, PartitionSpec as P

HEADS = 8
DK = 128
GROUP = 64
HALF = HEADS // 2
WIDTH = HALF * DK
HI = lax.Precision.HIGHEST
F32 = jnp.float32
BF16 = jnp.bfloat16
XY = ("x", "y")
SWAP = ((0, 1), (1, 0))


def swap(a):
    return lax.ppermute(a, "c", SWAP)


def spread(a, axis, count):
    return lax.all_to_all(jnp.broadcast_to(a[None], (count,) + a.shape), axis, 0, 0)


def local(inputs, queries, values, out_grad, key_weight, gate_down, gate_up, gate_bias):
    core = lax.axis_index("c")
    first = core == 0
    zs, ps = lax.axis_size("z"), lax.axis_size("x") * lax.axis_size("y")
    own = inputs[0]
    count, model = own.shape
    rows_w = key_weight.shape[0]
    blocks = 2 * count // GROUP

    def halves(a):
        lo, hi = a[..., :WIDTH], a[..., WIDTH:]
        return jnp.where(first, lo, hi), jnp.where(first, hi, lo)

    def paired(mine, theirs, axis):
        return jnp.concatenate(
            [jnp.where(first, mine, theirs), jnp.where(first, theirs, mine)], axis=axis
        )

    w_mine, w_other = halves(key_weight)
    w_chip = paired(w_mine, swap(w_other), 0)
    w_z = spread(w_chip, "z", zs)
    w_all = spread(w_z, XY, ps)
    w_half = jnp.transpose(w_all, (1, 0, 2, 3)).reshape(model, WIDTH)

    tokens = paired(own, swap(own), 0)
    qvg = jnp.stack([queries[0], values[0], out_grad[0]])
    mine, other = halves(qvg)
    qvg = paired(mine, swap(other), 1)
    shape = (blocks, GROUP, HALF, DK)
    query_f, value_f, grad_f = (qvg[i].reshape(shape).astype(F32) for i in range(3))

    latent = lax.dot_general(
        tokens, gate_down, (((1,), (1,)), ((), ())), preferred_element_type=F32
    ).astype(BF16)
    up_half = halves(gate_up)[0]
    logits = jnp.dot(latent, up_half, preferred_element_type=F32) + halves(gate_bias)[0]
    gamma = jax.nn.log_sigmoid(logits) / 16.0
    rows_idx = lax.broadcasted_iota(jnp.int32, (GROUP, GROUP), 0)
    cols_idx = lax.broadcasted_iota(jnp.int32, (GROUP, GROUP), 1)
    lower = (rows_idx >= cols_idx).astype(F32)
    beta = jnp.einsum("ij,njhk->nihk", lower, gamma.reshape(shape), precision=HI)
    span = beta[:, -1]
    total_log = jnp.sum(span, axis=0)
    exp_beta = jnp.exp(beta)
    exp_neg = jnp.exp(-beta)
    exp_tail = jnp.exp(span[:, None] - beta)
    exp_span = jnp.exp(span)
    query_scaled = query_f * exp_beta

    part = HALF * DK // ps
    decays = lax.all_to_all(jnp.exp(total_log).reshape(ps, part), XY, 0, 0)

    def scan_over_chips(state, reverse):
        pieces = lax.all_to_all(state.reshape(ps, part, DK), XY, 0, 0)
        out = [None] * ps
        run = jnp.zeros((part, DK), F32)
        for i in range(ps):
            at = ps - 1 - i if reverse else i
            out[at] = run
            run = decays[at][:, None] * run + pieces[at]
        return lax.all_to_all(jnp.stack(out), XY, 0, 0).reshape(HALF, DK, DK)

    add_g = jnp.einsum("nqex,nqev->nexv", query_scaled, grad_f, precision=HI)
    start_grad = jnp.zeros((HALF, DK, DK), F32)
    for n in reversed(range(blocks)):
        start_grad = exp_span[n][..., None] * start_grad + add_g[n]
    run = scan_over_chips(start_grad, True)
    grads = [None] * blocks
    for n in reversed(range(blocks)):
        grads[n] = run
        run = exp_span[n][..., None] * run + add_g[n]
    grads = jnp.stack(grads)

    keys = jnp.dot(tokens, w_half, preferred_element_type=F32).astype(BF16)
    key_f = keys.reshape(shape).astype(F32)
    add_s = jnp.einsum("nqex,nqev->nexv", key_f * exp_tail, value_f, precision=HI)
    end_state = jnp.zeros((HALF, DK, DK), F32)
    for n in range(blocks):
        end_state = exp_span[n][..., None] * end_state + add_s[n]
    run = scan_over_chips(end_state, False)
    states = [run]
    for n in range(blocks):
        run = exp_span[n][..., None] * run + add_s[n]
        states.append(run)
    states = jnp.stack(states)

    pairs = jnp.einsum("nihv,njhv->nhij", grad_f, value_f, precision=HI) * lower[None, None]
    key_delta = exp_tail * jnp.einsum(
        "nhkv,njhv->njhk", grads, value_f, precision=HI
    ) + exp_neg * jnp.einsum("nhij,nihk->njhk", pairs, query_scaled, precision=HI)
    key_bf = key_delta.reshape(2 * count, WIDTH).astype(BF16)

    weight_part = lax.dot_general(
        tokens, key_bf, (((0,), (0,)), ((), ())), preferred_element_type=F32
    ).astype(BF16)
    weight_part = weight_part.reshape(zs, ps, 2 * rows_w, WIDTH).transpose(1, 0, 2, 3)
    weight_xy = jnp.sum(lax.all_to_all(weight_part, XY, 0, 0).astype(F32), axis=0)
    weight_z = jnp.sum(
        lax.all_to_all(weight_xy.astype(BF16), "z", 0, 0).astype(F32), axis=0
    )
    w_lo, w_hi = weight_z[:rows_w], weight_z[rows_w:]
    key_weight_grad = paired(
        jnp.where(first, w_lo, w_hi), swap(jnp.where(first, w_hi, w_lo)), 1
    )

    query_delta = exp_beta * (
        jnp.einsum("nhkv,nihv->nihk", states[:-1], grad_f, precision=HI)
        + jnp.einsum("nhij,njhk->nihk", pairs, key_f * exp_neg, precision=HI)
    )
    gate_delta = query_f * query_delta - key_f * key_delta
    within = jnp.einsum("ij,njhk->nihk", lower.T, gate_delta, precision=HI)
    beyond = jnp.sum(states[1:] * grads, axis=-1)
    suffix = within + beyond[:, None]
    gate_half = (suffix.reshape(2 * count, WIDTH) * jax.nn.sigmoid(-logits) / 16.0).astype(BF16)
    gate_lo, gate_hi = gate_half[:count], gate_half[count:]
    gate_grad = paired(
        jnp.where(first, gate_lo, gate_hi), swap(jnp.where(first, gate_hi, gate_lo)), 1
    )

    up_part = lax.dot_general(
        latent, gate_half, (((0,), (0,)), ((), ())), preferred_element_type=F32
    )
    latent_part = lax.dot_general(
        gate_half, up_half, (((1,), (1,)), ((), ())), preferred_element_type=F32
    )
    latent_delta = (latent_part + swap(latent_part)).astype(BF16)
    tokens_half = jnp.where(first, tokens[:, : model // 2], tokens[:, model // 2 :])
    down_part = lax.dot_general(
        latent_delta, tokens_half, (((0,), (0,)), ((), ())), preferred_element_type=F32
    )
    rank = gate_up.shape[0]
    small = jnp.concatenate([up_part, down_part], axis=1).reshape(ps, -1, DK)
    small = jnp.sum(lax.all_to_all(small, XY, 0, 0), axis=0)
    small = jnp.sum(spread(small, "z", zs), axis=0)
    small = spread(small, XY, ps).reshape(rank, -1)
    small_other = swap(small)
    up_grad = paired(small[:, :WIDTH], small_other[:, :WIDTH], 1)
    down_grad = paired(small[:, WIDTH:], small_other[:, WIDTH:], 1)

    through_keys = lax.dot_general(
        key_bf, w_half, (((1,), (1,)), ((), ())), preferred_element_type=F32
    )
    keys_lo, keys_hi = through_keys[:count], through_keys[count:]
    own_keys = jnp.where(first, keys_lo, keys_hi) + swap(jnp.where(first, keys_hi, keys_lo))
    own_latent = jnp.where(first, latent_delta[:count], latent_delta[count:])
    through_gate = jnp.dot(own_latent, gate_down, preferred_element_type=F32)
    input_grad = (own_keys + through_gate).astype(BF16)
    return (input_grad[None], gate_grad[None], key_weight_grad, down_grad, up_grad)


def solution(mesh):
    grid = Mesh(mesh.devices.reshape(8, 4, 4, 2), ("z", "x", "y", "c"))
    seq = ("x", "y", "c")
    tok = P("z", seq, None)
    row = P(("z",) + seq, None)
    return jax.shard_map(
        local,
        mesh=grid,
        in_specs=(tok, tok, tok, tok, row, P(), P(), P()),
        out_specs=(tok, tok, row, P(), P()),
        check_vma=False,
    )
```

time: 1910 us -> 250 us (0.13)
  waiting for transfers between devices: 1700 us -> 77.9 us
  blocking collectives: 87.2 us -> 9.88 us
  starting transfers between devices: 0.2 us -> 75.9 us
    unnamed x6 -> x0, waiting for transfers between devices: 1280 us -> none
    psum x1 -> x0, waiting for transfers between devices: 225 us -> none  [local(): down_grad, up_grad = lax.psum((down_part, up_part), ('dp', 'seq'))]
    all_gather x3 -> x0, waiting for transfers between devices: 192 us -> none  [the longest x1 117 us: local(): whole_keyw = lax.all_gather(key_weight, ('dp', 'seq'), axis=0, tiled=True)]
    all_gather x2 -> x0, blocking collectives: 87.2 us -> none  [carried_in(): gathered = jax.tree.map(lambda a: lax.all_gather(a, axis), part)]
    all_to_all x0 -> x11, waiting for transfers between devices: none -> 75.8 us  [the longest x4 36.8 us: spread(): lax.all_to_all(jnp.broadcast_to(a[None], (count,) + a.shape), axis, 0, 0)]
    all_to_all x0 -> x11, starting transfers between devices: none -> 50.7 us  [the longest x4 20.1 us: spread(): lax.all_to_all(jnp.broadcast_to(a[None], (count,) + a.shape), axis, 0, 0)]
    add x62 -> x3, other arithmetic: 41.2 us -> 2.81 us  [the longest x2 1.5 us: local(): run = exp_span[n][..., None] * run + add_s[n]]
    ppermute x0 -> x8, starting transfers between devices: none -> 25.2 us  [swap(): return lax.ppermute(a, 'c', SWAP)]
  transfers between devices with their start and end apart: 5 -> 19, of which waited for: 5 -> 12; matrix products, arithmetic and copies ran while one was open for 4% -> 19% of each run, Pallas kernels for 0% -> 0%
where the time goes in v1:
time: 250 us; the launch traced here: 248 us
  waiting for transfers between devices  77.9 us (31%)
  starting transfers between devices  75.9 us (30%)
  other arithmetic  35.1 us (14%)
  local copies, waits for them, and re-layouts  25.3 us (10%)
  matrix products  22 us (9%)
  blocking collectives  9.88 us (4%)
    all_to_all x4, waiting for transfers between devices, spread(): lax.all_to_all(jnp.broadcast_to(a[None], (count,) + a.shape), axis, 0, 0)  36.8 us
    ppermute x8, starting transfers between devices, swap(): return lax.ppermute(a, 'c', SWAP)  25.2 us
    unnamed x16, other arithmetic  22.1 us
    all_to_all x4, starting transfers between devices, spread(): lax.all_to_all(jnp.broadcast_to(a[None], (count,) + a.shape), axis, 0, 0)  20.1 us
    all_to_all x1, waiting for transfers between devices, local(): lax.all_to_all(weight_part, XY, 0, 0).astype(F32)  14.5 us
    unnamed x77, local copies, waits for them, and re-layouts  10.9 us
    all_to_all x2, starting transfers between devices, scan_over_chips(): pieces = lax.all_to_all(state.reshape(ps, part, DK), XY, 0, 0)  10.2 us
    all_to_all x1, blocking collectives, local(): small = jnp.sum(lax.all_to_all(small, XY, 0, 0), axis=0)  9.88 us
  transfers between devices with their start and end apart: 19, of which 12 were waited for; matrix products, arithmetic and copies ran while one was open for 19% of the time, Pallas kernels for 0%

profile of v1, /device:TPU:1, one launch (start us, length us, event | category | flops | bytes accessed | tf_op | source)
XLA Modules:
  0.0 247.5 jit_solution(7673949634553047497)
XLA Ops:
  1.4 3.2 %collective-permute-start.2 = (bf16[8,512]{1,0:T(8,128)(2,1)S(1)}, bf16[8,512]{1,0:T(8,128)(2,1)S(1)}, u32[]{:S(2)}, u32[]{:S(2)}) collective-permute-start(bf16[8,512]{1,0:T(8,128)(2,1)S(1)} %broadcast_select_fusion.14), channel_id=1, source_target_pairs={{0,1},{1,0},{2,3},{3,2},{4,5},{5,4},{6,7},{7,6},{8,9},{9,8},{10,11... | collective-permute-start | bytes 24584 | tf_op jit(solution)/shard_map/ppermute | solution.py:19
  8.9 6.5 %all-to-all-start.3 = ((bf16[8,16,512]{2,1,0:T(8,128)(2,1)}), bf16[8,16,512]{2,1,0:T(8,128)(2,1)S(1)}, u32[]{:S(2)}, u32[]{:S(2)}) async-start(bf16[8,16,512]{2,1,0:T(8,128)(2,1)} %broadcast_in_dim.12), calls=%async_computation.3 | async-start | bytes 262144 | tf_op jit(solution)/shard_map/all_to_all | solution.py:23
  16.1 7.8 %all-to-all-done.3 = bf16[8,16,512]{2,1,0:T(8,128)(2,1)S(1)} async-done(((bf16[8,16,512]{2,1,0:T(8,128)(2,1)}), bf16[8,16,512]{2,1,0:T(8,128)(2,1)S(1)}, u32[]{:S(2)}, u32[]{:S(2)}) %all-to-all-start.3) | async-done | bytes 131104 | tf_op jit(solution)/shard_map/all_to_all | solution.py:23
  23.9 1.6 broadcast_in_dim.13
  25.5 6.8 %all-to-all-start.4 = ((bf16[16,8,16,512]{3,2,1,0:T(8,128)(2,1)}), bf16[16,8,16,512]{3,2,1,0:T(8,128)(2,1)}, u32[]{:S(2)}, u32[]{:S(2)}) async-start(bf16[16,8,16,512]{3,2,1,0:T(8,128)(2,1)} %broadcast_in_dim.13), calls=%async_computation.4 | async-start | bytes 4194304 | tf_op jit(solution)/shard_map/all_to_all | solution.py:23
  32.9 1.1 convolution_multiply_fusion
  34.7 1.3 fusion.22
  40.3 17.6 %all-to-all-done.4 = bf16[16,8,16,512]{3,2,1,0:T(8,128)(2,1)} async-done(((bf16[16,8,16,512]{3,2,1,0:T(8,128)(2,1)}), bf16[16,8,16,512]{3,2,1,0:T(8,128)(2,1)}, u32[]{:S(2)}, u32[]{:S(2)}) %all-to-all-start.4) | async-done | bytes 2097184 | tf_op jit(solution)/shard_map/all_to_all | solution.py:23
  58.0 5.4 %all-to-all-start = ((f32[16,1,32]{2,1,0:T(1,128)}), f32[16,1,32]{2,1,0:T(1,128)S(1)}, u32[]{:S(2)}, u32[]{:S(2)}) async-start(f32[16,1,32]{2,1,0:T(1,128)} %exp.38), calls=%async_computation | async-start | bytes 16384 | tf_op jit(solution)/shard_map/all_to_all | solution.py:76
  63.4 1.9 copy.82
  65.3 1.3 copy-done.1
  66.6 1.5 fusion.8
  68.1 2.0 reshape.1774
  70.1 2.1 fusion.27
  72.4 1.3 multiply_add_fusion.4
  73.7 6.7 %all-to-all-start.1 = ((f32[16,32,128]{2,1,0:T(8,128)}), f32[16,32,128]{2,1,0:T(8,128)S(1)}, u32[]{:S(2)}, u32[]{:S(2)}) async-start(f32[16,32,128]{2,1,0:T(8,128)} %get-tuple-element.60), calls=%async_computation.1 | async-start | bytes 524288 | tf_op jit(solution)/shard_map/all_to_all | solution.py:79
  80.4 2.8 %fusion.7 = f32[4,64,4,128]{3,1,2,0:T(8,128)} fusion(f32[4,4,64,64]{3,2,1,0:T(8,128)} %convolution_multiply_fusion, f32[4,64,4,128]{3,1,2,0:T(8,128)S(1)} %convolution_bitcast_fusion.2, f32[4,64,4,128]{3,2,1,0:T(4,128)S(1)} %reshape.1773), kind=kOutput, calls=%fused_computation.22 | convolution fusion | flops 101056512 | bytes 1835008 | tf_op jit(solution)/shard_map/nhij,nihk->njhk/dot_general | solution.py:115
  83.9 3.8 %all-to-all-done.1 = f32[16,32,128]{2,1,0:T(8,128)S(1)} async-done(((f32[16,32,128]{2,1,0:T(8,128)}), f32[16,32,128]{2,1,0:T(8,128)S(1)}, u32[]{:S(2)}, u32[]{:S(2)}) %all-to-all-start.1) | async-done | bytes 262176 | tf_op jit(solution)/shard_map/all_to_all | solution.py:79
  88.4 3.5 %all-to-all-start.5 = ((f32[16,32,128]{2,1,0:T(8,128)}), f32[16,32,128]{2,1,0:T(8,128)S(1)}, u32[]{:S(2)}, u32[]{:S(2)}) async-start(f32[16,32,128]{2,1,0:T(8,128)} %get-tuple-element.59), calls=%async_computation.5 | async-start | bytes 524288 | tf_op jit(solution)/shard_map/all_to_all | solution.py:79
  91.9 1.7 constant_dynamic-update-slice_fusion.18
  94.2 5.0 %all-to-all-done.5 = f32[16,32,128]{2,1,0:T(8,128)S(1)} async-done(((f32[16,32,128]{2,1,0:T(8,128)}), f32[16,32,128]{2,1,0:T(8,128)S(1)}, u32[]{:S(2)}, u32[]{:S(2)}) %all-to-all-start.5) | async-done | bytes 262176 | tf_op jit(solution)/shard_map/all_to_all | solution.py:79
  99.2 1.4 constant_dynamic-update-slice_fusion.33
  100.6 1.4 constant_dynamic-update-slice_fusion.32
  101.9 1.3 constant_dynamic-update-slice_fusion.31
  103.2 1.4 constant_dynamic-update-slice_fusion.30
  104.7 1.3 constant_dynamic-update-slice_fusion.15
  106.0 1.3 constant_dynamic-update-slice_fusion.29
  107.3 1.4 constant_dynamic-update-slice_fusion.28
  109.3 1.4 constant_dynamic-update-slice_fusion.27
  110.6 1.4 constant_dynamic-update-slice_fusion.26
  112.7 1.3 constant_dynamic-update-slice_fusion.25
  114.0 1.4 constant_dynamic-update-slice_fusion.24
  116.0 1.3 constant_dynamic-update-slice_fusion.23
  117.3 1.4 constant_dynamic-update-slice_fusion.22
  119.3 1.3 constant_dynamic-update-slice_fusion.21
  120.6 1.4 constant_dynamic-update-slice_fusion.20
  122.0 1.3 constant_dynamic-update-slice_fusion.19
  123.4 3.5 %all-to-all-start.6 = ((f32[16,32,128]{2,1,0:T(8,128)}), f32[16,32,128]{2,1,0:T(8,128)S(1)}, u32[]{:S(2)}, u32[]{:S(2)}) async-start(f32[16,32,128]{2,1,0:T(8,128)} %constant_dynamic-update-slice_fusion.19), calls=%async_computation.6 | async-start | bytes 524288 | tf_op jit(solution)/shard_map/all_to_all | solution.py:86
  127.5 1.4 constant_dynamic-update-slice_fusion.4
  129.5 4.7 %all-to-all-done.6 = f32[16,32,128]{2,1,0:T(8,128)S(1)} async-done(((f32[16,32,128]{2,1,0:T(8,128)}), f32[16,32,128]{2,1,0:T(8,128)S(1)}, u32[]{:S(2)}, u32[]{:S(2)}) %all-to-all-start.6) | async-done | bytes 262176 | tf_op jit(solution)/shard_map/all_to_all | solution.py:86
  134.9 3.7 %all-to-all-start.2 = ((f32[16,32,128]{2,1,0:T(8,128)}), f32[16,32,128]{2,1,0:T(8,128)S(1)}, u32[]{:S(2)}, u32[]{:S(2)}) async-start(f32[16,32,128]{2,1,0:T(8,128)} %constant_dynamic-update-slice_fusion.3), calls=%async_computation.2 | async-start | bytes 524288 | tf_op jit(solution)/shard_map/all_to_all | solution.py:86
  138.6 2.7 %convolution_bitcast_fusion.3 = f32[4,64,4,128]{3,1,2,0:T(8,128)} fusion(f32[4,4,64,64]{3,2,1,0:T(8,128)} %convolution_multiply_fusion, f32[4,64,4,128]{3,1,2,0:T(8,128)S(1)} %convolution_bitcast_fusion.2, f32[4,64,4,128]{3,2,1,0:T(4,128)} %reshape.1774), kind=kOutput, calls=%fused_computation.20 | convolution fusion | flops 100925440 | bytes 1835008 | tf_op jit(solution)/shard_map/nhij,njhk->nihk/dot_general | solution.py:133
  141.4 4.4 %all-to-all-done.2 = f32[16,32,128]{2,1,0:T(8,128)S(1)} async-done(((f32[16,32,128]{2,1,0:T(8,128)}), f32[16,32,128]{2,1,0:T(8,128)S(1)}, u32[]{:S(2)}, u32[]{:S(2)}) %all-to-all-start.2) | async-done | bytes 262176 | tf_op jit(solution)/shard_map/all_to_all | solution.py:86
  145.7 1.4 multiply_add_fusion
  147.3 1.2 fusion.67
  148.9 1.2 fusion.5
  151.4 9.2 %collective-permute-start.4 = (f32[256,16]{0,1:T(8,128)S(1)}, f32[256,16]{0,1:T(8,128)S(1)}, u32[]{:S(2)}, u32[]{:S(2)}) collective-permute-start(f32[256,16]{0,1:T(8,128)S(1)} %fusion.56), channel_id=1, source_target_pairs={{0,1},{1,0},{2,3},{3,2},{4,5},{5,4},{6,7},{7,6},{8,9},{9,8},{10,11... | collective-permute-start | bytes 49160 | tf_op jit(solution)/shard_map/ppermute | solution.py:19
  161.8 9.9 %all_to_all.61 = f32[16,12,128]{2,1,0:T(8,128)S(1)} all-to-all(f32[16,12,128]{2,1,0:T(8,128)S(1)} %reshape.1771), channel_id=1, replica_groups=mesh['z'=8,'x'=4,'y'=4,'c'=2] {'x','y'}, dimensions={0} | all-to-all | bytes 196608 | tf_op jit(solution)/shard_map/all_to_all | solution.py:158
  172.3 3.4 %all-to-all-start.10 = ((f32[8,12,128]{2,1,0:T(8,128)}), f32[8,12,128]{2,1,0:T(8,128)S(1)}, u32[]{:S(2)}, u32[]{:S(2)}) async-start(f32[8,12,128]{2,1,0:T(8,128)} %broadcast_in_dim.16), calls=%async_computation.10 | async-start | bytes 131072 | tf_op jit(solution)/shard_map/all_to_all | solution.py:23
  175.9 7.0 %all-to-all-done.10 = f32[8,12,128]{2,1,0:T(8,128)S(1)} async-done(((f32[8,12,128]{2,1,0:T(8,128)}), f32[8,12,128]{2,1,0:T(8,128)S(1)}, u32[]{:S(2)}, u32[]{:S(2)}) %all-to-all-start.10) | async-done | bytes 49184 | tf_op jit(solution)/shard_map/all_to_all | solution.py:23
  183.6 3.5 %all-to-all-start.11 = ((f32[16,12,128]{2,1,0:T(8,128)}), f32[16,12,128]{2,1,0:T(8,128)S(1)}, u32[]{:S(2)}, u32[]{:S(2)}) async-start(f32[16,12,128]{2,1,0:T(8,128)} %broadcast_in_dim.17), calls=%async_computation.11 | async-start | bytes 262144 | tf_op jit(solution)/shard_map/all_to_all | solution.py:23
  187.9 1.6 copy.140
  189.4 4.4 %all-to-all-done.11 = f32[16,12,128]{2,1,0:T(8,128)S(1)} async-done(((f32[16,12,128]{2,1,0:T(8,128)}), f32[16,12,128]{2,1,0:T(8,128)S(1)}, u32[]{:S(2)}, u32[]{:S(2)}) %all-to-all-start.11) | async-done | bytes 98336 | tf_op jit(solution)/shard_map/all_to_all | solution.py:23
  193.8 4.4 %all-to-all-start.7 = ((bf16[16,8,16,512]{3,2,1,0:T(8,128)(2,1)}), bf16[16,8,16,512]{3,2,1,0:T(8,128)(2,1)}, u32[]{:S(2)}, u32[]{:S(2)}) async-start(bf16[16,8,16,512]{3,2,1,0:T(8,128)(2,1)} %bitcast.127), calls=%async_computation.7 | async-start | bytes 4194304 | tf_op jit(solution)/shard_map/all_to_all | solution.py:122
  198.3 4.1 %collective-permute-start.5 = (bf16[128,512]{1,0:T(8,128)(2,1)S(1)}, bf16[128,512]{1,0:T(8,128)(2,1)S(1)}, u32[]{:S(2)}, u32[]{:S(2)}) collective-permute-start(bf16[128,512]{1,0:T(8,128)(2,1)S(1)} %broadcast_select_fusion.8), channel_id=1, source_target_pairs={{0,1},{1,0},{2,3},{3,2},{4,5},{5,4},{6,7},{7,6},{8,9},{9,8},{10,11... | collective-permute-start | bytes 393224 | tf_op jit(solution)/shard_map/ppermute | solution.py:19
  202.4 2.3 fusion.37
  204.8 1.1 slice_select_fusion
  207.3 1.4 collective-permute-done.7
  208.7 14.5 %all-to-all-done.7 = bf16[16,8,16,512]{3,2,1,0:T(8,128)(2,1)} async-done(((bf16[16,8,16,512]{3,2,1,0:T(8,128)(2,1)}), bf16[16,8,16,512]{3,2,1,0:T(8,128)(2,1)}, u32[]{:S(2)}, u32[]{:S(2)}) %all-to-all-start.7) | async-done | bytes 2097184 | tf_op jit(solution)/shard_map/all_to_all | solution.py:122
  223.2 2.7 %reduce_sum.59 = bf16[8,16,512]{2,1,0:T(8,128)(2,1)} reduce(bf16[16,8,16,512]{3,2,1,0:T(8,128)(2,1)} %all-to-all-done.7, bf16[]{:T(256)} %constant.21.clone.1), dimensions={0}, to_apply=%region_2.3 | reduce | flops 983040 | bytes 2228226 | tf_op jit(solution)/shard_map/reduce_sum | solution.py:122
  225.9 3.4 %all-to-all-start.8 = ((bf16[8,16,512]{2,1,0:T(8,128)(2,1)}), bf16[8,16,512]{2,1,0:T(8,128)(2,1)S(1)}, u32[]{:S(2)}, u32[]{:S(2)}) async-start(bf16[8,16,512]{2,1,0:T(8,128)(2,1)} %reduce_sum.59), calls=%async_computation.8 | async-start | bytes 262144 | tf_op jit(solution)/shard_map/all_to_all | solution.py:124
  230.5 6.5 %all-to-all-done.8 = bf16[8,16,512]{2,1,0:T(8,128)(2,1)S(1)} async-done(((bf16[8,16,512]{2,1,0:T(8,128)(2,1)}), bf16[8,16,512]{2,1,0:T(8,128)(2,1)S(1)}, u32[]{:S(2)}, u32[]{:S(2)}) %all-to-all-start.8) | async-done | bytes 131104 | tf_op jit(solution)/shard_map/all_to_all | solution.py:124
  237.1 7.4 %collective-permute-start.6 = (f32[8,512]{1,0:T(8,128)S(1)}, f32[8,512]{1,0:T(8,128)S(1)}, u32[]{:S(2)}, u32[]{:S(2)}) collective-permute-start(f32[8,512]{1,0:T(8,128)S(1)} %slice_select_fusion.6), channel_id=1, source_target_pairs={{0,1},{1,0},{2,3},{3,2},{4,5},{5,4},{6,7},{7,6},{8,9},{9,8},{10,11... | collective-permute-start | bytes 49160 | tf_op jit(solution)/shard_map/ppermute | solution.py:19
  244.6 2.3 fusion.17
  (148 shorter events, 26.2 us)
Async XLA Ops:
  0.6 33.4 %copy-start = (bf16[16,2048]{1,0:T(8,128)(2,1)S(1)}, bf16[16,2048]{1,0:T(8,128)(2,1)}, u32[]{:S(2)}) copy-start(bf16[16,2048]{1,0:T(8,128)(2,1)} %param.13) | copy-start | bytes 196612
  0.6 7.6 %copy-start.26 = (bf16[8,1024]{1,0:T(8,128)(2,1)S(1)}, bf16[8,1024]{1,0:T(8,128)(2,1)}, u32[]{:S(2)}) copy-start(bf16[8,1024]{1,0:T(8,128)(2,1)} %param.12) | copy-start | bytes 49156
  0.7 15.4 %copy-start.32 = (f32[1024]{0:T(1024)S(1)}, f32[1024]{0:T(1024)}, u32[]{:S(2)}) copy-start(f32[1024]{0:T(1024)} %param.15) | copy-start | bytes 12292
  1.4 6.8 %collective-permute-start.2 = (bf16[8,512]{1,0:T(8,128)(2,1)S(1)}, bf16[8,512]{1,0:T(8,128)(2,1)S(1)}, u32[]{:S(2)}, u32[]{:S(2)}) collective-permute-start(bf16[8,512]{1,0:T(8,128)(2,1)S(1)} %broadcast_select_fusion.14), channel_id=1, source_target_pairs={{0,1},{1,0},{2,3},{3,2},{4,5},{5,4},{6,7},{7,6},{8,9},{9,8},{10,11... | collective-permute-start | bytes 24584 | tf_op jit(solution)/shard_map/ppermute | solution.py:19
  4.7 29.3 %collective-permute-start = (bf16[128,2048]{1,0:T(8,128)(2,1)}, bf16[128,2048]{1,0:T(8,128)(2,1)S(1)}, u32[]{:S(2)}, u32[]{:S(2)}) collective-permute-start(bf16[128,2048]{1,0:T(8,128)(2,1)} %bitcast.148), channel_id=1, source_target_pairs={{0,1},{1,0},{2,3},{3,2},{4,5},{5,4},{6,7},{7,6},{8,9},{9,8},{10,11... | collective-permute-start | bytes 1572872 | tf_op jit(solution)/shard_map/ppermute | solution.py:19
  7.6 24.7 %collective-permute-start.1 = (bf16[3,128,512]{2,1,0:T(8,128)(2,1)S(1)}, bf16[3,128,512]{2,1,0:T(8,128)(2,1)S(1)}, u32[]{:S(2)}, u32[]{:S(2)}) collective-permute-start(bf16[3,128,512]{2,1,0:T(8,128)(2,1)S(1)} %broadcast_select_fusion.4), channel_id=1, source_target_pairs={{0,1},{1,0},{2,3},{3,2},{4,5},{5,4},{6,7},{7,6},{8,9},{9,8},{10,11... | collective-permute-start | bytes 1179656 | tf_op jit(solution)/shard_map/ppermute | solution.py:19
  8.9 14.9 %all-to-all-start.3 = ((bf16[8,16,512]{2,1,0:T(8,128)(2,1)}), bf16[8,16,512]{2,1,0:T(8,128)(2,1)S(1)}, u32[]{:S(2)}, u32[]{:S(2)}) async-start(bf16[8,16,512]{2,1,0:T(8,128)(2,1)} %broadcast_in_dim.12), calls=%async_computation.3 | async-start | bytes 262144 | tf_op jit(solution)/shard_map/all_to_all | solution.py:23
  25.5 32.5 %all-to-all-start.4 = ((bf16[16,8,16,512]{3,2,1,0:T(8,128)(2,1)}), bf16[16,8,16,512]{3,2,1,0:T(8,128)(2,1)}, u32[]{:S(2)}, u32[]{:S(2)}) async-start(bf16[16,8,16,512]{3,2,1,0:T(8,128)(2,1)} %broadcast_in_dim.13), calls=%async_computation.4 | async-start | bytes 4194304 | tf_op jit(solution)/shard_map/all_to_all | solution.py:23
  32.4 1.5 copy-start.16
  32.6 37.5 %copy-start.5 = (bf16[4,64,4,128]{3,2,1,0:T(4,128)(2,1)}, bf16[4,64,4,128]{3,2,1,0:T(4,128)(2,1)S(1)}, u32[]{:S(2)}) copy-start(bf16[4,64,4,128]{3,2,1,0:T(4,128)(2,1)S(1)} %reshape_squeeze.7) | copy-start | bytes 786436
  32.8 5.4 %copy-start.3 = (bf16[4,64,4,128]{3,2,1,0:T(4,128)(2,1)}, bf16[4,64,4,128]{3,2,1,0:T(4,128)(2,1)S(1)}, u32[]{:S(2)}) copy-start(bf16[4,64,4,128]{3,2,1,0:T(4,128)(2,1)S(1)} %reshape_squeeze.8) | copy-start | bytes 786436
  33.9 0.8 copy-start.28
  34.0 2.0 copy-start.20
  34.0 2.0 copy-start.17
  34.7 3.6 %copy-start.30 = (bf16[256,16]{0,1:T(8,128)(2,1)}, bf16[256,16]{0,1:T(8,128)(2,1)S(1)}, u32[]{:S(2)}) copy-start(bf16[256,16]{0,1:T(8,128)(2,1)S(1)} %convolution_convert_fusion.2) | copy-start | bytes 24580
  36.6 33.5 %copy-start.24 = (f32[4,1,4,128]{3,1,2,0:T(1,128)}, f32[4,1,4,128]{3,1,2,0:T(1,128)S(1)}, u32[]{:S(2)}) copy-start(f32[4,1,4,128]{3,1,2,0:T(1,128)S(1)} %get-tuple-element.48) | copy-start | bytes 24580
  58.0 15.7 %all-to-all-start = ((f32[16,1,32]{2,1,0:T(1,128)}), f32[16,1,32]{2,1,0:T(1,128)S(1)}, u32[]{:S(2)}, u32[]{:S(2)}) async-start(f32[16,1,32]{2,1,0:T(1,128)} %exp.38), calls=%async_computation | async-start | bytes 16384 | tf_op jit(solution)/shard_map/all_to_all | solution.py:76
  63.4 3.2 %copy-start.18 = (bf16[128,2048]{1,0:T(8,128)(2,1)S(1)}, bf16[128,2048]{1,0:T(8,128)(2,1)}, u32[]{:S(2)}) copy-start(bf16[128,2048]{1,0:T(8,128)(2,1)} %copy-done.17) | copy-start | bytes 1572868
  63.4 3.2 %copy-start.21 = (bf16[128,2048]{1,0:T(8,128)(2,1)S(1)}, bf16[128,2048]{1,0:T(8,128)(2,1)}, u32[]{:S(2)}) copy-start(bf16[128,2048]{1,0:T(8,128)(2,1)} %copy-done.20) | copy-start | bytes 1572868
  65.3 1.3 copy-start.1
  70.1 2.2 copy-start.12
  70.1 2.3 copy-start.13
  70.1 2.3 copy-start.14
  70.1 2.3 copy-start.15
  73.7 14.0 %all-to-all-start.1 = ((f32[16,32,128]{2,1,0:T(8,128)}), f32[16,32,128]{2,1,0:T(8,128)S(1)}, u32[]{:S(2)}, u32[]{:S(2)}) async-start(f32[16,32,128]{2,1,0:T(8,128)} %get-tuple-element.60), calls=%async_computation.1 | async-start | bytes 524288 | tf_op jit(solution)/shard_map/all_to_all | solution.py:79
  87.7 0.7 copy-start.11
  88.4 10.8 %all-to-all-start.5 = ((f32[16,32,128]{2,1,0:T(8,128)}), f32[16,32,128]{2,1,0:T(8,128)S(1)}, u32[]{:S(2)}, u32[]{:S(2)}) async-start(f32[16,32,128]{2,1,0:T(8,128)} %get-tuple-element.59), calls=%async_computation.5 | async-start | bytes 524288 | tf_op jit(solution)/shard_map/all_to_all | solution.py:79
  123.4 10.8 %all-to-all-start.6 = ((f32[16,32,128]{2,1,0:T(8,128)}), f32[16,32,128]{2,1,0:T(8,128)S(1)}, u32[]{:S(2)}, u32[]{:S(2)}) async-start(f32[16,32,128]{2,1,0:T(8,128)} %constant_dynamic-update-slice_fusion.19), calls=%async_computation.6 | async-start | bytes 524288 | tf_op jit(solution)/shard_map/all_to_all | solution.py:86
  134.2 0.7 copy-start.7
  134.9 10.8 %all-to-all-start.2 = ((f32[16,32,128]{2,1,0:T(8,128)}), f32[16,32,128]{2,1,0:T(8,128)S(1)}, u32[]{:S(2)}, u32[]{:S(2)}) async-start(f32[16,32,128]{2,1,0:T(8,128)} %constant_dynamic-update-slice_fusion.3), calls=%async_computation.2 | async-start | bytes 524288 | tf_op jit(solution)/shard_map/all_to_all | solution.py:86
  141.3 5.8 %copy-start.27 = (f32[4,128]{1,0:T(4,128)S(1)}, f32[4,128]{1,0:T(4,128)}, u32[]{:S(2)}) copy-start(f32[4,128]{1,0:T(4,128)} %get-tuple-element.63) | copy-start | bytes 6148
  145.7 1.5 copy-start.6
  145.7 1.5 copy-start.10
  145.7 1.6 copy-start.25
  147.3 1.6 copy-start.2
  147.3 1.6 copy-start.4
  147.3 1.6 copy-start.8
  147.3 1.6 copy-start.9
  150.1 1.0 copy-start.23
  150.1 1.2 copy-start.29
  150.1 10.5 %copy-start.31 = (bf16[256,16]{0,1:T(8,128)(2,1)S(1)}, bf16[256,16]{0,1:T(8,128)(2,1)}, u32[]{:S(2)}) copy-start(bf16[256,16]{0,1:T(8,128)(2,1)} %copy-done.30) | copy-start | bytes 24580
  150.1 11.4 %copy-start.19 = (bf16[128,2048]{1,0:T(8,128)(2,1)S(1)}, bf16[128,2048]{1,0:T(8,128)(2,1)}, u32[]{:S(2)}) copy-start(bf16[128,2048]{1,0:T(8,128)(2,1)} %copy-done.17) | copy-start | bytes 1572868
  150.1 11.3 %copy-start.22 = (bf16[128,2048]{1,0:T(8,128)(2,1)S(1)}, bf16[128,2048]{1,0:T(8,128)(2,1)}, u32[]{:S(2)}) copy-start(bf16[128,2048]{1,0:T(8,128)(2,1)} %copy-done.20) | copy-start | bytes 1572868
  151.4 10.0 %collective-permute-start.4 = (f32[256,16]{0,1:T(8,128)S(1)}, f32[256,16]{0,1:T(8,128)S(1)}, u32[]{:S(2)}, u32[]{:S(2)}) collective-permute-start(f32[256,16]{0,1:T(8,128)S(1)} %fusion.56), channel_id=1, source_target_pairs={{0,1},{1,0},{2,3},{3,2},{4,5},{5,4},{6,7},{7,6},{8,9},{9,8},{10,11... | collective-permute-start | bytes 49160 | tf_op jit(solution)/shard_map/ppermute | solution.py:19
  172.3 10.6 %all-to-all-start.10 = ((f32[8,12,128]{2,1,0:T(8,128)}), f32[8,12,128]{2,1,0:T(8,128)S(1)}, u32[]{:S(2)}, u32[]{:S(2)}) async-start(f32[8,12,128]{2,1,0:T(8,128)} %broadcast_in_dim.16), calls=%async_computation.10 | async-start | bytes 131072 | tf_op jit(solution)/shard_map/all_to_all | solution.py:23
  183.6 10.2 %all-to-all-start.11 = ((f32[16,12,128]{2,1,0:T(8,128)}), f32[16,12,128]{2,1,0:T(8,128)S(1)}, u32[]{:S(2)}, u32[]{:S(2)}) async-start(f32[16,12,128]{2,1,0:T(8,128)} %broadcast_in_dim.17), calls=%async_computation.11 | async-start | bytes 262144 | tf_op jit(solution)/shard_map/all_to_all | solution.py:23
  193.8 29.4 %all-to-all-start.7 = ((bf16[16,8,16,512]{3,2,1,0:T(8,128)(2,1)}), bf16[16,8,16,512]{3,2,1,0:T(8,128)(2,1)}, u32[]{:S(2)}, u32[]{:S(2)}) async-start(bf16[16,8,16,512]{3,2,1,0:T(8,128)(2,1)} %bitcast.127), calls=%async_computation.7 | async-start | bytes 4194304 | tf_op jit(solution)/shard_map/all_to_all | solution.py:122
  198.3 7.6 %collective-permute-start.5 = (bf16[128,512]{1,0:T(8,128)(2,1)S(1)}, bf16[128,512]{1,0:T(8,128)(2,1)S(1)}, u32[]{:S(2)}, u32[]{:S(2)}) collective-permute-start(bf16[128,512]{1,0:T(8,128)(2,1)S(1)} %broadcast_select_fusion.8), channel_id=1, source_target_pairs={{0,1},{1,0},{2,3},{3,2},{4,5},{5,4},{6,7},{7,6},{8,9},{9,8},{10,11... | collective-permute-start | bytes 393224 | tf_op jit(solution)/shard_map/ppermute | solution.py:19
  205.9 38.7 %collective-permute-start.3 = (f32[128,2048]{1,0:T(8,128)}, f32[128,2048]{1,0:T(8,128)}, u32[]{:S(2)}, u32[]{:S(2)}) collective-permute-start(f32[128,2048]{1,0:T(8,128)} %slice_select_fusion), channel_id=1, source_target_pairs={{0,1},{1,0},{2,3},{3,2},{4,5},{5,4},{6,7},{7,6},{8,9},{9,8},{10,11... | collective-permute-start | bytes 3145736 | tf_op jit(solution)/shard_map/ppermute | solution.py:19
  206.0 2.7 %collective-permute-start.7 = (f32[16,1536]{1,0:T(8,128)S(1)}, f32[16,1536]{1,0:T(8,128)S(1)}, u32[]{:S(2)}, u32[]{:S(2)}) collective-permute-start(f32[16,1536]{1,0:T(8,128)S(1)} %bitcast.150), channel_id=1, source_target_pairs={{0,1},{1,0},{2,3},{3,2},{4,5},{5,4},{6,7},{7,6},{8,9},{9,8},{10,11... | collective-permute-start | bytes 294920 | tf_op jit(solution)/shard_map/ppermute | solution.py:19
  225.9 11.2 %all-to-all-start.8 = ((bf16[8,16,512]{2,1,0:T(8,128)(2,1)}), bf16[8,16,512]{2,1,0:T(8,128)(2,1)S(1)}, u32[]{:S(2)}, u32[]{:S(2)}) async-start(bf16[8,16,512]{2,1,0:T(8,128)(2,1)} %reduce_sum.59), calls=%async_computation.8 | async-start | bytes 262144 | tf_op jit(solution)/shard_map/all_to_all | solution.py:124
  237.1 9.8 %collective-permute-start.6 = (f32[8,512]{1,0:T(8,128)S(1)}, f32[8,512]{1,0:T(8,128)S(1)}, u32[]{:S(2)}, u32[]{:S(2)}) collective-permute-start(f32[8,512]{1,0:T(8,128)S(1)} %slice_select_fusion.6), channel_id=1, source_target_pairs={{0,1},{1,0},{2,3},{3,2},{4,5},{5,4},{6,7},{7,6},{8,9},{9,8},{10,11... | collective-permute-start | bytes 49160 | tf_op jit(solution)/shard_map/ppermute | solution.py:19

commit v2 on v1

v2 whole, which is shorter than its diff:
```python
import jax
import jax.numpy as jnp
from jax import lax
from jax.experimental import pallas as pl
from jax.experimental.pallas import tpu as pltpu
from jax.sharding import Mesh, PartitionSpec as P

HEADS = 8
DK = 128
GROUP = 64
HALF = HEADS // 2
WIDTH = HALF * DK
TOK = 128
PAIR = 2 * TOK
BLOCKS = PAIR // GROUP
MODEL = 2048
RANK = 16
ZS = 8
PS = 16
ROWS = HALF * DK // PS
F32 = jnp.float32
BF16 = jnp.bfloat16
XY = ("x", "y")
SWAP = ((0, 1), (1, 0))
MB = 1 << 20


def shape(dims, dtype=F32):
    return jax.ShapeDtypeStruct(dims, dtype)


BIG = 56
KEYS = 16


def kernel(body, outs, name, limit, scratch=(), specs=None):
    extra = {} if specs is None else {"in_specs": specs}
    return pl.pallas_call(
        body,
        out_shape=outs,
        name=name,
        scratch_shapes=scratch,
        compiler_params=pltpu.CompilerParams(vmem_limit_bytes=limit * MB),
        **extra,
    )


def split(a):
    hi = a.astype(BF16)
    return hi, (a - hi.astype(F32)).astype(BF16)


def dot(a, b, dims=((1,), (0,))):
    return lax.dot_general(a, b, (dims, ((), ())), preferred_element_type=F32)


NT = ((1,), (1,))
TN = ((0,), (0,))


def dot_hl(a, b, dims=((1,), (0,))):
    hi, lo = split(b)
    return dot(a, hi, dims) + dot(a, lo, dims)


def dot_ff(a, b, dims=((1,), (0,))):
    ah, al = split(a)
    bh, bl = split(b)
    return dot(ah, bh, dims) + dot(ah, bl, dims) + dot(al, bh, dims)


def dot_mask(mask, b):
    hi, lo = split(b)
    rest = (b - hi.astype(F32) - lo.astype(F32)).astype(BF16)
    return dot(mask, hi) + dot(mask, lo) + dot(mask, rest)


def is_first():
    return lax.axis_index("c") == 0


def pick(first, a, b):
    return jnp.where(first, a, b)


def low_mask():
    rows = lax.broadcasted_iota(jnp.int32, (GROUP, GROUP), 0)
    cols = lax.broadcasted_iota(jnp.int32, (GROUP, GROUP), 1)
    return rows >= cols, rows <= cols


def tok_of(n):
    return slice(n * GROUP, (n + 1) * GROUP)


def col_of(h):
    return slice(h * DK, (h + 1) * DK)


def span_of(beta, n):
    return beta[(n + 1) * GROUP - 1 : (n + 1) * GROUP]


def prep_body(q, g, v, w, give):
    first = is_first()
    for i, ref in enumerate((q, g, v)):
        give[i * TOK : (i + 1) * TOK] = pick(first, ref[:, WIDTH:], ref[:, :WIDTH])
    rows = pick(first, w[:, WIDTH:], w[:, :WIDTH]).astype(F32)
    give[3 * TOK :] = jnp.concatenate([rows, jnp.zeros_like(rows)], axis=0).astype(BF16)


def gates_body(own, peer, down, up, bias, q, g, v, w, got,
               tok, lat, logit, beta, q_o, g_o, v_o, w_o, adds, send):
    first = is_first()
    tok[:TOK] = pick(first, own[...], peer[...])
    tok[TOK:] = pick(first, peer[...], own[...])
    for i, (ref, out) in enumerate(((q, q_o), (g, g_o), (v, v_o))):
        mine = pick(first, ref[:, :WIDTH], ref[:, WIDTH:])
        theirs = got[i * TOK : (i + 1) * TOK]
        out[:TOK] = pick(first, mine, theirs)
        out[TOK:] = pick(first, theirs, mine)
    mine = pick(first, w[:, :WIDTH], w[:, WIDTH:]).astype(F32)
    theirs = got[3 * TOK :].astype(F32)[:8]
    w_o[...] = jnp.concatenate(
        [pick(first, mine, theirs), pick(first, theirs, mine)], axis=0
    ).astype(BF16)
    latent = dot(tok[...], down[...], NT).astype(BF16)
    lat[...] = latent
    up_half = pick(first, up[:, :WIDTH], up[:, WIDTH:])
    bias_half = pick(first, bias[:, :WIDTH], bias[:, WIDTH:])
    x = dot(latent, up_half) + bias_half
    logit[...] = x
    gamma = (jnp.minimum(x, 0.0) - jnp.log1p(jnp.exp(-jnp.abs(x)))) * (1.0 / 16.0)
    lower = low_mask()[0].astype(BF16)
    run = [jnp.zeros((DK, DK), F32)] * HALF
    total = jnp.zeros((1, WIDTH), F32)
    for n in reversed(range(BLOCKS)):
        b = dot_mask(lower, gamma[tok_of(n)])
        beta[tok_of(n)] = b
        last = b[GROUP - 1 : GROUP]
        total = total + last
        decay = jnp.exp(last)
        scaled = q_o[tok_of(n)].astype(F32) * jnp.exp(b)
        grad = g_o[tok_of(n)]
        for h in range(HALF):
            part = dot_hl(grad[:, col_of(h)], scaled[:, col_of(h)], TN)
            adds[n, col_of(h)] = part
            run[h] = decay[:, col_of(h)] * run[h] + part
    decay = jnp.exp(total)
    for p in range(PS):
        h, at = p // PER, (p % PER) * ROWS
        send[p, :ROWS] = run[h][at : at + ROWS]
        send[p, ROWS:] = jnp.broadcast_to(decay[:, col_of(h)], (8, DK))


def scan_back_body(recv, wz, send):
    run = jnp.zeros((ROWS, DK), F32)
    w = wz[...]
    for p in reversed(range(PS)):
        send[p, : ZS * 16] = w
        wide = jnp.concatenate([run[8 * i : 8 * i + 8] for i in range(ROWS // 8)], axis=1)
        hi = wide.astype(BF16).astype(F32)
        send[p, ZS * 16 :] = jnp.concatenate([hi, wide - hi], axis=0).astype(BF16)
        run = recv[p, ROWS : ROWS + 1] * run + recv[p, :ROWS]


def unpack_w(recv, w):
    for p in range(PS):
        for z in range(ZS):
            w[z * 256 + p * 16 : z * 256 + p * 16 + 16] = recv[p, z * 16 : z * 16 + 16]


def added_states(key, v, beta, n):
    b = beta[tok_of(n)]
    last = b[GROUP - 1 : GROUP]
    tail = key[tok_of(n)].astype(F32) * jnp.exp(last - b)
    vals = v[tok_of(n)]
    return [dot_hl(vals[:, col_of(h)], tail[:, col_of(h)], TN) for h in range(HALF)], jnp.exp(last)


def keys_body(recv, tok, beta, v, key_o, send, w):
    unpack_w(recv, w)
    key_o[...] = dot(tok[...], w[...]).astype(BF16)
    run = [jnp.zeros((DK, DK), F32)] * HALF
    for n in range(BLOCKS):
        parts, decay = added_states(key_o, v, beta, n)
        run = [decay[:, col_of(h)] * run[h] + parts[h] for h in range(HALF)]
    for p in range(PS):
        h, at = p // PER, (p % PER) * ROWS
        send[p] = run[h][at : at + ROWS]


def scan_fwd_body(recv, old, after, send):
    run = jnp.zeros((ROWS, DK), F32)
    for p in range(PS):
        send[p] = run
        run = old[p, ROWS : ROWS + 1] * run + recv[p]


def delta_body(q_r, g_r, v_r, key_r, beta, recv, adds, tok,
               kd_o, local, gin, o_0, o_1, o_2, o_3, blocks):
    low, high = low_mask()
    for p in range(PS):
        both = recv[p, ZS * 16 :].astype(F32)
        wide = both[:8] + both[8:]
        for i in range(ROWS // 8):
            gin[p * ROWS + 8 * i : p * ROWS + 8 * i + 8] = wide[:, col_of(i)]
    run = [gin[col_of(h)] for h in range(HALF)]
    for n in reversed(range(BLOCKS)):
        b = beta[tok_of(n)]
        last = b[GROUP - 1 : GROUP]
        grow, shrink, tail = jnp.exp(b), jnp.exp(-b), jnp.exp(last - b)
        decay = jnp.exp(last)
        q = q_r[tok_of(n)].astype(F32)
        k = key_r[tok_of(n)].astype(F32)
        q_s, k_s = q * grow, k * shrink
        for h in range(HALF):
            c = col_of(h)
            g, v = g_r[tok_of(n), c], v_r[tok_of(n), c]
            pairs = jnp.where(low, dot(g, v, NT), 0.0)
            pairs_t = jnp.where(high, dot(v, g, NT), 0.0)
            kd = tail[:, c] * dot_hl(v, run[h]) + shrink[:, c] * dot_ff(pairs_t, q_s[:, c])
            qd = grow[:, c] * dot_ff(pairs, k_s[:, c])
            kd_o[tok_of(n), c] = kd.astype(BF16)
            local[tok_of(n), c] = q[:, c] * qd - k[:, c] * kd
            run[h] = decay[:, c] * run[h] + adds[n, c]
    kd = kd_o[...]
    for z in range(ZS):
        block = dot(tok[:, z * 256 : z * 256 + 256], kd, TN).astype(BF16)
        for x in range(4):
            blocks[x, z] = block[x * 64 : x * 64 + 64]
    place = lax.axis_index("x")
    for k, out in enumerate((o_0, o_1, o_2, o_3)):
        to = lax.rem(place + k, 4)
        for z in range(ZS):
            for y in range(4):
                out[y, z * 16 : z * 16 + 16] = blocks[to, z, y * 16 : y * 16 + 16]


def y_body(a, b, c, d, own, o_1, o_2, o_3, total):
    for y in range(4):
        total[y] = (a[y].astype(F32) + b[y].astype(F32)) + (c[y].astype(F32) + d[y].astype(F32))
    place = lax.axis_index("y")
    own[...] = total[place]
    for k, out in enumerate((o_1, o_2, o_3)):
        out[...] = total[lax.rem(place + k + 1, 4)].astype(BF16)


def gate_body(sin, gin, key_r, v_r, beta, q_r, g_r, local, logit, lat, up,
              gate_o, gate_keep, gate_give, up_part, lat_part, delta):
    first = is_first()
    high = low_mask()[1].astype(BF16)
    run = [sin[h * PER : (h + 1) * PER].reshape(DK, DK) for h in range(HALF)]
    for n in range(BLOCKS):
        parts, decay = added_states(key_r, v_r, beta, n)
        qd = jnp.concatenate(
            [dot_hl(g_r[tok_of(n), col_of(h)], run[h]) for h in range(HALF)], axis=1
        ) * jnp.exp(beta[tok_of(n)])
        delta[tok_of(n)] = q_r[tok_of(n)].astype(F32) * qd + local[tok_of(n)]
        run = [decay[:, col_of(h)] * run[h] + parts[h] for h in range(HALF)]
    beyond = jnp.concatenate(
        [jnp.sum(run[h] * gin[col_of(h)], axis=0, keepdims=True) for h in range(HALF)], axis=1
    )
    for n in reversed(range(BLOCKS)):
        suffix = dot_mask(high, delta[tok_of(n)]) + beyond
        beyond = suffix[:1]
        x = logit[tok_of(n)]
        gate_o[tok_of(n)] = (suffix * (1.0 / (1.0 + jnp.exp(x))) * (1.0 / 16.0)).astype(BF16)
    gate = gate_o[...]
    gate_keep[...] = pick(first, gate[:TOK], gate[TOK:])
    gate_give[...] = pick(first, gate[TOK:], gate[:TOK])
    up_half = pick(first, up[:, :WIDTH], up[:, WIDTH:])
    up_part[...] = dot(lat[...], gate, TN)
    lat_part[...] = dot(gate, up_half, NT)


def down_body(lat_a, lat_b, tok, up_part, lat_o, send):
    first = is_first()
    latent = (lat_a[...] + lat_b[...]).astype(BF16)
    lat_o[...] = pick(first, latent[:TOK], latent[TOK:])
    half = MODEL // 2
    down = dot(latent, pick(first, tok[:, :half], tok[:, half:]), TN)
    for j in range(WIDTH // DK):
        send[:, j] = up_part[:, col_of(j)]
    for j in range(half // DK):
        send[:, WIDTH // DK + j] = down[:, col_of(j)]


def through_body(kd, recv, keep, give, w):
    first = is_first()
    unpack_w(recv, w)
    mine = pick(first, kd[:TOK], kd[TOK:])
    other = pick(first, kd[TOK:], kd[:TOK])
    give[...] = dot(other, w[...], NT)
    keep[...] = dot(mine, w[...], NT)


def input_body(keep, got, lat, down, out):
    out[...] = (keep[...] + got[...] + dot(lat[...], down[...])).astype(BF16)


PARTS = (WIDTH + MODEL // 2) // DK
PER = DK // ROWS


def mid_body(own, a, b, c, small, send):
    wsum = (own[...] + a[...].astype(F32)) + (b[...].astype(F32) + c[...].astype(F32))
    total = jnp.sum(small[...], axis=0)
    wide = jnp.concatenate(
        [jnp.concatenate([total[4 * i + j : 4 * i + j + 1] for j in range(4)], axis=1)
         for i in range(PARTS // 4)], axis=0)
    hi = wide.astype(BF16).astype(F32)
    extra = jnp.concatenate([hi, wide - hi, jnp.zeros((10, WIDTH), F32)], axis=0).astype(BF16)
    for z in range(ZS):
        send[z, :16] = wsum[z * 16 : z * 16 + 16].astype(BF16)
        send[z, 16:] = extra


def last_body(recv, keep, give):
    first = is_first()
    total = jnp.sum(recv[...].astype(F32), axis=0)
    small = total[16:19] + total[19:22]
    pad = jnp.zeros((5, WIDTH), F32)
    keep[...] = jnp.concatenate([pick(first, total[:8], total[8:16]), small, pad], axis=0)
    give[...] = jnp.concatenate([pick(first, total[8:16], total[:8]), small, pad], axis=0)


def pack_body(mine, theirs, w_o, send):
    first = is_first()
    a, b = pick(first, mine[...], theirs[...]), pick(first, theirs[...], mine[...])
    w_o[:, :WIDTH] = a[:8]
    w_o[:, WIDTH:] = b[:8]
    both = jnp.concatenate([a[8:11], b[8:11], jnp.zeros((2, WIDTH), F32)], axis=0)
    for p in range(PS):
        send[p] = both


def out_body(recv, down_o, up_o):
    for half in range(2):
        at = half * 3
        up_o[:, half * WIDTH : (half + 1) * WIDTH] = recv[:, at]
        for i in range(2):
            lo = half * 2 * WIDTH + i * WIDTH
            down_o[:, lo : lo + WIDTH] = recv[:, at + 1 + i]


def swap(a):
    return lax.ppermute(a, "c", SWAP)


def ring(a, axis, step):
    return lax.ppermute(a, axis, [(i, (i + step) % 4) for i in range(4)])


def a2a(a, axis):
    return lax.all_to_all(a, axis, 0, 0)


def local(inputs, queries, values, out_grad, key_weight, gate_down, gate_up, gate_bias):
    first = is_first()
    own = inputs[0]
    q, g, v = queries[0], out_grad[0], values[0]
    give = kernel(prep_body, shape((3 * TOK + 16, WIDTH), BF16), "prep", 8)(q, g, v, key_weight)
    half_bf = shape((PAIR, WIDTH), BF16)
    half_f = shape((PAIR, WIDTH))
    tok, lat, logit, beta, q, g, v, wz, add_g, send1 = kernel(
        gates_body,
        (shape((PAIR, MODEL), BF16), shape((PAIR, RANK), BF16), half_f, half_f,
         half_bf, half_bf, half_bf, shape((16, WIDTH), BF16),
         shape((BLOCKS, WIDTH, DK)), shape((PS, ROWS + 8, DK))),
        "gates", BIG,
    )(own, swap(own), gate_down, gate_up, gate_bias[None], q, g, v, key_weight, swap(give))
    place = lax.axis_index("z")
    for bit in (1, 2, 4):
        other = lax.ppermute(wz, "z", [(i, i ^ bit) for i in range(ZS)])
        even = (place & bit) == 0
        wz = jnp.concatenate([jnp.where(even, wz, other), jnp.where(even, other, wz)], axis=0)

    recv1 = a2a(send1, XY)
    send2 = kernel(scan_back_body, shape((PS, ZS * 16 + 16, WIDTH), BF16), "scan_back", 8)(recv1, wz)
    recv2 = a2a(send2, XY)
    keys, send3 = kernel(
        keys_body, (half_bf, shape((PS, ROWS, DK))), "keys", KEYS,
        scratch=[pltpu.VMEM((MODEL, WIDTH), BF16)],
    )(recv2, tok, beta, v)
    recv3 = a2a(send3, XY)
    kd, local_part, gin, o_0, o_1, o_2, o_3 = kernel(
        delta_body,
        (half_bf, half_f, shape((WIDTH, DK))) + (shape((4, ZS * 16, WIDTH), BF16),) * 4,
        "delta", BIG, scratch=[pltpu.VMEM((4, ZS, 64, WIDTH), BF16)],
    )(q, g, v, keys, beta, recv2, add_g, tok)
    x_sums = [ring(a, "x", k + 1) for k, a in enumerate((o_1, o_2, o_3))]
    send4 = kernel(
        scan_fwd_body, shape((PS, ROWS, DK)), "scan_fwd", 8,
        specs=[pl.BlockSpec(memory_space=pltpu.VMEM)] * 2 + [pl.BlockSpec(memory_space=pl.ANY)],
    )(recv3, recv1, kd)
    recv4 = a2a(send4, XY)
    y_own, y_1, y_2, y_3 = kernel(
        y_body,
        (shape((ZS * 16, WIDTH)),) + (shape((ZS * 16, WIDTH), BF16),) * 3,
        "y_sums", BIG, scratch=[pltpu.VMEM((4, ZS * 16, WIDTH), F32)],
    )(o_0, *x_sums)
    y_sums = [ring(a, "y", k + 1) for k, a in enumerate((y_1, y_2, y_3))]
    gate, gate_m, gate_x, up_part, lat_part = kernel(
        gate_body,
        (half_bf, shape((TOK, WIDTH), BF16), shape((TOK, WIDTH), BF16),
         shape((RANK, WIDTH)), shape((PAIR, RANK))),
        "gate", BIG, scratch=[pltpu.VMEM((PAIR, WIDTH), F32)],
    )(recv4, gin, keys, v, beta, q, g, local_part, logit, lat, gate_up)
    lat_own, send5 = kernel(
        down_body, (shape((TOK, RANK), BF16), shape((PS, PARTS, DK))), "down", 8
    )(lat_part, swap(lat_part), tok, up_part)
    send6 = kernel(mid_body, shape((ZS, 32, WIDTH), BF16), "mid", 8)(
        y_own, *y_sums, a2a(send5, XY)
    )
    recv6 = a2a(send6, "z")
    keep, theirs = kernel(last_body, (shape((16, WIDTH)), shape((16, WIDTH))), "last", 4)(recv6)
    key_weight_grad, send7 = kernel(
        pack_body, (shape((8, 2 * WIDTH)), shape((PS, 8, WIDTH))), "pack", 4
    )(keep, swap(theirs))
    down_grad, up_grad = kernel(
        out_body, (shape((RANK, MODEL)), shape((RANK, 2 * WIDTH))), "grads", 4
    )(a2a(send7, XY))

    gate_p = swap(gate_x)
    gate_grad = jnp.concatenate(
        [jnp.where(first, gate_m, gate_p), jnp.where(first, gate_p, gate_m)], axis=1
    )
    mine, other = kernel(
        through_body, (shape((TOK, MODEL)), shape((TOK, MODEL))), "through", BIG,
        scratch=[pltpu.VMEM((MODEL, WIDTH), BF16)],
    )(kd, recv2)
    input_grad = kernel(input_body, shape((TOK, MODEL), BF16), "input", 16)(
        mine, swap(other), lat_own, gate_down
    )
    return (input_grad[None], gate_grad[None], key_weight_grad, down_grad, up_grad)


def solution(mesh):
    grid = Mesh(mesh.devices.reshape(8, 4, 4, 2), ("z", "x", "y", "c"))
    seq = ("x", "y", "c")
    tok = P("z", seq, None)
    row = P(("z",) + seq, None)
    return jax.shard_map(
        local,
        mesh=grid,
        in_specs=(tok, tok, tok, tok, row, P(), P(), P()),
        out_specs=(tok, tok, row, P(), P()),
        check_vma=False,
    )
```

time: 250 us -> 187 us (0.75)
  blocking collectives: 9.88 us -> 61.2 us
  waiting for transfers between devices: 77.9 us -> 30.2 us
  other arithmetic: 35.1 us -> 1.55 us
  Pallas kernels: 0 us -> 30.6 us
  starting transfers between devices: 75.9 us -> 50.8 us
  matrix products: 22 us -> 0 us
  local copies, waits for them, and re-layouts: 25.3 us -> 10.9 us
    all_to_all x11 -> x4, waiting for transfers between devices: 75.8 us -> 21 us  [a2a(): return lax.all_to_all(a, axis, 0, 0)]
    all_to_all x1 -> x3, blocking collectives: 9.88 us -> 61.2 us  [a2a(): return lax.all_to_all(a, axis, 0, 0)]
    all_to_all x11 -> x4, starting transfers between devices: 50.7 us -> 18.6 us  [a2a(): return lax.all_to_all(a, axis, 0, 0)]
    pallas_call x0 -> x15, Pallas kernels: none -> 30.6 us  [the longest x1 8.01 us: local(): kernel(delta_body, (half_bf, half_f, shape((WIDTH, DK))) + (shape((4, ZS...]
    unnamed x16 -> x0, other arithmetic: 22.1 us -> none
    dot_general x18 -> x0, matrix products: 22 us -> none  [the longest x1 2.84 us: local(): jnp.einsum('nhij,nihk->njhk', pairs, query_scaled, precision=HI)]
    ppermute x0 -> x9, starting transfers between devices: none -> 14.1 us  [the longest x6 7.67 us: ring(): return lax.ppermute(a, axis, [(i, (i + step) % 4) for i in range(4)])]
    ppermute x8 -> x6, starting transfers between devices: 25.2 us -> 18 us  [swap(): return lax.ppermute(a, 'c', SWAP)]
  transfers between devices with their start and end apart: 19 -> 19, of which waited for: 12 -> 8; matrix products, arithmetic and copies ran while one was open for 19% -> 0% of each run, Pallas kernels for 0% -> 8%
where the time goes in v2:
time: 187 us; the launch traced here: 186 us
  blocking collectives  61.2 us (33%)
  starting transfers between devices  50.8 us (27%)
  Pallas kernels  30.6 us (16%)
  waiting for transfers between devices  30.2 us (16%)
  local copies, waits for them, and re-layouts  10.9 us (6%)
    all_to_all x3, blocking collectives, a2a(): return lax.all_to_all(a, axis, 0, 0)  61.2 us
    all_to_all x4, waiting for transfers between devices, a2a(): return lax.all_to_all(a, axis, 0, 0)  21 us
    all_to_all x4, starting transfers between devices, a2a(): return lax.all_to_all(a, axis, 0, 0)  18.6 us
    ppermute x6, starting transfers between devices, swap(): return lax.ppermute(a, 'c', SWAP)  18 us
    unnamed x50, local copies, waits for them, and re-layouts  10.9 us
    pallas_call x1, Pallas kernels, local(): kernel(delta_body, (half_bf, half_f, shape((WIDTH, DK))) + (shape((4, ZS...  8.01 us
    ppermute x6, starting transfers between devices, ring(): return lax.ppermute(a, axis, [(i, (i + step) % 4) for i in range(4)])  7.67 us
    ppermute x3, starting transfers between devices, local(): other = lax.ppermute(wz, 'z', [(i, i ^ bit) for i in range(ZS)])  6.43 us
  transfers between devices with their start and end apart: 19, of which 8 were waited for; matrix products, arithmetic and copies ran while one was open for 0% of the time, Pallas kernels for 8%

profile of v2, /device:TPU:1, one launch (start us, length us, event | category | flops | bytes accessed | tf_op | source)
XLA Modules:
  0.0 186.0 jit_solution(4696927336622997176)
XLA Ops:
  0.6 3.3 %collective-permute-start = (bf16[128,2048]{1,0:T(8,128)(2,1)}, bf16[128,2048]{1,0:T(8,128)(2,1)S(1)}, u32[]{:S(2)}, u32[]{:S(2)}) collective-permute-start(bf16[128,2048]{1,0:T(8,128)(2,1)} %bitcast.14), channel_id=1, source_target_pairs={{0,1},{1,0},{2,3},{3,2},{4,5},{5,4},{6,7},{7,6},{8,9},{9,8},{10,11... | collective-permute-start | bytes 1572872 | tf_op jit(solution)/shard_map/ppermute | solution.py:348
  4.0 0.9 copy-done.7
  4.9 0.9 copy-done.8
  5.9 0.9 copy-done.9
  6.8 0.7 copy-done.16
  7.6 0.1 collective-permute-start.1
  7.7 1.7 collective-permute-done.1.got
  9.4 0.0 collective-permute-done.peer
  9.4 0.8 copy-done.23
  10.2 0.2 copy-done.22
  10.3 5.1 %gates.1 = (bf16[256,2048]{1,0:T(8,128)(2,1)}, bf16[256,16]{1,0:T(8,128)(2,1)}, f32[256,512]{1,0:T(8,128)}, f32[256,512]{1,0:T(8,128)}, bf16[256,512]{1,0:T(8,12...) custom-call(bf16[128,2048]{1,0:T(8,128)(2,1)} %bitcast.15, ...), custom_call_target="tpu_custom_call" | custom-call | tf_op jit(solution)/shard_map/gates/pallas_call | solution.py:366
  15.4 2.8 %collective-permute-done.2 = bf16[16,512]{1,0:T(8,128)(2,1)S(1)} collective-permute-done((bf16[16,512]{1,0:T(8,128)(2,1)}, bf16[16,512]{1,0:T(8,128)(2,1)S(1)}, u32[]{:S(2)}, u32[]{:S(2)}) %collective-permute-start.2) | collective-permute-done | bytes 16416 | tf_op jit(solution)/shard_map/ppermute | solution.py:375
  18.2 0.7 broadcast_select_fusion.7
  19.0 1.5 collective-permute-start.3
  20.5 2.6 %collective-permute-done.3 = bf16[32,512]{1,0:T(8,128)(2,1)S(1)} collective-permute-done((bf16[32,512]{1,0:T(8,128)(2,1)S(1)}, bf16[32,512]{1,0:T(8,128)(2,1)S(1)}, u32[]{:S(2)}, u32[]{:S(2)}) %collective-permute-start.3) | collective-permute-done | bytes 32800 | tf_op jit(solution)/shard_map/ppermute | solution.py:375
  23.1 4.9 %collective-permute-start.4 = (bf16[64,512]{1,0:T(8,128)(2,1)S(1)}, bf16[64,512]{1,0:T(8,128)(2,1)S(1)}, u32[]{:S(2)}, u32[]{:S(2)}) collective-permute-start(bf16[64,512]{1,0:T(8,128)(2,1)S(1)} %pad_maximum_fusion.1), channel_id=1, source_target_pairs={{0,128},{32,160},{64,192},{96,224},{128,0},{160,32},{192,64},{224,... | collective-permute-start | bytes 196616 | tf_op jit(solution)/shard_map/ppermute | solution.py:375
  28.0 6.8 %all-to-all-start = ((f32[16,40,128]{2,1,0:T(8,128)}), f32[16,40,128]{2,1,0:T(8,128)S(1)}, u32[]{:S(2)}, u32[]{:S(2)}) async-start(f32[16,40,128]{2,1,0:T(8,128)} %get-tuple-element.45), calls=%async_computation | async-start | bytes 655360 | tf_op jit(solution)/shard_map/all_to_all | solution.py:356
  34.8 7.7 %all-to-all-done.recv.old = f32[16,40,128]{2,1,0:T(8,128)S(1)} async-done(((f32[16,40,128]{2,1,0:T(8,128)}), f32[16,40,128]{2,1,0:T(8,128)S(1)}, u32[]{:S(2)}, u32[]{:S(2)}) %all-to-all-start) | async-done | bytes 327712 | tf_op jit(solution)/shard_map/all_to_all | solution.py:356
  42.5 0.2 scan_back.1
  42.8 0.7 copy-done.4
  43.5 29.8 %all_to_all.35.recv = bf16[16,144,512]{2,1,0:T(8,128)(2,1)S(1)} all-to-all(bf16[16,144,512]{2,1,0:T(8,128)(2,1)S(1)} %scan_back.1), channel_id=1, replica_groups=mesh['z'=8,'x'=4,'y'=4,'c'=2] {'x','y'}, dimensions={0} | all-to-all | bytes 4718592 | tf_op jit(solution)/shard_map/all_to_all | solution.py:356
  73.4 1.1 keys.1
  74.5 0.7 copy-done.10
  75.2 8.0 %delta.1 = (bf16[256,512]{1,0:T(8,128)(2,1)}, f32[256,512]{1,0:T(8,128)}, f32[512,128]{1,0:T(8,128)}, bf16[4,128,512]{2,1,0:T(8,128)(2,1)}, bf16[4,128,512]{2,1,...) custom-call(bf16[256,512]{1,0:T(8,128)(2,1)} %get-tuple-element.42.q_r, ...), custom_call_target="tpu_custom_call" | custom-call | tf_op jit(solution)/shard_map/delta/pallas_call | solution.py:387
  83.2 1.3 collective-permute-start.10
  84.5 0.2 collective-permute-start.8
  84.7 1.3 collective-permute-start.9
  86.0 20.5 %all_to_all.36.recv = f32[16,32,128]{2,1,0:T(8,128)S(1)} all-to-all(f32[16,32,128]{2,1,0:T(8,128)S(1)} %get-tuple-element.54), channel_id=1, replica_groups=mesh['z'=8,'x'=4,'y'=4,'c'=2] {'x','y'}, dimensions={0} | all-to-all | bytes 524288 | tf_op jit(solution)/shard_map/all_to_all | solution.py:356
  106.5 0.9 copy-done.11
  107.5 0.7 scan_fwd.1
  108.2 4.9 %all-to-all-start.3 = ((f32[16,32,128]{2,1,0:T(8,128)}), f32[16,32,128]{2,1,0:T(8,128)S(1)}, u32[]{:S(2)}, u32[]{:S(2)}) async-start(f32[16,32,128]{2,1,0:T(8,128)} %scan_fwd.1), calls=%async_computation.3 | async-start | bytes 524288 | tf_op jit(solution)/shard_map/all_to_all | solution.py:356
  113.1 4.2 %through.1 = (f32[128,2048]{1,0:T(8,128)}, f32[128,2048]{1,0:T(8,128)}) custom-call(bf16[256,512]{1,0:T(8,128)(2,1)} %get-tuple-element.51.kd.after, bf16[16,144,512]{2,1,0:T(8,128)(2,1)} %copy-done), custom_call_target="tpu_custom_call" | custom-call | tf_op jit(solution)/shard_map/through/pallas_call | solution.py:429
  117.3 8.4 %collective-permute-start.5 = (f32[128,2048]{1,0:T(8,128)}, f32[128,2048]{1,0:T(8,128)S(1)}, u32[]{:S(2)}, u32[]{:S(2)}) collective-permute-start(f32[128,2048]{1,0:T(8,128)} %get-tuple-element.53), channel_id=1, source_target_pairs={{0,1},{1,0},{2,3},{3,2},{4,5},{5,4},{6,7},{7,6},{8,9},{9,8},{10,11... | collective-permute-start | bytes 3145736 | tf_op jit(solution)/shard_map/ppermute | solution.py:348
  125.7 0.0 collective-permute-done.9.c
  125.8 0.8 copy-done.20
  126.6 0.8 copy-done.21
  127.4 2.8 %y_sums.1 = (f32[128,512]{1,0:T(8,128)}, bf16[128,512]{1,0:T(8,128)(2,1)}, bf16[128,512]{1,0:T(8,128)(2,1)}, bf16[128,512]{1,0:T(8,128)(2,1)}) custom-call(bf16[4,128,512]{2,1,0:T(8,128)(2,1)} %get-tuple-element.64.a, bf16[4,128,512]{2,1,0:T(8,128)(2,1)} %copy-done.20, bf16[4,128,512]{2,1,0:T(8,128)(2,1)} %copy-done.21, bf16[4,128,512]{2,1,0:T(8,128)(2,1)} %copy-done.19), custom_call_target="tpu_custom_call" | custom-call | tf_op jit(solution)/shard_map/y_sums/pallas_call | solution.py:398
  130.2 1.3 collective-permute-start.11
  131.5 2.4 %collective-permute-start.12 = (bf16[128,512]{1,0:T(8,128)(2,1)}, bf16[128,512]{1,0:T(8,128)(2,1)S(1)}, u32[]{:S(2)}, u32[]{:S(2)}) collective-permute-start(bf16[128,512]{1,0:T(8,128)(2,1)} %get-tuple-element.70), channel_id=1, source_target_pairs={{0,4},{2,6},{4,0},{6,2},{1,5},{3,7},{5,1},{7,3},{8,12},{10,14},{12... | collective-permute-start | bytes 393224 | tf_op jit(solution)/shard_map/ppermute | solution.py:352
  133.9 1.2 collective-permute-start.13
  135.1 0.0 all-to-all-done.3.sin
  135.1 0.7 copy-done.18
  135.8 3.9 %gate.1 = (bf16[256,512]{1,0:T(8,128)(2,1)}, bf16[128,512]{1,0:T(8,128)(2,1)}, bf16[128,512]{1,0:T(8,128)(2,1)}, f32[16,512]{1,0:T(8,128)}, f32[256,16]{1,0:T(8,128)}) custom-call(f32[16,32,128]{2,1,0:T(8,128)} %copy-done.18, f32[512,128]{1,0:T(8,128)} %get-tuple-element.55.gin, bf16[256,512]{1,0:T(8,128)(2,1)} %copy-done.10, ...), custom_call_target="tpu_custom_call" | custom-call | tf_op jit(solution)/shard_map/gate/pallas_call | solution.py:404
  139.7 0.9 collective-permute-start.6
  140.6 1.2 collective-permute-done.6.lat_b
  141.8 0.9 copy-done.15
  142.7 0.8 copy-done.17
  143.4 0.2 down.4
  143.7 0.0 copy-start.24
  143.7 10.8 %all_to_all.37.small = f32[16,12,128]{2,1,0:T(8,128)S(1)} all-to-all(f32[16,12,128]{2,1,0:T(8,128)S(1)} %get-tuple-element.72), channel_id=1, replica_groups=mesh['z'=8,'x'=4,'y'=4,'c'=2] {'x','y'}, dimensions={0} | all-to-all | bytes 196608 | tf_op jit(solution)/shard_map/all_to_all | solution.py:356
  154.5 0.0 collective-permute-done.11.a
  154.5 0.0 collective-permute-done.12.b
  154.5 1.7 mid.1
  156.2 3.4 %all-to-all-start.5 = ((bf16[8,32,512]{2,1,0:T(8,128)(2,1)}), bf16[8,32,512]{2,1,0:T(8,128)(2,1)S(1)}, u32[]{:S(2)}, u32[]{:S(2)}) async-start(bf16[8,32,512]{2,1,0:T(8,128)(2,1)} %mid.1), calls=%async_computation.5 | async-start | bytes 524288 | tf_op jit(solution)/shard_map/all_to_all | solution.py:356
  159.6 1.9 %collective-permute-start.7 = (bf16[128,512]{1,0:T(8,128)(2,1)}, bf16[128,512]{1,0:T(8,128)(2,1)S(1)}, u32[]{:S(2)}, u32[]{:S(2)}) collective-permute-start(bf16[128,512]{1,0:T(8,128)(2,1)} %get-tuple-element.63), channel_id=1, source_target_pairs={{0,1},{1,0},{2,3},{3,2},{4,5},{5,4},{6,7},{7,6},{8,9},{9,8},{10,11... | collective-permute-start | bytes 393224 | tf_op jit(solution)/shard_map/ppermute | solution.py:348
  161.5 7.5 %all-to-all-done.5.recv = bf16[8,32,512]{2,1,0:T(8,128)(2,1)S(1)} async-done(((bf16[8,32,512]{2,1,0:T(8,128)(2,1)}), bf16[8,32,512]{2,1,0:T(8,128)(2,1)S(1)}, u32[]{:S(2)}, u32[]{:S(2)}) %all-to-all-start.5) | async-done | bytes 262176 | tf_op jit(solution)/shard_map/all_to_all | solution.py:356
  169.0 3.4 %collective-permute-start.14 = (f32[16,512]{1,0:T(8,128)S(1)}, f32[16,512]{1,0:T(8,128)S(1)}, u32[]{:S(2)}, u32[]{:S(2)}) collective-permute-start(f32[16,512]{1,0:T(8,128)S(1)} %get-tuple-element.74), channel_id=1, source_target_pairs={{0,1},{1,0},{2,3},{3,2},{4,5},{5,4},{6,7},{7,6},{8,9},{9,8},{10,11... | collective-permute-start | bytes 98312 | tf_op jit(solution)/shard_map/ppermute | solution.py:348
  172.4 0.9 collective-permute-done.14.theirs
  173.3 0.7 pack.1
  174.1 3.6 %all-to-all-start.6 = ((f32[16,8,512]{2,1,0:T(8,128)}), f32[16,8,512]{2,1,0:T(8,128)S(1)}, u32[]{:S(2)}, u32[]{:S(2)}) async-start(f32[16,8,512]{2,1,0:T(8,128)} %get-tuple-element.76), calls=%async_computation.6 | async-start | bytes 524288 | tf_op jit(solution)/shard_map/all_to_all | solution.py:356
  177.7 0.7 maximum_bitcast_fusion
  178.5 1.1 input.1
  179.5 5.7 %all-to-all-done.6.recv = f32[16,8,512]{2,1,0:T(8,128)S(1)} async-done(((f32[16,8,512]{2,1,0:T(8,128)}), f32[16,8,512]{2,1,0:T(8,128)S(1)}, u32[]{:S(2)}, u32[]{:S(2)}) %all-to-all-start.6) | async-done | bytes 262176 | tf_op jit(solution)/shard_map/all_to_all | solution.py:356
  185.2 0.7 grads.1
  (50 shorter events, 0.3 us)
Async XLA Ops:
  0.6 8.8 %collective-permute-start = (bf16[128,2048]{1,0:T(8,128)(2,1)}, bf16[128,2048]{1,0:T(8,128)(2,1)S(1)}, u32[]{:S(2)}, u32[]{:S(2)}) collective-permute-start(bf16[128,2048]{1,0:T(8,128)(2,1)} %bitcast.14), channel_id=1, source_target_pairs={{0,1},{1,0},{2,3},{3,2},{4,5},{5,4},{6,7},{7,6},{8,9},{9,8},{10,11... | collective-permute-start | bytes 1572872 | tf_op jit(solution)/shard_map/ppermute | solution.py:348
  4.0 0.9 copy-start.7
  4.9 0.9 copy-start.8
  5.9 0.9 copy-start.9
  6.8 0.7 copy-start.16
  7.6 1.8 collective-permute-start.1
  9.4 0.8 copy-start.23
  9.4 0.9 copy-start.22
  15.4 2.8 %collective-permute-start.2 = (bf16[16,512]{1,0:T(8,128)(2,1)}, bf16[16,512]{1,0:T(8,128)(2,1)S(1)}, u32[]{:S(2)}, u32[]{:S(2)}) collective-permute-start(bf16[16,512]{1,0:T(8,128)(2,1)} %get-tuple-element.46), channel_id=1, source_target_pairs={{0,32},{32,0},{64,96},{96,64},{128,160},{160,128},{192,224},{224,1... | collective-permute-start | bytes 49160 | tf_op jit(solution)/shard_map/ppermute | solution.py:375
  19.0 4.1 %collective-permute-start.3 = (bf16[32,512]{1,0:T(8,128)(2,1)S(1)}, bf16[32,512]{1,0:T(8,128)(2,1)S(1)}, u32[]{:S(2)}, u32[]{:S(2)}) collective-permute-start(bf16[32,512]{1,0:T(8,128)(2,1)S(1)} %pad_maximum_fusion.2), channel_id=1, source_target_pairs={{0,64},{32,96},{64,0},{96,32},{128,192},{160,224},{192,128},{224,1... | collective-permute-start | bytes 98312 | tf_op jit(solution)/shard_map/ppermute | solution.py:375
  23.1 11.7 %collective-permute-start.4 = (bf16[64,512]{1,0:T(8,128)(2,1)S(1)}, bf16[64,512]{1,0:T(8,128)(2,1)S(1)}, u32[]{:S(2)}, u32[]{:S(2)}) collective-permute-start(bf16[64,512]{1,0:T(8,128)(2,1)S(1)} %pad_maximum_fusion.1), channel_id=1, source_target_pairs={{0,128},{32,160},{64,192},{96,224},{128,0},{160,32},{192,64},{224,... | collective-permute-start | bytes 196616 | tf_op jit(solution)/shard_map/ppermute | solution.py:375
  28.0 14.5 %all-to-all-start = ((f32[16,40,128]{2,1,0:T(8,128)}), f32[16,40,128]{2,1,0:T(8,128)S(1)}, u32[]{:S(2)}, u32[]{:S(2)}) async-start(f32[16,40,128]{2,1,0:T(8,128)} %get-tuple-element.45), calls=%async_computation | async-start | bytes 655360 | tf_op jit(solution)/shard_map/all_to_all | solution.py:356
  42.8 0.8 copy-start.4
  43.5 29.9 %copy-start.1 = (bf16[256,2048]{1,0:T(8,128)(2,1)S(1)}, bf16[256,2048]{1,0:T(8,128)(2,1)}, u32[]{:S(2)}) copy-start(bf16[256,2048]{1,0:T(8,128)(2,1)} %get-tuple-element.47.tok) | copy-start | bytes 3145732
  43.5 29.9 %copy-start.3 = (f32[256,512]{1,0:T(8,128)S(1)}, f32[256,512]{1,0:T(8,128)}, u32[]{:S(2)}) copy-start(f32[256,512]{1,0:T(8,128)} %get-tuple-element.48.beta) | copy-start | bytes 1572868
  43.5 29.9 %copy-start.6 = (bf16[256,512]{1,0:T(8,128)(2,1)S(1)}, bf16[256,512]{1,0:T(8,128)(2,1)}, u32[]{:S(2)}) copy-start(bf16[256,512]{1,0:T(8,128)(2,1)} %get-tuple-element.44.v.v_r) | copy-start | bytes 786436
  73.4 1.8 copy-start
  74.5 0.7 copy-start.10
  75.2 31.3 %copy-start.5 = (f32[16,40,128]{2,1,0:T(8,128)S(1)}, f32[16,40,128]{2,1,0:T(8,128)}, u32[]{:S(2)}) copy-start(f32[16,40,128]{2,1,0:T(8,128)} %copy-done.4) | copy-start | bytes 983044
  83.2 42.5 %collective-permute-start.10 = (bf16[4,128,512]{2,1,0:T(8,128)(2,1)}, bf16[4,128,512]{2,1,0:T(8,128)(2,1)S(1)}, u32[]{:S(2)}, u32[]{:S(2)}) collective-permute-start(bf16[4,128,512]{2,1,0:T(8,128)(2,1)} %get-tuple-element.67), channel_id=1, source_target_pairs={{0,24},{8,0},{16,8},{24,16},{1,25},{9,1},{17,9},{25,17},{2,26},{10... | collective-permute-start | bytes 1572872 | tf_op jit(solution)/shard_map/ppermute | solution.py:352
  84.5 41.2 %collective-permute-start.8 = (bf16[4,128,512]{2,1,0:T(8,128)(2,1)}, bf16[4,128,512]{2,1,0:T(8,128)(2,1)S(1)}, u32[]{:S(2)}, u32[]{:S(2)}) collective-permute-start(bf16[4,128,512]{2,1,0:T(8,128)(2,1)} %get-tuple-element.65), channel_id=1, source_target_pairs={{0,8},{8,16},{16,24},{24,0},{1,9},{9,17},{17,25},{25,1},{2,10},{10... | collective-permute-start | bytes 1572872 | tf_op jit(solution)/shard_map/ppermute | solution.py:352
  84.7 41.1 %collective-permute-start.9 = (bf16[4,128,512]{2,1,0:T(8,128)(2,1)}, bf16[4,128,512]{2,1,0:T(8,128)(2,1)S(1)}, u32[]{:S(2)}, u32[]{:S(2)}) collective-permute-start(bf16[4,128,512]{2,1,0:T(8,128)(2,1)} %get-tuple-element.66), channel_id=1, source_target_pairs={{0,16},{8,24},{16,0},{24,8},{1,17},{9,25},{17,1},{25,9},{2,18},{10... | collective-permute-start | bytes 1572872 | tf_op jit(solution)/shard_map/ppermute | solution.py:352
  106.5 1.0 copy-start.11
  108.2 26.9 %all-to-all-start.3 = ((f32[16,32,128]{2,1,0:T(8,128)}), f32[16,32,128]{2,1,0:T(8,128)S(1)}, u32[]{:S(2)}, u32[]{:S(2)}) async-start(f32[16,32,128]{2,1,0:T(8,128)} %scan_fwd.1), calls=%async_computation.3 | async-start | bytes 524288 | tf_op jit(solution)/shard_map/all_to_all | solution.py:356
  117.3 61.2 %collective-permute-start.5 = (f32[128,2048]{1,0:T(8,128)}, f32[128,2048]{1,0:T(8,128)S(1)}, u32[]{:S(2)}, u32[]{:S(2)}) collective-permute-start(f32[128,2048]{1,0:T(8,128)} %get-tuple-element.53), channel_id=1, source_target_pairs={{0,1},{1,0},{2,3},{3,2},{4,5},{5,4},{6,7},{7,6},{8,9},{9,8},{10,11... | collective-permute-start | bytes 3145736 | tf_op jit(solution)/shard_map/ppermute | solution.py:348
  125.7 1.6 copy-start.19
  125.7 0.8 copy-start.20
  126.6 0.8 copy-start.21
  127.4 14.4 %copy-start.2 = (bf16[256,2048]{1,0:T(8,128)(2,1)S(1)}, bf16[256,2048]{1,0:T(8,128)(2,1)}, u32[]{:S(2)}) copy-start(bf16[256,2048]{1,0:T(8,128)(2,1)} %get-tuple-element.47.tok) | copy-start | bytes 3145732
  130.2 24.3 %collective-permute-start.11 = (bf16[128,512]{1,0:T(8,128)(2,1)}, bf16[128,512]{1,0:T(8,128)(2,1)S(1)}, u32[]{:S(2)}, u32[]{:S(2)}) collective-permute-start(bf16[128,512]{1,0:T(8,128)(2,1)} %get-tuple-element.69), channel_id=1, source_target_pairs={{0,2},{2,4},{4,6},{6,0},{1,3},{3,5},{5,7},{7,1},{8,10},{10,12},{12... | collective-permute-start | bytes 393224 | tf_op jit(solution)/shard_map/ppermute | solution.py:352
  131.5 22.9 %collective-permute-start.12 = (bf16[128,512]{1,0:T(8,128)(2,1)}, bf16[128,512]{1,0:T(8,128)(2,1)S(1)}, u32[]{:S(2)}, u32[]{:S(2)}) collective-permute-start(bf16[128,512]{1,0:T(8,128)(2,1)} %get-tuple-element.70), channel_id=1, source_target_pairs={{0,4},{2,6},{4,0},{6,2},{1,5},{3,7},{5,1},{7,3},{8,12},{10,14},{12... | collective-permute-start | bytes 393224 | tf_op jit(solution)/shard_map/ppermute | solution.py:352
  133.9 20.5 %collective-permute-start.13 = (bf16[128,512]{1,0:T(8,128)(2,1)}, bf16[128,512]{1,0:T(8,128)(2,1)}, u32[]{:S(2)}, u32[]{:S(2)}) collective-permute-start(bf16[128,512]{1,0:T(8,128)(2,1)} %get-tuple-element.71), channel_id=1, source_target_pairs={{0,6},{2,0},{4,2},{6,4},{1,7},{3,1},{5,3},{7,5},{8,14},{10,8},{12,... | collective-permute-start | bytes 393224 | tf_op jit(solution)/shard_map/ppermute | solution.py:352
  135.1 0.7 copy-start.18
  135.8 18.7 %copy-start.14 = (f32[128,512]{1,0:T(8,128)S(1)}, f32[128,512]{1,0:T(8,128)}, u32[]{:S(2)}) copy-start(f32[128,512]{1,0:T(8,128)} %get-tuple-element.68.own) | copy-start | bytes 786436
  139.7 2.1 %collective-permute-start.6 = (f32[256,16]{1,0:T(8,128)}, f32[256,16]{1,0:T(8,128)S(1)}, u32[]{:S(2)}, u32[]{:S(2)}) collective-permute-start(f32[256,16]{1,0:T(8,128)} %get-tuple-element.59.lat_a), channel_id=1, source_target_pairs={{0,1},{1,0},{2,3},{3,2},{4,5},{5,4},{6,7},{7,6},{8,9},{9,8},{10,11... | collective-permute-start | bytes 49160 | tf_op jit(solution)/shard_map/ppermute | solution.py:348
  141.8 0.9 copy-start.15
  142.7 0.8 copy-start.17
  143.4 35.0 %copy-start.12 = (f32[128,2048]{1,0:T(8,128)S(1)}, f32[128,2048]{1,0:T(8,128)}, u32[]{:S(2)}) copy-start(f32[128,2048]{1,0:T(8,128)} %get-tuple-element.52.keep) | copy-start | bytes 3145732
  143.4 35.0 %copy-start.13 = (bf16[16,2048]{1,0:T(8,128)(2,1)S(1)}, bf16[16,2048]{1,0:T(8,128)(2,1)}, u32[]{:S(2)}) copy-start(bf16[16,2048]{1,0:T(8,128)(2,1)} %down.5) | copy-start | bytes 196612
  143.7 34.0 %copy-start.24 = (bf16[128,512]{1,0:T(8,128)(2,1)S(1)}, bf16[128,512]{1,0:T(8,128)(2,1)}, u32[]{:S(2)}) copy-start(bf16[128,512]{1,0:T(8,128)(2,1)} %get-tuple-element.62) | copy-start | bytes 393220
  156.2 12.8 %all-to-all-start.5 = ((bf16[8,32,512]{2,1,0:T(8,128)(2,1)}), bf16[8,32,512]{2,1,0:T(8,128)(2,1)S(1)}, u32[]{:S(2)}, u32[]{:S(2)}) async-start(bf16[8,32,512]{2,1,0:T(8,128)(2,1)} %mid.1), calls=%async_computation.5 | async-start | bytes 524288 | tf_op jit(solution)/shard_map/all_to_all | solution.py:356
  159.6 18.1 %collective-permute-start.7 = (bf16[128,512]{1,0:T(8,128)(2,1)}, bf16[128,512]{1,0:T(8,128)(2,1)S(1)}, u32[]{:S(2)}, u32[]{:S(2)}) collective-permute-start(bf16[128,512]{1,0:T(8,128)(2,1)} %get-tuple-element.63), channel_id=1, source_target_pairs={{0,1},{1,0},{2,3},{3,2},{4,5},{5,4},{6,7},{7,6},{8,9},{9,8},{10,11... | collective-permute-start | bytes 393224 | tf_op jit(solution)/shard_map/ppermute | solution.py:348
  169.0 4.3 %collective-permute-start.14 = (f32[16,512]{1,0:T(8,128)S(1)}, f32[16,512]{1,0:T(8,128)S(1)}, u32[]{:S(2)}, u32[]{:S(2)}) collective-permute-start(f32[16,512]{1,0:T(8,128)S(1)} %get-tuple-element.74), channel_id=1, source_target_pairs={{0,1},{1,0},{2,3},{3,2},{4,5},{5,4},{6,7},{7,6},{8,9},{9,8},{10,11... | collective-permute-start | bytes 98312 | tf_op jit(solution)/shard_map/ppermute | solution.py:348
  174.1 11.2 %all-to-all-start.6 = ((f32[16,8,512]{2,1,0:T(8,128)}), f32[16,8,512]{2,1,0:T(8,128)S(1)}, u32[]{:S(2)}, u32[]{:S(2)}) async-start(f32[16,8,512]{2,1,0:T(8,128)} %get-tuple-element.76), calls=%async_computation.6 | async-start | bytes 524288 | tf_op jit(solution)/shard_map/all_to_all | solution.py:356

commit v3 on v2

v3 whole, which is shorter than its diff:
```python
import jax
import jax.numpy as jnp
from jax import lax
from jax.experimental import pallas as pl
from jax.experimental.pallas import tpu as pltpu
from jax.sharding import Mesh, PartitionSpec as P

HEADS = 8
DK = 128
GROUP = 64
HALF = HEADS // 2
WIDTH = HALF * DK
QUART = WIDTH // 2
TOK = 128
PAIR = 2 * TOK
BLOCKS = PAIR // GROUP
MODEL = 2048
RANK = 16
ZS = 8
PS = 16
ROWS = HALF * DK // PS
F32 = jnp.float32
BF16 = jnp.bfloat16
XY = ("x", "y")
SWAP = ((0, 1), (1, 0))
MB = 1 << 20


def shape(dims, dtype=F32):
    return jax.ShapeDtypeStruct(dims, dtype)


BIG = 56
KEYS = 16


VM = pl.BlockSpec(memory_space=pltpu.VMEM)
ANY = pl.BlockSpec(memory_space=pl.ANY)


def kernel(body, outs, name, limit, scratch=(), specs=None, out_specs=None, alias=None):
    extra = {} if specs is None else {"in_specs": specs, "out_specs": out_specs}
    if alias:
        extra["input_output_aliases"] = alias
    return pl.pallas_call(
        body,
        out_shape=outs,
        name=name,
        scratch_shapes=scratch,
        compiler_params=pltpu.CompilerParams(vmem_limit_bytes=limit * MB),
        **extra,
    )


def split(a):
    hi = a.astype(BF16)
    return hi, (a - hi.astype(F32)).astype(BF16)


def dot(a, b, dims=((1,), (0,))):
    return lax.dot_general(a, b, (dims, ((), ())), preferred_element_type=F32)


NT = ((1,), (1,))
TN = ((0,), (0,))


def dot_hl(a, b, dims=((1,), (0,))):
    hi, lo = split(b)
    return dot(a, hi, dims) + dot(a, lo, dims)


def dot_ff(a, b, dims=((1,), (0,))):
    ah, al = split(a)
    bh, bl = split(b)
    return dot(ah, bh, dims) + dot(ah, bl, dims) + dot(al, bh, dims)


def dot_mask(mask, b):
    hi, lo = split(b)
    rest = (b - hi.astype(F32) - lo.astype(F32)).astype(BF16)
    return dot(mask, hi) + dot(mask, lo) + dot(mask, rest)


def is_first():
    return lax.axis_index("c") == 0


def pick(first, a, b):
    return jnp.where(first, a, b)


def low_mask():
    rows = lax.broadcasted_iota(jnp.int32, (GROUP, GROUP), 0)
    cols = lax.broadcasted_iota(jnp.int32, (GROUP, GROUP), 1)
    return rows >= cols, rows <= cols


def tok_of(n):
    return slice(n * GROUP, (n + 1) * GROUP)


def col_of(h):
    return slice(h * DK, (h + 1) * DK)


def span_of(beta, n):
    return beta[(n + 1) * GROUP - 1 : (n + 1) * GROUP]


def gates_body(own, peer, down, up, bias, q, g, v, q_p, g_p, v_p,
               tok, lat, logit, beta, q_o, g_o, v_o, adds, start):
    first = is_first()
    tok[:TOK] = pick(first, own[...], peer[...])
    tok[TOK:] = pick(first, peer[...], own[...])
    for ref, other, out in ((q, q_p, q_o), (g, g_p, g_o), (v, v_p, v_o)):
        mine = pick(first, ref[:, :WIDTH], ref[:, WIDTH:])
        theirs = pick(first, other[:, :WIDTH], other[:, WIDTH:])
        out[:TOK] = pick(first, mine, theirs)
        out[TOK:] = pick(first, theirs, mine)
    latent = dot(tok[...], down[...], NT).astype(BF16)
    lat[...] = latent
    up_half = pick(first, up[:, :WIDTH], up[:, WIDTH:])
    bias_half = pick(first, bias[:, :WIDTH], bias[:, WIDTH:])
    x = dot(latent, up_half) + bias_half
    logit[...] = x
    gamma = (jnp.minimum(x, 0.0) - jnp.log1p(jnp.exp(-jnp.abs(x)))) * (1.0 / 16.0)
    lower = low_mask()[0].astype(BF16)
    run = [jnp.zeros((DK, DK), F32)] * HALF
    total = jnp.zeros((1, WIDTH), F32)
    for n in reversed(range(BLOCKS)):
        b = dot_mask(lower, gamma[tok_of(n)])
        beta[tok_of(n)] = b
        last = b[GROUP - 1 : GROUP]
        total = total + last
        decay = jnp.exp(last)
        scaled = q_o[tok_of(n)].astype(F32) * jnp.exp(b)
        grad = g_o[tok_of(n)]
        for h in range(HALF):
            part = dot_hl(grad[:, col_of(h)], scaled[:, col_of(h)], TN)
            adds[n, col_of(h)] = part
            run[h] = decay[:, col_of(h)] * run[h] + part
    decay = jnp.exp(total)
    for p in range(PS):
        h, at = p // PER, (p % PER) * ROWS
        start[p, :ROWS] = run[h][at : at + ROWS]
        start[p, ROWS:] = jnp.broadcast_to(decay[:, col_of(h)], (8, DK))


def unpack_w(recv, w):
    for p in range(PS):
        for z in range(ZS):
            w[z * 256 + p * 16 : z * 256 + p * 16 + 16] = recv[p, z * 16 : z * 16 + 16]


def added_states(key, v, beta, n):
    b = beta[tok_of(n)]
    last = b[GROUP - 1 : GROUP]
    tail = key[tok_of(n)].astype(F32) * jnp.exp(last - b)
    vals = v[tok_of(n)]
    return [dot_hl(vals[:, col_of(h)], tail[:, col_of(h)], TN) for h in range(HALF)], jnp.exp(last)


def keys_body(recv, tok, beta, v, start, key_o, send, w):
    unpack_w(recv, w)
    key_o[...] = dot(tok[...], w[...]).astype(BF16)
    run = [jnp.zeros((DK, DK), F32)] * HALF
    for n in range(BLOCKS):
        parts, decay = added_states(key_o, v, beta, n)
        run = [decay[:, col_of(h)] * run[h] + parts[h] for h in range(HALF)]
    for p in range(PS):
        h, at = p // PER, (p % PER) * ROWS
        send[p, : ROWS + 8] = start[p]
        send[p, ROWS + 8 :] = run[h][at : at + ROWS]


def scan_body(recv, send):
    run = jnp.zeros((ROWS, DK), F32)
    for p in reversed(range(PS)):
        send[p, :ROWS] = run
        run = recv[p, ROWS : ROWS + 1] * run + recv[p, :ROWS]
    run = jnp.zeros((ROWS, DK), F32)
    for p in range(PS):
        send[p, ROWS:] = run
        run = recv[p, ROWS : ROWS + 1] * run + recv[p, ROWS + 8 :]


def inner_body(q_r, g_r, v_r, key_r, beta, kd_o, local):
    low, high = low_mask()
    for n in range(BLOCKS):
        b = beta[tok_of(n)]
        grow, shrink = jnp.exp(b), jnp.exp(-b)
        q = q_r[tok_of(n)].astype(F32)
        k = key_r[tok_of(n)].astype(F32)
        q_s, k_s = q * grow, k * shrink
        for h in range(HALF):
            c = col_of(h)
            g, v = g_r[tok_of(n), c], v_r[tok_of(n), c]
            pairs = jnp.where(low, dot(g, v, NT), 0.0)
            pairs_t = jnp.where(high, dot(v, g, NT), 0.0)
            kd = shrink[:, c] * dot_ff(pairs_t, q_s[:, c])
            qd = grow[:, c] * dot_ff(pairs, k_s[:, c])
            kd_o[tok_of(n), c] = kd
            local[tok_of(n), c] = q[:, c] * qd - k[:, c] * kd


def gate_body(recv, adds, key_r, v_r, beta, q_r, g_r, kd_in, local, logit, lat, up,
              kd_o, kd_keep, kd_give, gate_o, gate_keep, gate_give, up_part, lat_part, delta):
    first = is_first()
    high = low_mask()[1].astype(BF16)
    back = [jnp.concatenate([recv[h * PER + i, :ROWS] for i in range(PER)], axis=0)
            for h in range(HALF)]
    run = [jnp.concatenate([recv[h * PER + i, ROWS:] for i in range(PER)], axis=0)
           for h in range(HALF)]
    grads = list(back)
    for n in reversed(range(BLOCKS)):
        b = beta[tok_of(n)]
        last = b[GROUP - 1 : GROUP]
        decay = jnp.exp(last)
        kd = jnp.concatenate(
            [dot_hl(v_r[tok_of(n), col_of(h)], grads[h]) for h in range(HALF)], axis=1
        ) * jnp.exp(last - b)
        kd_o[tok_of(n)] = (kd + kd_in[tok_of(n)]).astype(BF16)
        delta[tok_of(n)] = local[tok_of(n)] - key_r[tok_of(n)].astype(F32) * kd
        grads = [decay[:, col_of(h)] * grads[h] + adds[n, col_of(h)] for h in range(HALF)]
    for n in range(BLOCKS):
        parts, decay = added_states(key_r, v_r, beta, n)
        qd = jnp.concatenate(
            [dot_hl(g_r[tok_of(n), col_of(h)], run[h]) for h in range(HALF)], axis=1
        ) * jnp.exp(beta[tok_of(n)])
        delta[tok_of(n)] += q_r[tok_of(n)].astype(F32) * qd
        run = [decay[:, col_of(h)] * run[h] + parts[h] for h in range(HALF)]
    odd = lax.rem(lax.axis_index("z"), 2) == 1
    kd_lo, kd_hi = kd_o[:, :QUART], kd_o[:, QUART:]
    kd_keep[...] = pick(odd, kd_hi, kd_lo)
    kd_give[...] = pick(odd, kd_lo, kd_hi)
    beyond = jnp.concatenate(
        [jnp.sum(run[h] * back[h], axis=0, keepdims=True) for h in range(HALF)], axis=1
    )
    for n in reversed(range(BLOCKS)):
        suffix = dot_mask(high, delta[tok_of(n)]) + beyond
        beyond = suffix[:1]
        x = logit[tok_of(n)]
        gate_o[tok_of(n)] = (suffix * (1.0 / (1.0 + jnp.exp(x))) * (1.0 / 16.0)).astype(BF16)
    gate = gate_o[...]
    gate_keep[...] = pick(first, gate[:TOK], gate[TOK:])
    gate_give[...] = pick(first, gate[TOK:], gate[:TOK])
    up_half = pick(first, up[:, :WIDTH], up[:, WIDTH:])
    up_part[...] = dot(lat[...], gate, TN)
    lat_part[...] = dot(gate, up_half, NT)


SMALL = 3 * RANK


def down_body(lat_a, lat_b, tok, up_part, lat_o, both):
    first = is_first()
    latent = (lat_a[...] + lat_b[...]).astype(BF16)
    lat_o[...] = pick(first, latent[:TOK], latent[TOK:])
    half = MODEL // 2
    down = dot(latent, pick(first, tok[:, :half], tok[:, half:]), TN)
    both[...] = jnp.concatenate(
        [up_part[...], down[:, :WIDTH], down[:, WIDTH:]], axis=0
    ).astype(BF16)


def weight_body(tok, kd_r, far, far_peer, far_kd, small, send):
    first = is_first()
    kd, kd_far = kd_r[...], far_kd[...]
    kd_a = pick(first, kd_far[:TOK], kd_far[TOK:])
    kd_b = pick(first, kd_far[TOK:], kd_far[:TOK])
    for z in range(ZS):
        cols = slice(z * 256, z * 256 + 256)
        block = dot(tok[:, cols], kd, TN)
        block = block + dot(far[:, cols], kd_a, TN) + dot(far_peer[:, cols], kd_b, TN)
        block = block.astype(BF16)
        at, lane = SMALL + (z % 4) * 16, (z // 4) * QUART
        for p in range(PS):
            send[p, at : at + 16, lane : lane + QUART] = block[p * 16 : p * 16 + 16]
    few = small[...]
    for p in range(PS):
        send[p, :SMALL] = few


def through_body(kd, recv, keep, give, w):
    first = is_first()
    unpack_w(recv, w)
    mine = pick(first, kd[:TOK], kd[TOK:])
    other = pick(first, kd[TOK:], kd[:TOK])
    give[...] = dot(other, w[...], NT)
    keep[...] = dot(mine, w[...], NT)


def input_body(keep, got, lat, down, out):
    out[...] = (keep[...] + got[...] + dot(lat[...], down[...])).astype(BF16)


PER = DK // ROWS


def plane_body(recv, send):
    total = jnp.sum(recv[...].astype(F32), axis=0).astype(BF16)
    for z in range(ZS):
        at, lane = SMALL + (z % 4) * 16, (z // 4) * QUART
        send[z, :SMALL] = total[:SMALL]
        send[z, SMALL:, :QUART] = total[at : at + 16, lane : lane + QUART]
        send[z, SMALL:, QUART:] = jnp.zeros((16, QUART), BF16)


def total_body(recv, keep, give):
    first = is_first()
    small = jnp.sum(recv[:, :SMALL].astype(F32), axis=0)
    parts = [recv[z, SMALL:, :QUART].astype(F32) for z in range(ZS)]
    rows = jnp.concatenate([sum(parts[0::2]), sum(parts[1::2])], axis=1)
    keep[...] = jnp.concatenate([small, pick(first, rows[:8], rows[8:])], axis=0)
    give[...] = jnp.concatenate([small, pick(first, rows[8:], rows[:8])], axis=0)


def out_body(mine, theirs, down_o, up_o, w_o):
    first = is_first()
    halves = (pick(first, mine[...], theirs[...]), pick(first, theirs[...], mine[...]))
    for i, a in enumerate(halves):
        up_o[:, i * WIDTH : (i + 1) * WIDTH] = a[:RANK]
        down_o[:, 2 * i * WIDTH : (2 * i + 1) * WIDTH] = a[RANK : 2 * RANK]
        down_o[:, (2 * i + 1) * WIDTH : (2 * i + 2) * WIDTH] = a[2 * RANK : 3 * RANK]
        w_o[:, i * WIDTH : (i + 1) * WIDTH] = a[3 * RANK :]


def swap(a):
    return lax.ppermute(a, "c", SWAP)


def across(a):
    return lax.ppermute(a, "z", [(i, i ^ 1) for i in range(ZS)])


def a2a(a, axis):
    return lax.all_to_all(a, axis, 0, 0)


def local(inputs, queries, values, out_grad, key_weight, gate_down, gate_up, gate_bias):
    first = is_first()
    own = inputs[0]
    q, g, v = queries[0], out_grad[0], values[0]
    half_bf = shape((PAIR, WIDTH), BF16)
    half_f = shape((PAIR, WIDTH))
    packed = shape((PS, ROWS + 8, DK))

    lo, hi = key_weight[:, :WIDTH], key_weight[:, WIDTH:]
    w_m, w_p = jnp.where(first, lo, hi), swap(jnp.where(first, hi, lo))
    w_chip = jnp.concatenate([jnp.where(first, w_m, w_p), jnp.where(first, w_p, w_m)], axis=0)
    w_z = a2a(jnp.broadcast_to(w_chip[None], (ZS, 16, WIDTH)), "z").reshape(ZS * 16, WIDTH)
    w_all = a2a(jnp.broadcast_to(w_z[None], (PS, ZS * 16, WIDTH)), XY)

    tok, lat, logit, beta, q, g, v, add_g, start = kernel(
        gates_body,
        (shape((PAIR, MODEL), BF16), shape((PAIR, RANK), BF16), half_f, half_f,
         half_bf, half_bf, half_bf, shape((BLOCKS, WIDTH, DK)), packed),
        "gates", BIG,
    )(own, swap(own), gate_down, gate_up, gate_bias[None], q, g, v, swap(q), swap(g), swap(v))
    far = across(own)
    far_peer = swap(far)
    keys, send = kernel(
        keys_body, (half_bf, shape((PS, 2 * ROWS + 8, DK))), "keys", KEYS,
        scratch=[pltpu.VMEM((MODEL, WIDTH), BF16)],
    )(w_all, tok, beta, v, start)
    recv = a2a(send, XY)
    kd_local, local_part = kernel(inner_body, (half_f, half_f), "inner", BIG)(q, g, v, keys, beta)
    recv = a2a(kernel(scan_body, shape((PS, 2 * ROWS, DK)), "scan", 8)(recv), XY)
    quarter = shape((PAIR, QUART), BF16)
    kd, kd_keep, kd_give, gate, gate_m, gate_x, up_part, lat_part = kernel(
        gate_body,
        (half_bf, quarter, quarter, half_bf, shape((TOK, WIDTH), BF16),
         shape((TOK, WIDTH), BF16), shape((RANK, WIDTH)), shape((PAIR, RANK))),
        "gate", BIG, scratch=[pltpu.VMEM((PAIR, WIDTH), F32)],
    )(recv, add_g, keys, v, beta, q, g, kd_local, local_part, logit, lat, gate_up)
    far_kd = across(kd_give)
    lat_own, small = kernel(
        down_body, (shape((TOK, RANK), BF16), shape((SMALL, WIDTH), BF16)), "down", 8
    )(lat_part, swap(lat_part), tok, up_part)
    send = kernel(
        weight_body, shape((PS, SMALL + ZS * 8, WIDTH), BF16), "weights", BIG
    )(tok, kd_keep, far, far_peer, far_kd, small)
    send = kernel(plane_body, shape((ZS, SMALL + 16, WIDTH), BF16), "plane", 8)(a2a(send, XY))
    end = shape((SMALL + 8, WIDTH))
    keep, give = kernel(total_body, (end, end), "total", 8)(a2a(send, "z"))
    down_grad, up_grad, key_weight_grad = kernel(
        out_body,
        (shape((RANK, MODEL)), shape((RANK, 2 * WIDTH)), shape((8, 2 * WIDTH))), "grads", 8,
    )(keep, swap(give))

    gate_p = swap(gate_x)
    gate_grad = jnp.concatenate(
        [jnp.where(first, gate_m, gate_p), jnp.where(first, gate_p, gate_m)], axis=1
    )
    mine, other = kernel(
        through_body, (shape((TOK, MODEL)), shape((TOK, MODEL))), "through", BIG,
        scratch=[pltpu.VMEM((MODEL, WIDTH), BF16)],
    )(kd, w_all)
    input_grad = kernel(input_body, shape((TOK, MODEL), BF16), "input", 16)(
        mine, swap(other), lat_own, gate_down
    )
    return (input_grad[None], gate_grad[None], key_weight_grad, down_grad, up_grad)


def solution(mesh):
    grid = Mesh(mesh.devices.reshape(8, 4, 4, 2), ("z", "x", "y", "c"))
    seq = ("x", "y", "c")
    tok = P("z", seq, None)
    row = P(("z",) + seq, None)
    return jax.shard_map(
        local,
        mesh=grid,
        in_specs=(tok, tok, tok, tok, row, P(), P(), P()),
        out_specs=(tok, tok, row, P(), P()),
        check_vma=False,
    )
```

time: 187 us -> 168 us (0.90)
  blocking collectives: 61.2 us -> 14.2 us
  waiting for transfers between devices: 30.2 us -> 60.1 us
  starting transfers between devices: 50.8 us -> 47.3 us
    all_to_all x3 -> x1, blocking collectives: 61.2 us -> 14.2 us  [a2a(): return lax.all_to_all(a, axis, 0, 0)]
    all_to_all x4 -> x5, waiting for transfers between devices: 21 us -> 55.1 us  [a2a(): return lax.all_to_all(a, axis, 0, 0)]
    ppermute x9 -> x2, starting transfers between devices: 14.1 us -> 0.63 us  [across(): return lax.ppermute(a, 'z', [(i, i ^ 1) for i in range(ZS)])]
    all_to_all x4 -> x5, starting transfers between devices: 18.6 us -> 24.2 us  [a2a(): return lax.all_to_all(a, axis, 0, 0)]
    ppermute x9 -> x2, waiting for transfers between devices: 5.39 us -> 0.01 us  [across(): return lax.ppermute(a, 'z', [(i, i ^ 1) for i in range(ZS)])]
    ppermute x6 -> x10, starting transfers between devices: 18 us -> 22.5 us  [swap(): return lax.ppermute(a, 'c', SWAP)]
    pallas_call x12 -> x9, Pallas kernels: 20.2 us -> 18.4 us  [the longest x1 5.09 us: local(): kernel(inner_body, (half_f, half_f), 'inner', BIG)(q, g, v, keys, beta)]
    ppermute x6 -> x10, waiting for transfers between devices: 3.79 us -> 5.05 us  [swap(): return lax.ppermute(a, 'c', SWAP)]
  transfers between devices with their start and end apart: 19 -> 17, of which waited for: 8 -> 10; matrix products, arithmetic and copies ran while one was open for 0% -> 0% of each run, Pallas kernels for 8% -> 14%
where the time goes in v3:
time: 168 us; the launch traced here: 167 us
  waiting for transfers between devices  60.1 us (36%)
  starting transfers between devices  47.3 us (28%)
  Pallas kernels  30 us (18%)
  blocking collectives  14.2 us (8%)
  local copies, waits for them, and re-layouts  12 us (7%)
  other arithmetic  2.2 us (1%)
    all_to_all x5, waiting for transfers between devices, a2a(): return lax.all_to_all(a, axis, 0, 0)  55.1 us
    all_to_all x5, starting transfers between devices, a2a(): return lax.all_to_all(a, axis, 0, 0)  24.2 us
    ppermute x10, starting transfers between devices, swap(): return lax.ppermute(a, 'c', SWAP)  22.5 us
    all_to_all x1, blocking collectives, a2a(): return lax.all_to_all(a, axis, 0, 0)  14.2 us
    unnamed x54, local copies, waits for them, and re-layouts  10.5 us
    pallas_call x1, Pallas kernels, local(): kernel(gates_body, (shape((PAIR, MODEL), BF16), shape((PAIR, RANK), BF16)...  5.19 us
    pallas_call x1, Pallas kernels, local(): kernel(inner_body, (half_f, half_f), 'inner', BIG)(q, g, v, keys, beta)  5.09 us
    ppermute x10, waiting for transfers between devices, swap(): return lax.ppermute(a, 'c', SWAP)  5.05 us
  transfers between devices with their start and end apart: 17, of which 10 were waited for; matrix products, arithmetic and copies ran while one was open for 0% of the time, Pallas kernels for 14%

profile of v3, /device:TPU:1, one launch (start us, length us, event | category | flops | bytes accessed | tf_op | source)
XLA Modules:
  0.0 166.6 jit_solution(14771801951231258311)
XLA Ops:
  0.6 0.7 broadcast_select_fusion.4
  1.4 3.2 %collective-permute-start = (bf16[8,512]{1,0:T(8,128)(2,1)S(1)}, bf16[8,512]{1,0:T(8,128)(2,1)S(1)}, u32[]{:S(2)}, u32[]{:S(2)}) collective-permute-start(bf16[8,512]{1,0:T(8,128)(2,1)S(1)} %broadcast_select_fusion.4), channel_id=1, source_target_pairs={{0,1},{1,0},{2,3},{3,2},{4,5},{5,4},{6,7},{7,6},{8,9},{9,8},{10,11... | collective-permute-start | bytes 24584 | tf_op jit(solution)/shard_map/ppermute | solution.py:330
  4.6 0.8 collective-permute-done
  5.4 0.7 broadcast_select_fusion.3
  6.2 14.2 %all_to_all.30 = bf16[8,16,512]{2,1,0:T(8,128)(2,1)S(1)} all-to-all(bf16[8,16,512]{2,1,0:T(8,128)(2,1)S(1)} %broadcast_in_dim.22), channel_id=1, replica_groups=mesh['z'=8,'x'=4,'y'=4,'c'=2] {'z'}, dimensions={0} | all-to-all | bytes 262144 | tf_op jit(solution)/shard_map/all_to_all | solution.py:338
  20.3 1.5 broadcast_in_dim.24
  21.9 6.9 %all-to-all-start.1 = ((bf16[16,128,512]{2,1,0:T(8,128)(2,1)}), bf16[16,128,512]{2,1,0:T(8,128)(2,1)S(1)}, u32[]{:S(2)}, u32[]{:S(2)}) async-start(bf16[16,128,512]{2,1,0:T(8,128)(2,1)} %broadcast_in_dim.24), calls=%async_computation.1 | async-start | bytes 4194304 | tf_op jit(solution)/shard_map/all_to_all | solution.py:338
  28.8 2.5 %collective-permute-start.1 = (bf16[128,2048]{1,0:T(8,128)(2,1)S(1)}, bf16[128,2048]{1,0:T(8,128)(2,1)S(1)}, u32[]{:S(2)}, u32[]{:S(2)}) collective-permute-start(bf16[128,2048]{1,0:T(8,128)(2,1)S(1)} %bitcast.11), channel_id=1, source_target_pairs={{0,1},{1,0},{2,3},{3,2},{4,5},{5,4},{6,7},{7,6},{8,9},{9,8},{10,11... | collective-permute-start | bytes 1572872 | tf_op jit(solution)/shard_map/ppermute | solution.py:330
  31.3 0.1 collective-permute-start.2
  31.4 0.4 collective-permute-start.3
  31.8 0.1 collective-permute-start.4
  31.9 1.3 collective-permute-done.2.q_p
  33.2 0.4 collective-permute-done.3.g_p
  33.6 0.4 collective-permute-done.4.v_p
  34.0 0.3 copy-done.22
  34.3 0.4 copy-done.23
  34.6 0.2 copy-done.15
  34.8 5.2 %gates.1 = (bf16[256,2048]{1,0:T(8,128)(2,1)}, bf16[256,16]{1,0:T(8,128)(2,1)}, f32[256,512]{1,0:T(8,128)}, f32[256,512]{1,0:T(8,128)}, bf16[256,512]{1,0:T(8,12...) custom-call(bf16[128,2048]{1,0:T(8,128)(2,1)} %bitcast.10, ...), custom_call_target="tpu_custom_call" | custom-call | tf_op jit(solution)/shard_map/gates/pallas_call | solution.py:355
  40.0 14.2 %all-to-all-done.1.recv = bf16[16,128,512]{2,1,0:T(8,128)(2,1)S(1)} async-done(((bf16[16,128,512]{2,1,0:T(8,128)(2,1)}), bf16[16,128,512]{2,1,0:T(8,128)(2,1)S(1)}, u32[]{:S(2)}, u32[]{:S(2)}) %all-to-all-start.1) | async-done | bytes 2097184 | tf_op jit(solution)/shard_map/all_to_all | solution.py:338
  54.2 2.0 %copy-done.1 = bf16[256,2048]{1,0:T(8,128)(2,1)S(1)} copy-done((bf16[256,2048]{1,0:T(8,128)(2,1)S(1)}, bf16[256,2048]{1,0:T(8,128)(2,1)}, u32[]{:S(2)}) %copy-start.1) | copy-done | bytes 1048600
  56.2 1.0 copy-done.3
  57.2 0.9 copy-done.4
  58.2 1.0 copy-done.7
  59.2 1.9 %keys.1 = (bf16[256,512]{1,0:T(8,128)(2,1)S(1)}, f32[16,72,128]{2,1,0:T(8,128)}) custom-call(bf16[16,128,512]{2,1,0:T(8,128)(2,1)S(1)} %all-to-all-done.1.recv, bf16[256,2048]{1,0:T(8,128)(2,1)S(1)} %copy-done.1, f32[256,512]{1,0:T(8,128)S(1)} %copy-done.3, bf16[256,512]{1,0:T(8,128)(2,1)S(1)} %copy-done.4, f32[16,40,128]{2,1,0:T(8,128)S(1)} %copy-done.7), custom_call_target="tpu_custom_call" | custom-call | tf_op jit(solution)/shard_map/keys/pallas_call | solution.py:363
  61.1 0.7 copy-done.5
  61.8 5.9 %all-to-all-start.2 = ((f32[16,72,128]{2,1,0:T(8,128)}), f32[16,72,128]{2,1,0:T(8,128)S(1)}, u32[]{:S(2)}, u32[]{:S(2)}) async-start(f32[16,72,128]{2,1,0:T(8,128)} %get-tuple-element.38), calls=%async_computation.2 | async-start | bytes 1179648 | tf_op jit(solution)/shard_map/all_to_all | solution.py:338
  67.7 0.3 collective-permute-start.8
  68.0 9.1 %all-to-all-done.2.recv = f32[16,72,128]{2,1,0:T(8,128)S(1)} async-done(((f32[16,72,128]{2,1,0:T(8,128)}), f32[16,72,128]{2,1,0:T(8,128)S(1)}, u32[]{:S(2)}, u32[]{:S(2)}) %all-to-all-start.2) | async-done | bytes 589856 | tf_op jit(solution)/shard_map/all_to_all | solution.py:338
  77.0 0.8 scan.1
  77.9 3.6 %all-to-all-start.3 = ((f32[16,64,128]{2,1,0:T(8,128)}), f32[16,64,128]{2,1,0:T(8,128)S(1)}, u32[]{:S(2)}, u32[]{:S(2)}) async-start(f32[16,64,128]{2,1,0:T(8,128)} %scan.1), calls=%async_computation.3 | async-start | bytes 1048576 | tf_op jit(solution)/shard_map/all_to_all | solution.py:338
  81.5 0.0 collective-permute-done.8.far
  81.5 4.3 %collective-permute-start.9 = (bf16[128,2048]{1,0:T(8,128)(2,1)S(1)}, bf16[128,2048]{1,0:T(8,128)(2,1)S(1)}, u32[]{:S(2)}, u32[]{:S(2)}) collective-permute-start(bf16[128,2048]{1,0:T(8,128)(2,1)S(1)} %collective-permute-done.8.far), channel_id=1, source_target_pairs={{0,1},{1,0},{2,3},{3,2},{4,5},{5,4},{6,7},{7,6},{8,9},{9,8},{10,11... | collective-permute-start | bytes 1572872 | tf_op jit(solution)/shard_map/ppermute | solution.py:330
  85.8 5.1 %inner.1 = (f32[256,512]{1,0:T(8,128)}, f32[256,512]{1,0:T(8,128)}) custom-call(bf16[256,512]{1,0:T(8,128)(2,1)} %get-tuple-element.41.q_r, bf16[256,512]{1,0:T(8,128)(2,1)} %get-tuple-element.42.g_r, bf16[256,512]{1,0:T(8,128)(2,1)} %get-tuple-element.36.v.v_r, bf16[256,512]{1,0:T(8,128)(2,1)} %copy-done.5, f32[256,512]{1,0:T(8,128)} %get-tuple-element.35.beta), custom_call_target="tpu_custom_call" | custom-call | tf_op jit(solution)/shard_map/inner/pallas_call | solution.py:368
  90.9 0.8 copy-done.12
  91.7 4.7 %gate.1 = (bf16[256,512]{1,0:T(8,128)(2,1)}, bf16[256,256]{1,0:T(8,128)(2,1)}, bf16[256,256]{1,0:T(8,128)(2,1)}, bf16[256,512]{1,0:T(8,128)(2,1)}, bf16[128,512]...) custom-call(f32[16,64,128]{2,1,0:T(8,128)} %copy-done.12, ...), custom_call_target="tpu_custom_call" | custom-call | tf_op jit(solution)/shard_map/gate/pallas_call | solution.py:371
  96.4 0.3 collective-permute-start.10
  96.7 5.1 %collective-permute-start.6 = (f32[256,16]{1,0:T(8,128)}, f32[256,16]{1,0:T(8,128)S(1)}, u32[]{:S(2)}, u32[]{:S(2)}) collective-permute-start(f32[256,16]{1,0:T(8,128)} %get-tuple-element.50.lat_a), channel_id=1, source_target_pairs={{0,1},{1,0},{2,3},{3,2},{4,5},{5,4},{6,7},{7,6},{8,9},{9,8},{10,11... | collective-permute-start | bytes 49160 | tf_op jit(solution)/shard_map/ppermute | solution.py:330
  101.8 1.2 collective-permute-done.6.lat_b
  103.0 0.9 copy-done.9
  104.0 0.8 copy-done.11
  104.7 0.2 down.4
  104.9 0.6 copy-done.10
  105.5 0.0 collective-permute-done.9.far_peer
  105.5 0.0 collective-permute-done.10.far_kd
  105.6 0.0 copy-start.25
  105.6 0.8 copy-done.17
  106.3 0.0 copy-done.25
  106.4 3.9 %weights.1 = bf16[16,112,512]{2,1,0:T(8,128)(2,1)} custom-call(bf16[256,2048]{1,0:T(8,128)(2,1)} %get-tuple-element.34.tok, bf16[256,256]{1,0:T(8,128)(2,1)} %get-tuple-element.55.kd_r, bf16[128,2048]{1,0:T(8,128)(2,1)} %copy-done.16, bf16[128,2048]{1,0:T(8,128)(2,1)} %copy-done.17, bf16[256,256]{1,0:T(8,128)(2,1)} %copy-done.25, bf16[48,512]{1,0:T(8,128)(2,1)} %copy-done.10), custom_call_target="tpu_custom_call" | custom-call | tf_op jit(solution)/shard_map/weights/pallas_call | solution.py:381
  110.2 3.7 %all-to-all-start.4 = ((bf16[16,112,512]{2,1,0:T(8,128)(2,1)}), bf16[16,112,512]{2,1,0:T(8,128)(2,1)S(1)}, u32[]{:S(2)}, u32[]{:S(2)}) async-start(bf16[16,112,512]{2,1,0:T(8,128)(2,1)} %weights.1), calls=%async_computation.4 | async-start | bytes 3670016 | tf_op jit(solution)/shard_map/all_to_all | solution.py:338
  114.0 4.2 %through.1 = (f32[128,2048]{1,0:T(8,128)}, f32[128,2048]{1,0:T(8,128)}) custom-call(bf16[256,512]{1,0:T(8,128)(2,1)} %get-tuple-element.47.kd, bf16[16,128,512]{2,1,0:T(8,128)(2,1)} %copy-done), custom_call_target="tpu_custom_call" | custom-call | tf_op jit(solution)/shard_map/through/pallas_call | solution.py:396
  118.1 0.0 copy-start.8
  118.2 0.9 collective-permute-start.5
  119.1 20.1 %all-to-all-done.4.recv = bf16[16,112,512]{2,1,0:T(8,128)(2,1)S(1)} async-done(((bf16[16,112,512]{2,1,0:T(8,128)(2,1)}), bf16[16,112,512]{2,1,0:T(8,128)(2,1)S(1)}, u32[]{:S(2)}, u32[]{:S(2)}) %all-to-all-start.4) | async-done | bytes 1835040 | tf_op jit(solution)/shard_map/all_to_all | solution.py:338
  139.1 1.0 plane.1
  140.2 4.1 %all-to-all-start.5 = ((bf16[8,64,512]{2,1,0:T(8,128)(2,1)}), bf16[8,64,512]{2,1,0:T(8,128)(2,1)S(1)}, u32[]{:S(2)}, u32[]{:S(2)}) async-start(bf16[8,64,512]{2,1,0:T(8,128)(2,1)} %plane.1), calls=%async_computation.5 | async-start | bytes 1048576 | tf_op jit(solution)/shard_map/all_to_all | solution.py:338
  144.3 2.5 %collective-permute-start.7 = (bf16[128,512]{1,0:T(8,128)(2,1)S(1)}, bf16[128,512]{1,0:T(8,128)(2,1)S(1)}, u32[]{:S(2)}, u32[]{:S(2)}) collective-permute-start(bf16[128,512]{1,0:T(8,128)(2,1)S(1)} %copy-done.26), channel_id=1, source_target_pairs={{0,1},{1,0},{2,3},{3,2},{4,5},{5,4},{6,7},{7,6},{8,9},{9,8},{10,11... | collective-permute-start | bytes 393224 | tf_op jit(solution)/shard_map/ppermute | solution.py:330
  146.7 1.0 collective-permute-done.7
  147.7 11.7 %all-to-all-done.5.recv = bf16[8,64,512]{2,1,0:T(8,128)(2,1)S(1)} async-done(((bf16[8,64,512]{2,1,0:T(8,128)(2,1)}), bf16[8,64,512]{2,1,0:T(8,128)(2,1)S(1)}, u32[]{:S(2)}, u32[]{:S(2)}) %all-to-all-start.5) | async-done | bytes 524320 | tf_op jit(solution)/shard_map/all_to_all | solution.py:338
  159.5 0.1 total.1
  159.5 3.3 %collective-permute-start.11 = (f32[56,512]{1,0:T(8,128)S(1)}, f32[56,512]{1,0:T(8,128)S(1)}, u32[]{:S(2)}, u32[]{:S(2)}) collective-permute-start(f32[56,512]{1,0:T(8,128)S(1)} %get-tuple-element.59), channel_id=1, source_target_pairs={{0,1},{1,0},{2,3},{3,2},{4,5},{5,4},{6,7},{7,6},{8,9},{9,8},{10,11... | collective-permute-start | bytes 344072 | tf_op jit(solution)/shard_map/ppermute | solution.py:330
  162.9 0.7 maximum_bitcast_fusion
  163.6 2.3 %input.1 = bf16[128,2048]{1,0:T(8,128)(2,1)} custom-call(f32[128,2048]{1,0:T(8,128)S(1)} %copy-done.6, f32[128,2048]{1,0:T(8,128)} %collective-permute-done.5.got, bf16[128,16]{1,0:T(8,128)(2,1)S(1)} %get-tuple-element.52.lat, bf16[16,2048]{1,0:T(8,128)(2,1)S(1)} %copy-done.8), custom_call_target="tpu_custom_call" | custom-call | tf_op jit(solution)/shard_map/input/pallas_call | solution.py:400
  165.9 0.0 collective-permute-done.11.theirs
  165.9 0.7 grads.1
  (44 shorter events, 0.1 us)
Async XLA Ops:
  1.4 4.1 %collective-permute-start = (bf16[8,512]{1,0:T(8,128)(2,1)S(1)}, bf16[8,512]{1,0:T(8,128)(2,1)S(1)}, u32[]{:S(2)}, u32[]{:S(2)}) collective-permute-start(bf16[8,512]{1,0:T(8,128)(2,1)S(1)} %broadcast_select_fusion.4), channel_id=1, source_target_pairs={{0,1},{1,0},{2,3},{3,2},{4,5},{5,4},{6,7},{7,6},{8,9},{9,8},{10,11... | collective-permute-start | bytes 24584 | tf_op jit(solution)/shard_map/ppermute | solution.py:330
  21.9 6.9 %copy-start.13 = (bf16[1,128,2048]{2,1,0:T(8,128)(2,1)S(1)}, bf16[1,128,2048]{2,1,0:T(8,128)(2,1)}, u32[]{:S(2)}) copy-start(bf16[1,128,2048]{2,1,0:T(8,128)(2,1)} %param.8) | copy-start | bytes 1572868
  21.9 9.4 %copy-start.18 = (bf16[1,128,1024]{2,1,0:T(8,128)(2,1)S(1)}, bf16[1,128,1024]{2,1,0:T(8,128)(2,1)}, u32[]{:S(2)}) copy-start(bf16[1,128,1024]{2,1,0:T(8,128)(2,1)} %param.9) | copy-start | bytes 786436
  21.9 9.5 %copy-start.19 = (bf16[1,128,1024]{2,1,0:T(8,128)(2,1)S(1)}, bf16[1,128,1024]{2,1,0:T(8,128)(2,1)}, u32[]{:S(2)}) copy-start(bf16[1,128,1024]{2,1,0:T(8,128)(2,1)} %param.11) | copy-start | bytes 786436
  21.9 9.9 %copy-start.20 = (bf16[1,128,1024]{2,1,0:T(8,128)(2,1)S(1)}, bf16[1,128,1024]{2,1,0:T(8,128)(2,1)}, u32[]{:S(2)}) copy-start(bf16[1,128,1024]{2,1,0:T(8,128)(2,1)} %param.10) | copy-start | bytes 786436
  21.9 32.3 %all-to-all-start.1 = ((bf16[16,128,512]{2,1,0:T(8,128)(2,1)}), bf16[16,128,512]{2,1,0:T(8,128)(2,1)S(1)}, u32[]{:S(2)}, u32[]{:S(2)}) async-start(bf16[16,128,512]{2,1,0:T(8,128)(2,1)} %broadcast_in_dim.24), calls=%async_computation.1 | async-start | bytes 4194304 | tf_op jit(solution)/shard_map/all_to_all | solution.py:338
  28.8 5.1 %collective-permute-start.1 = (bf16[128,2048]{1,0:T(8,128)(2,1)S(1)}, bf16[128,2048]{1,0:T(8,128)(2,1)S(1)}, u32[]{:S(2)}, u32[]{:S(2)}) collective-permute-start(bf16[128,2048]{1,0:T(8,128)(2,1)S(1)} %bitcast.11), channel_id=1, source_target_pairs={{0,1},{1,0},{2,3},{3,2},{4,5},{5,4},{6,7},{7,6},{8,9},{9,8},{10,11... | collective-permute-start | bytes 1572872 | tf_op jit(solution)/shard_map/ppermute | solution.py:330
  31.3 1.9 %collective-permute-start.2 = (bf16[128,1024]{1,0:T(8,128)(2,1)S(1)}, bf16[128,1024]{1,0:T(8,128)(2,1)S(1)}, u32[]{:S(2)}, u32[]{:S(2)}) collective-permute-start(bf16[128,1024]{1,0:T(8,128)(2,1)S(1)} %bitcast.15), channel_id=1, source_target_pairs={{0,1},{1,0},{2,3},{3,2},{4,5},{5,4},{6,7},{7,6},{8,9},{9,8},{10,11... | collective-permute-start | bytes 786440 | tf_op jit(solution)/shard_map/ppermute | solution.py:330
  31.4 2.2 %collective-permute-start.3 = (bf16[128,1024]{1,0:T(8,128)(2,1)S(1)}, bf16[128,1024]{1,0:T(8,128)(2,1)S(1)}, u32[]{:S(2)}, u32[]{:S(2)}) collective-permute-start(bf16[128,1024]{1,0:T(8,128)(2,1)S(1)} %bitcast.17), channel_id=1, source_target_pairs={{0,1},{1,0},{2,3},{3,2},{4,5},{5,4},{6,7},{7,6},{8,9},{9,8},{10,11... | collective-permute-start | bytes 786440 | tf_op jit(solution)/shard_map/ppermute | solution.py:330
  31.8 2.1 %collective-permute-start.4 = (bf16[128,1024]{1,0:T(8,128)(2,1)S(1)}, bf16[128,1024]{1,0:T(8,128)(2,1)S(1)}, u32[]{:S(2)}, u32[]{:S(2)}) collective-permute-start(bf16[128,1024]{1,0:T(8,128)(2,1)S(1)} %bitcast.19), channel_id=1, source_target_pairs={{0,1},{1,0},{2,3},{3,2},{4,5},{5,4},{6,7},{7,6},{8,9},{9,8},{10,11... | collective-permute-start | bytes 786440 | tf_op jit(solution)/shard_map/ppermute | solution.py:330
  33.2 0.8 copy-start.21
  33.6 0.7 copy-start.22
  33.9 0.7 copy-start.23
  33.9 0.9 copy-start.15
  54.2 6.9 %copy-start = (bf16[16,128,512]{2,1,0:T(8,128)(2,1)}, bf16[16,128,512]{2,1,0:T(8,128)(2,1)S(1)}, u32[]{:S(2)}) copy-start(bf16[16,128,512]{2,1,0:T(8,128)(2,1)S(1)} %all-to-all-done.1.recv) | copy-start | bytes 6291460
  54.2 2.0 %copy-start.1 = (bf16[256,2048]{1,0:T(8,128)(2,1)S(1)}, bf16[256,2048]{1,0:T(8,128)(2,1)}, u32[]{:S(2)}) copy-start(bf16[256,2048]{1,0:T(8,128)(2,1)} %get-tuple-element.34.tok) | copy-start | bytes 3145732
  56.2 1.0 copy-start.3
  57.2 0.9 copy-start.4
  58.2 1.0 copy-start.7
  59.2 8.5 %copy-start.14 = (bf16[1,128,2048]{2,1,0:T(8,128)(2,1)S(1)}, bf16[1,128,2048]{2,1,0:T(8,128)(2,1)}, u32[]{:S(2)}) copy-start(bf16[1,128,2048]{2,1,0:T(8,128)(2,1)} %param.8) | copy-start | bytes 1572868
  61.1 0.7 copy-start.5
  61.8 15.3 %all-to-all-start.2 = ((f32[16,72,128]{2,1,0:T(8,128)}), f32[16,72,128]{2,1,0:T(8,128)S(1)}, u32[]{:S(2)}, u32[]{:S(2)}) async-start(f32[16,72,128]{2,1,0:T(8,128)} %get-tuple-element.38), calls=%async_computation.2 | async-start | bytes 1179648 | tf_op jit(solution)/shard_map/all_to_all | solution.py:338
  67.7 13.8 %collective-permute-start.8 = (bf16[128,2048]{1,0:T(8,128)(2,1)S(1)}, bf16[128,2048]{1,0:T(8,128)(2,1)S(1)}, u32[]{:S(2)}, u32[]{:S(2)}) collective-permute-start(bf16[128,2048]{1,0:T(8,128)(2,1)S(1)} %bitcast.12), channel_id=1, source_target_pairs={{0,32},{32,0},{64,96},{96,64},{128,160},{160,128},{192,224},{224,1... | collective-permute-start | bytes 1572872 | tf_op jit(solution)/shard_map/ppermute | solution.py:334
  77.9 13.0 %all-to-all-start.3 = ((f32[16,64,128]{2,1,0:T(8,128)}), f32[16,64,128]{2,1,0:T(8,128)S(1)}, u32[]{:S(2)}, u32[]{:S(2)}) async-start(f32[16,64,128]{2,1,0:T(8,128)} %scan.1), calls=%async_computation.3 | async-start | bytes 1048576 | tf_op jit(solution)/shard_map/all_to_all | solution.py:338
  81.5 14.9 %copy-start.16 = (bf16[128,2048]{1,0:T(8,128)(2,1)}, bf16[128,2048]{1,0:T(8,128)(2,1)S(1)}, u32[]{:S(2)}) copy-start(bf16[128,2048]{1,0:T(8,128)(2,1)S(1)} %collective-permute-done.8.far) | copy-start | bytes 1572868
  81.5 24.1 %collective-permute-start.9 = (bf16[128,2048]{1,0:T(8,128)(2,1)S(1)}, bf16[128,2048]{1,0:T(8,128)(2,1)S(1)}, u32[]{:S(2)}, u32[]{:S(2)}) collective-permute-start(bf16[128,2048]{1,0:T(8,128)(2,1)S(1)} %collective-permute-done.8.far), channel_id=1, source_target_pairs={{0,1},{1,0},{2,3},{3,2},{4,5},{5,4},{6,7},{7,6},{8,9},{9,8},{10,11... | collective-permute-start | bytes 1572872 | tf_op jit(solution)/shard_map/ppermute | solution.py:330
  90.9 0.8 copy-start.12
  91.7 11.3 %copy-start.2 = (bf16[256,2048]{1,0:T(8,128)(2,1)S(1)}, bf16[256,2048]{1,0:T(8,128)(2,1)}, u32[]{:S(2)}) copy-start(bf16[256,2048]{1,0:T(8,128)(2,1)} %get-tuple-element.34.tok) | copy-start | bytes 3145732
  96.4 9.2 %collective-permute-start.10 = (bf16[256,256]{1,0:T(8,128)(2,1)}, bf16[256,256]{1,0:T(8,128)(2,1)S(1)}, u32[]{:S(2)}, u32[]{:S(2)}) collective-permute-start(bf16[256,256]{1,0:T(8,128)(2,1)} %get-tuple-element.56), channel_id=1, source_target_pairs={{0,32},{32,0},{64,96},{96,64},{128,160},{160,128},{192,224},{224,1... | collective-permute-start | bytes 393224 | tf_op jit(solution)/shard_map/ppermute | solution.py:334
  96.7 6.3 %collective-permute-start.6 = (f32[256,16]{1,0:T(8,128)}, f32[256,16]{1,0:T(8,128)S(1)}, u32[]{:S(2)}, u32[]{:S(2)}) collective-permute-start(f32[256,16]{1,0:T(8,128)} %get-tuple-element.50.lat_a), channel_id=1, source_target_pairs={{0,1},{1,0},{2,3},{3,2},{4,5},{5,4},{6,7},{7,6},{8,9},{9,8},{10,11... | collective-permute-start | bytes 49160 | tf_op jit(solution)/shard_map/ppermute | solution.py:330
  103.0 0.9 copy-start.9
  104.0 0.8 copy-start.11
  104.9 0.6 copy-start.10
  105.5 0.8 copy-start.17
  105.6 0.8 copy-start.25
  110.2 28.9 %all-to-all-start.4 = ((bf16[16,112,512]{2,1,0:T(8,128)(2,1)}), bf16[16,112,512]{2,1,0:T(8,128)(2,1)S(1)}, u32[]{:S(2)}, u32[]{:S(2)}) async-start(bf16[16,112,512]{2,1,0:T(8,128)(2,1)} %weights.1), calls=%async_computation.4 | async-start | bytes 3670016 | tf_op jit(solution)/shard_map/all_to_all | solution.py:338
  118.1 26.1 %copy-start.26 = (bf16[128,512]{1,0:T(8,128)(2,1)S(1)}, bf16[128,512]{1,0:T(8,128)(2,1)}, u32[]{:S(2)}) copy-start(bf16[128,512]{1,0:T(8,128)(2,1)} %get-tuple-element.54) | copy-start | bytes 393220
  118.1 29.6 %copy-start.24 = (bf16[128,512]{1,0:T(8,128)(2,1)S(1)}, bf16[128,512]{1,0:T(8,128)(2,1)}, u32[]{:S(2)}) copy-start(bf16[128,512]{1,0:T(8,128)(2,1)} %get-tuple-element.53) | copy-start | bytes 393220
  118.1 45.5 %copy-start.6 = (f32[128,2048]{1,0:T(8,128)S(1)}, f32[128,2048]{1,0:T(8,128)}, u32[]{:S(2)}) copy-start(f32[128,2048]{1,0:T(8,128)} %get-tuple-element.48.keep) | copy-start | bytes 3145732
  118.1 45.5 %copy-start.8 = (bf16[16,2048]{1,0:T(8,128)(2,1)S(1)}, bf16[16,2048]{1,0:T(8,128)(2,1)}, u32[]{:S(2)}) copy-start(bf16[16,2048]{1,0:T(8,128)(2,1)} %down.5) | copy-start | bytes 196612
  118.2 45.4 %collective-permute-start.5 = (f32[128,2048]{1,0:T(8,128)}, f32[128,2048]{1,0:T(8,128)}, u32[]{:S(2)}, u32[]{:S(2)}) collective-permute-start(f32[128,2048]{1,0:T(8,128)} %get-tuple-element.49), channel_id=1, source_target_pairs={{0,1},{1,0},{2,3},{3,2},{4,5},{5,4},{6,7},{7,6},{8,9},{9,8},{10,11... | collective-permute-start | bytes 3145736 | tf_op jit(solution)/shard_map/ppermute | solution.py:330
  140.2 19.3 %all-to-all-start.5 = ((bf16[8,64,512]{2,1,0:T(8,128)(2,1)}), bf16[8,64,512]{2,1,0:T(8,128)(2,1)S(1)}, u32[]{:S(2)}, u32[]{:S(2)}) async-start(bf16[8,64,512]{2,1,0:T(8,128)(2,1)} %plane.1), calls=%async_computation.5 | async-start | bytes 1048576 | tf_op jit(solution)/shard_map/all_to_all | solution.py:338
  144.3 3.4 %collective-permute-start.7 = (bf16[128,512]{1,0:T(8,128)(2,1)S(1)}, bf16[128,512]{1,0:T(8,128)(2,1)S(1)}, u32[]{:S(2)}, u32[]{:S(2)}) collective-permute-start(bf16[128,512]{1,0:T(8,128)(2,1)S(1)} %copy-done.26), channel_id=1, source_target_pairs={{0,1},{1,0},{2,3},{3,2},{4,5},{5,4},{6,7},{7,6},{8,9},{9,8},{10,11... | collective-permute-start | bytes 393224 | tf_op jit(solution)/shard_map/ppermute | solution.py:330
  159.5 6.4 %collective-permute-start.11 = (f32[56,512]{1,0:T(8,128)S(1)}, f32[56,512]{1,0:T(8,128)S(1)}, u32[]{:S(2)}, u32[]{:S(2)}) collective-permute-start(f32[56,512]{1,0:T(8,128)S(1)} %get-tuple-element.59), channel_id=1, source_target_pairs={{0,1},{1,0},{2,3},{3,2},{4,5},{5,4},{6,7},{7,6},{8,9},{9,8},{10,11... | collective-permute-start | bytes 344072 | tf_op jit(solution)/shard_map/ppermute | solution.py:330

commit v4 on v3

--- a/solution.py
+++ b/solution.py
@@ -35,7 +35,7 @@
 
 
 VM = pl.BlockSpec(memory_space=pltpu.VMEM)
-ANY = pl.BlockSpec(memory_space=pl.ANY)
+HBM = pl.BlockSpec(memory_space=pltpu.HBM)
 
 
 def kernel(body, outs, name, limit, scratch=(), specs=None, out_specs=None, alias=None):
@@ -143,14 +143,12 @@
     decay = jnp.exp(total)
     for p in range(PS):
         h, at = p // PER, (p % PER) * ROWS
-        start[p, :ROWS] = run[h][at : at + ROWS]
-        start[p, ROWS:] = jnp.broadcast_to(decay[:, col_of(h)], (8, DK))
-
-
-def unpack_w(recv, w):
-    for p in range(PS):
-        for z in range(ZS):
-            w[z * 256 + p * 16 : z * 256 + p * 16 + 16] = recv[p, z * 16 : z * 16 + 16]
+        start[p, :ROWS] = run[h][at : at + ROWS].astype(BF16)
+        row = decay[:, col_of(h)]
+        top = row.astype(BF16).astype(F32)
+        start[p, ROWS:] = jnp.concatenate(
+            [jnp.broadcast_to(top, (8, DK)), jnp.broadcast_to(row - top, (8, DK))], axis=0
+        ).astype(BF16)
 
 
 def added_states(key, v, beta, n):
@@ -161,28 +159,64 @@
     return [dot_hl(vals[:, col_of(h)], tail[:, col_of(h)], TN) for h in range(HALF)], jnp.exp(last)
 
 
-def keys_body(recv, tok, beta, v, start, key_o, send, w):
-    unpack_w(recv, w)
+def load(pairs, sems):
+    copies = [pltpu.make_async_copy(a, b, sems.at[i]) for i, (a, b) in enumerate(pairs)]
+    for copy in copies:
+        copy.start()
+    return copies
+
+
+def far_keys_body(recv, far, far_peer, _, key_o, w, a, b, sems):
+    copies = load(((far, a), (far_peer, b)), sems)
+    for p in range(PS):
+        for z in range(ZS):
+            w[z * 256 + p * 16 : z * 256 + p * 16 + 16] = recv[p, z * 16 : z * 16 + 16]
+    for copy in copies:
+        copy.wait()
+    first = is_first()
+    key_a, key_b = dot(a[...], w[...]), dot(b[...], w[...])
+    key_o[:TOK] = pick(first, key_a, key_b).astype(BF16)
+    key_o[TOK:] = pick(first, key_b, key_a).astype(BF16)
+
+
+def near_keys_body(tok, w, key_o):
     key_o[...] = dot(tok[...], w[...]).astype(BF16)
+
+
+def odd_z():
+    return lax.rem(lax.axis_index("z"), 2) == 1
+
+
+def keys_body(mine, theirs, beta_h, v_h, start, _, key_o, send, w_o, beta, v, sems):
+    copies = load(((beta_h, beta), (v_h, v)), sems)
+    odd = odd_z()
+    key_o[:, :QUART] = pick(odd, theirs[...], mine[...])
+    key_o[:, QUART:] = pick(odd, mine[...], theirs[...])
+    for copy in copies:
+        copy.wait()
     run = [jnp.zeros((DK, DK), F32)] * HALF
     for n in range(BLOCKS):
         parts, decay = added_states(key_o, v, beta, n)
         run = [decay[:, col_of(h)] * run[h] + parts[h] for h in range(HALF)]
     for p in range(PS):
         h, at = p // PER, (p % PER) * ROWS
-        send[p, : ROWS + 8] = start[p]
-        send[p, ROWS + 8 :] = run[h][at : at + ROWS]
+        send[p, : ROWS + 16] = start[p]
+        send[p, ROWS + 16 :] = run[h][at : at + ROWS].astype(BF16)
 
 
 def scan_body(recv, send):
+    def decay(p):
+        rows = recv[p, ROWS : ROWS + 16].astype(F32)
+        return rows[:1] + rows[8:9]
+
     run = jnp.zeros((ROWS, DK), F32)
     for p in reversed(range(PS)):
-        send[p, :ROWS] = run
-        run = recv[p, ROWS : ROWS + 1] * run + recv[p, :ROWS]
+        send[p, :ROWS] = run.astype(BF16)
+        run = decay(p) * run + recv[p, :ROWS].astype(F32)
     run = jnp.zeros((ROWS, DK), F32)
     for p in range(PS):
-        send[p, ROWS:] = run
-        run = recv[p, ROWS : ROWS + 1] * run + recv[p, ROWS + 8 :]
+        send[p, ROWS:] = run.astype(BF16)
+        run = decay(p) * run + recv[p, ROWS + 16 :].astype(F32)
 
 
 def inner_body(q_r, g_r, v_r, key_r, beta, kd_o, local):
@@ -204,13 +238,13 @@
             local[tok_of(n), c] = q[:, c] * qd - k[:, c] * kd
 
 
-def gate_body(recv, adds, key_r, v_r, beta, q_r, g_r, kd_in, local, logit, lat, up,
+def gate_body(recv, adds, key_r, v_r, beta, q_r, g_r, kd_in, local, logit, lat, up, _,
               kd_o, kd_keep, kd_give, gate_o, gate_keep, gate_give, up_part, lat_part, delta):
     first = is_first()
     high = low_mask()[1].astype(BF16)
-    back = [jnp.concatenate([recv[h * PER + i, :ROWS] for i in range(PER)], axis=0)
+    back = [jnp.concatenate([recv[h * PER + i, :ROWS] for i in range(PER)], axis=0).astype(F32)
             for h in range(HALF)]
-    run = [jnp.concatenate([recv[h * PER + i, ROWS:] for i in range(PER)], axis=0)
+    run = [jnp.concatenate([recv[h * PER + i, ROWS:] for i in range(PER)], axis=0).astype(F32)
            for h in range(HALF)]
     grads = list(back)
     for n in reversed(range(BLOCKS)):
@@ -230,7 +264,7 @@
         ) * jnp.exp(beta[tok_of(n)])
         delta[tok_of(n)] += q_r[tok_of(n)].astype(F32) * qd
         run = [decay[:, col_of(h)] * run[h] + parts[h] for h in range(HALF)]
-    odd = lax.rem(lax.axis_index("z"), 2) == 1
+    odd = odd_z()
     kd_lo, kd_hi = kd_o[:, :QUART], kd_o[:, QUART:]
     kd_keep[...] = pick(odd, kd_hi, kd_lo)
     kd_give[...] = pick(odd, kd_lo, kd_hi)
@@ -282,13 +316,11 @@
         send[p, :SMALL] = few
 
 
-def through_body(kd, recv, keep, give, w):
-    first = is_first()
-    unpack_w(recv, w)
-    mine = pick(first, kd[:TOK], kd[TOK:])
-    other = pick(first, kd[TOK:], kd[:TOK])
-    give[...] = dot(other, w[...], NT)
-    keep[...] = dot(mine, w[...], NT)
+def through_body(kd, kd_far, w, w_far, keep, give):
+    first = is_first()
+    total = dot(kd[...], w[...], NT) + dot(kd_far[...], w_far[...], NT)
+    give[...] = pick(first, total[TOK:], total[:TOK])
+    keep[...] = pick(first, total[:TOK], total[TOK:])
 
 
 def input_body(keep, got, lat, down, out):
@@ -307,7 +339,7 @@
         send[z, SMALL:, QUART:] = jnp.zeros((16, QUART), BF16)
 
 
-def total_body(recv, keep, give):
+def total_body(recv, a, b, keep, give):
     first = is_first()
     small = jnp.sum(recv[:, :SMALL].astype(F32), axis=0)
     parts = [recv[z, SMALL:, :QUART].astype(F32) for z in range(ZS)]
@@ -344,13 +376,16 @@
     q, g, v = queries[0], out_grad[0], values[0]
     half_bf = shape((PAIR, WIDTH), BF16)
     half_f = shape((PAIR, WIDTH))
-    packed = shape((PS, ROWS + 8, DK))
+    packed = shape((PS, ROWS + 16, DK), BF16)
+    quarter = shape((PAIR, QUART), BF16)
 
     lo, hi = key_weight[:, :WIDTH], key_weight[:, WIDTH:]
     w_m, w_p = jnp.where(first, lo, hi), swap(jnp.where(first, hi, lo))
     w_chip = jnp.concatenate([jnp.where(first, w_m, w_p), jnp.where(first, w_p, w_m)], axis=0)
-    w_z = a2a(jnp.broadcast_to(w_chip[None], (ZS, 16, WIDTH)), "z").reshape(ZS * 16, WIDTH)
-    w_all = a2a(jnp.broadcast_to(w_z[None], (PS, ZS * 16, WIDTH)), XY)
+    w_two = jnp.stack([w_chip[:, :QUART], w_chip[:, QUART:]])
+    w_z = jnp.broadcast_to(w_two[None], (ZS // 2, 2, 16, QUART)).reshape(ZS, 16, QUART)
+    w_z = a2a(w_z, "z").reshape(ZS * 16, QUART)
+    w_all = a2a(jnp.broadcast_to(w_z[None], (PS, ZS * 16, QUART)), XY)
 
     tok, lat, logit, beta, q, g, v, add_g, start = kernel(
         gates_body,
@@ -360,20 +395,30 @@
     )(own, swap(own), gate_down, gate_up, gate_bias[None], q, g, v, swap(q), swap(g), swap(v))
     far = across(own)
     far_peer = swap(far)
-    keys, send = kernel(
-        keys_body, (half_bf, shape((PS, 2 * ROWS + 8, DK))), "keys", KEYS,
-        scratch=[pltpu.VMEM((MODEL, WIDTH), BF16)],
-    )(w_all, tok, beta, v, start)
+    tok_sems = pltpu.SemaphoreType.DMA((2,))
+    keys_far, w = kernel(
+        far_keys_body, (quarter, shape((MODEL, QUART), BF16)), "far_keys", 16,
+        specs=[VM, HBM, HBM, HBM], out_specs=(VM, VM),
+        scratch=[pltpu.VMEM((TOK, MODEL), BF16)] * 2 + [tok_sems],
+    )(w_all, far, far_peer, beta)
+    keys_mine = kernel(near_keys_body, quarter, "near_keys", 16)(tok, w)
+    keys, send, w = kernel(
+        keys_body,
+        (half_bf, shape((PS, 2 * ROWS + 16, DK), BF16), shape((MODEL, QUART), BF16)),
+        "keys", 16, specs=[VM, VM, HBM, HBM, VM, HBM], out_specs=(VM, VM, HBM), alias={5: 2},
+        scratch=[pltpu.VMEM((PAIR, WIDTH), F32), pltpu.VMEM((PAIR, WIDTH), BF16), tok_sems],
+    )(keys_mine, across(keys_far), beta, v, start, w)
+    w_far = across(w)
     recv = a2a(send, XY)
     kd_local, local_part = kernel(inner_body, (half_f, half_f), "inner", BIG)(q, g, v, keys, beta)
-    recv = a2a(kernel(scan_body, shape((PS, 2 * ROWS, DK)), "scan", 8)(recv), XY)
-    quarter = shape((PAIR, QUART), BF16)
+    recv = a2a(kernel(scan_body, shape((PS, 2 * ROWS, DK), BF16), "scan", 8)(recv), XY)
     kd, kd_keep, kd_give, gate, gate_m, gate_x, up_part, lat_part = kernel(
         gate_body,
         (half_bf, quarter, quarter, half_bf, shape((TOK, WIDTH), BF16),
          shape((TOK, WIDTH), BF16), shape((RANK, WIDTH)), shape((PAIR, RANK))),
         "gate", BIG, scratch=[pltpu.VMEM((PAIR, WIDTH), F32)],
-    )(recv, add_g, keys, v, beta, q, g, kd_local, local_part, logit, lat, gate_up)
+        specs=[VM] * 12 + [HBM], out_specs=(VM,) * 8,
+    )(recv, add_g, keys, v, beta, q, g, kd_local, local_part, logit, lat, gate_up, w_far)
     far_kd = across(kd_give)
     lat_own, small = kernel(
         down_body, (shape((TOK, RANK), BF16), shape((SMALL, WIDTH), BF16)), "down", 8
@@ -382,24 +427,25 @@
         weight_body, shape((PS, SMALL + ZS * 8, WIDTH), BF16), "weights", BIG
     )(tok, kd_keep, far, far_peer, far_kd, small)
     send = kernel(plane_body, shape((ZS, SMALL + 16, WIDTH), BF16), "plane", 8)(a2a(send, XY))
-    end = shape((SMALL + 8, WIDTH))
-    keep, give = kernel(total_body, (end, end), "total", 8)(a2a(send, "z"))
-    down_grad, up_grad, key_weight_grad = kernel(
-        out_body,
-        (shape((RANK, MODEL)), shape((RANK, 2 * WIDTH)), shape((8, 2 * WIDTH))), "grads", 8,
-    )(keep, swap(give))
-
     gate_p = swap(gate_x)
     gate_grad = jnp.concatenate(
         [jnp.where(first, gate_m, gate_p), jnp.where(first, gate_p, gate_m)], axis=1
     )
     mine, other = kernel(
-        through_body, (shape((TOK, MODEL)), shape((TOK, MODEL))), "through", BIG,
-        scratch=[pltpu.VMEM((MODEL, WIDTH), BF16)],
-    )(kd, w_all)
-    input_grad = kernel(input_body, shape((TOK, MODEL), BF16), "input", 16)(
+        through_body, (shape((TOK, MODEL)), shape((TOK, MODEL))), "through", BIG
+    )(kd_keep, kd_give, w, w_far)
+    input_grad = kernel(input_body, shape((TOK, MODEL), BF16), "input", BIG)(
         mine, swap(other), lat_own, gate_down
     )
+    end = shape((SMALL + 8, WIDTH))
+    keep, give = kernel(
+        total_body, (end, end), "total", 8, specs=[VM, HBM, HBM], out_specs=(VM, VM)
+    )(a2a(send, "z"), input_grad, gate_grad)
+    down_grad, up_grad, key_weight_grad = kernel(
+        out_body,
+        (shape((RANK, MODEL)), shape((RANK, 2 * WIDTH)), shape((8, 2 * WIDTH))), "grads", 8,
+    )(keep, swap(give))
+
     return (input_grad[None], gate_grad[None], key_weight_grad, down_grad, up_grad)
 
 

time: 168 us -> 155 us (0.923)
  waiting for transfers between devices: 60.1 us -> 49.5 us
  local copies, waits for them, and re-layouts: 12 us -> 13.9 us
  blocking collectives: 14.2 us -> 12.4 us
    all_to_all x5, waiting for transfers between devices: 55.1 us -> 40 us  [a2a(): return lax.all_to_all(a, axis, 0, 0)]
    ppermute x10, starting transfers between devices: 22.5 us -> 18.3 us  [swap(): return lax.ppermute(a, 'c', SWAP)]
    ppermute x2 -> x4, waiting for transfers between devices: 0.01 us -> 3.18 us  [across(): return lax.ppermute(a, 'z', [(i, i ^ 1) for i in range(ZS)])]
    ppermute x2 -> x4, starting transfers between devices: 0.63 us -> 3.5 us  [across(): return lax.ppermute(a, 'z', [(i, i ^ 1) for i in range(ZS)])]
    all_to_all x1, blocking collectives: 14.2 us -> 12.4 us  [a2a(): return lax.all_to_all(a, axis, 0, 0)]
    unnamed x54 -> x58, local copies, waits for them, and re-layouts: 10.5 us -> 12.2 us
    pallas_call x4 -> x6, Pallas kernels: 5.08 us -> 5.11 us  [the longest x1 2.6 us: local(): kernel(input_body, shape((TOK, MODEL), BF16), 'input', BIG)]
  transfers between devices with their start and end apart: 17 -> 19, of which waited for: 10 -> 13; matrix products, arithmetic and copies ran while one was open for 0% -> 1% of each run, Pallas kernels for 14% -> 12%
where the time goes in v4:
time: 155 us; the launch traced here: 154 us
  waiting for transfers between devices  49.5 us (32%)
  starting transfers between devices  45.9 us (30%)
  Pallas kernels  29.5 us (19%)
  local copies, waits for them, and re-layouts  13.9 us (9%)
  blocking collectives  12.4 us (8%)
  other arithmetic  2.32 us (1%)
    all_to_all x5, waiting for transfers between devices, a2a(): return lax.all_to_all(a, axis, 0, 0)  40 us
    all_to_all x5, starting transfers between devices, a2a(): return lax.all_to_all(a, axis, 0, 0)  24.1 us
    ppermute x10, starting transfers between devices, swap(): return lax.ppermute(a, 'c', SWAP)  18.3 us
    all_to_all x1, blocking collectives, a2a(): return lax.all_to_all(a, axis, 0, 0)  12.4 us
    unnamed x58, local copies, waits for them, and re-layouts  12.2 us
    ppermute x10, waiting for transfers between devices, swap(): return lax.ppermute(a, 'c', SWAP)  6.36 us
    pallas_call x1, Pallas kernels, local(): kernel(gates_body, (shape((PAIR, MODEL), BF16), shape((PAIR, RANK), BF16)...  5.14 us
    pallas_call x1, Pallas kernels, local(): kernel(inner_body, (half_f, half_f), 'inner', BIG)(q, g, v, keys, beta)  5.12 us
  transfers between devices with their start and end apart: 19, of which 13 were waited for; matrix products, arithmetic and copies ran while one was open for 1% of the time, Pallas kernels for 12%

profile of v4, /device:TPU:1, one launch (start us, length us, event | category | flops | bytes accessed | tf_op | source)
XLA Modules:
  0.0 154.4 jit_solution(1273695796427877043)
XLA Ops:
  0.7 0.8 broadcast_select_fusion.4
  1.5 3.2 %collective-permute-start.4 = (bf16[8,512]{1,0:T(8,128)(2,1)S(1)}, bf16[8,512]{1,0:T(8,128)(2,1)S(1)}, u32[]{:S(2)}, u32[]{:S(2)}) collective-permute-start(bf16[8,512]{1,0:T(8,128)(2,1)S(1)} %broadcast_select_fusion.4), channel_id=1, source_target_pairs={{0,1},{1,0},{2,3},{3,2},{4,5},{5,4},{6,7},{7,6},{8,9},{9,8},{10,11... | collective-permute-start | bytes 24584 | tf_op jit(solution)/shard_map/ppermute | solution.py:362
  4.7 0.8 collective-permute-done.4
  5.5 0.7 broadcast_select_fusion.3
  6.3 0.6 broadcast_in_dim.23
  6.9 6.4 %all-to-all-start = ((bf16[8,16,256]{2,1,0:T(8,128)(2,1)}), bf16[8,16,256]{2,1,0:T(8,128)(2,1)S(1)}, u32[]{:S(2)}, u32[]{:S(2)}) async-start(bf16[8,16,256]{2,1,0:T(8,128)(2,1)} %bitcast.7), calls=%async_computation | async-start | bytes 131072 | tf_op jit(solution)/shard_map/all_to_all | solution.py:370
  13.4 1.5 collective-permute-start.5
  14.8 5.8 %all-to-all-done = bf16[8,16,256]{2,1,0:T(8,128)(2,1)S(1)} async-done(((bf16[8,16,256]{2,1,0:T(8,128)(2,1)}), bf16[8,16,256]{2,1,0:T(8,128)(2,1)S(1)}, u32[]{:S(2)}, u32[]{:S(2)}) %all-to-all-start) | async-done | bytes 65568 | tf_op jit(solution)/shard_map/all_to_all | solution.py:370
  20.6 1.1 broadcast_in_dim.25
  21.7 6.9 %all-to-all-start.1 = ((bf16[16,128,256]{2,1,0:T(8,128)(2,1)}), bf16[16,128,256]{2,1,0:T(8,128)(2,1)S(1)}, u32[]{:S(2)}, u32[]{:S(2)}) async-start(bf16[16,128,256]{2,1,0:T(8,128)(2,1)} %broadcast_in_dim.25), calls=%async_computation.1 | async-start | bytes 2097152 | tf_op jit(solution)/shard_map/all_to_all | solution.py:370
  28.6 2.5 %collective-permute-start = (bf16[128,2048]{1,0:T(8,128)(2,1)S(1)}, bf16[128,2048]{1,0:T(8,128)(2,1)S(1)}, u32[]{:S(2)}, u32[]{:S(2)}) collective-permute-start(bf16[128,2048]{1,0:T(8,128)(2,1)S(1)} %bitcast.17), channel_id=1, source_target_pairs={{0,1},{1,0},{2,3},{3,2},{4,5},{5,4},{6,7},{7,6},{8,9},{9,8},{10,11... | collective-permute-start | bytes 1572872 | tf_op jit(solution)/shard_map/ppermute | solution.py:362
  31.2 0.4 collective-permute-start.1
  31.7 0.4 collective-permute-start.2
  32.1 1.6 %collective-permute-done.1.q_p = bf16[128,1024]{1,0:T(8,128)(2,1)S(1)} collective-permute-done((bf16[128,1024]{1,0:T(8,128)(2,1)S(1)}, bf16[128,1024]{1,0:T(8,128)(2,1)S(1)}, u32[]{:S(2)}, u32[]{:S(2)}) %collective-permute-start.1) | collective-permute-done | bytes 262176 | tf_op jit(solution)/shard_map/ppermute | solution.py:362
  33.7 0.4 collective-permute-done.3.v_p
  34.1 0.4 collective-permute-done.2.g_p
  34.5 0.3 copy-done.24
  34.8 0.4 copy-done.25
  35.4 5.1 %gates.1 = (bf16[256,2048]{1,0:T(8,128)(2,1)}, bf16[256,16]{1,0:T(8,128)(2,1)}, f32[256,512]{1,0:T(8,128)}, f32[256,512]{1,0:T(8,128)}, bf16[256,512]{1,0:T(8,12...) custom-call(bf16[128,2048]{1,0:T(8,128)(2,1)} %bitcast.16, ...), custom_call_target="tpu_custom_call" | custom-call | tf_op jit(solution)/shard_map/gates/pallas_call | solution.py:390
  40.5 0.8 copy-done.7
  41.3 2.0 %all-to-all-done.1.recv = bf16[16,128,256]{2,1,0:T(8,128)(2,1)S(1)} async-done(((bf16[16,128,256]{2,1,0:T(8,128)(2,1)}), bf16[16,128,256]{2,1,0:T(8,128)(2,1)S(1)}, u32[]{:S(2)}, u32[]{:S(2)}) %all-to-all-start.1) | async-done | bytes 1048608 | tf_op jit(solution)/shard_map/all_to_all | solution.py:370
  43.3 1.0 copy-done.2
  44.3 1.0 copy-done.6
  45.4 1.0 copy-done.8
  46.4 0.6 far_keys.1
  47.0 0.3 collective-permute-start.7
  47.3 0.4 near_keys.1.mine
  47.8 3.2 %collective-permute-done.7.theirs = bf16[256,256]{1,0:T(8,128)(2,1)S(1)} collective-permute-done((bf16[256,256]{1,0:T(8,128)(2,1)S(1)}, bf16[256,256]{1,0:T(8,128)(2,1)S(1)}, u32[]{:S(2)}, u32[]{:S(2)}) %collective-permute-start.7) | collective-permute-done | bytes 131104 | tf_op jit(solution)/shard_map/ppermute | solution.py:366
  51.0 0.6 keys.1
  51.6 0.7 copy-done.9
  52.5 12.4 %all_to_all.30.recv = bf16[16,80,128]{2,1,0:T(8,128)(2,1)S(1)} all-to-all(bf16[16,80,128]{2,1,0:T(8,128)(2,1)S(1)} %get-tuple-element.42), channel_id=1, replica_groups=mesh['z'=8,'x'=4,'y'=4,'c'=2] {'x','y'}, dimensions={0} | all-to-all | bytes 655360 | tf_op jit(solution)/shard_map/all_to_all | solution.py:370
  64.9 0.8 scan.1
  65.7 3.5 %all-to-all-start.3 = ((bf16[16,64,128]{2,1,0:T(8,128)(2,1)}), bf16[16,64,128]{2,1,0:T(8,128)(2,1)S(1)}, u32[]{:S(2)}, u32[]{:S(2)}) async-start(bf16[16,64,128]{2,1,0:T(8,128)(2,1)} %scan.1), calls=%async_computation.3 | async-start | bytes 524288 | tf_op jit(solution)/shard_map/all_to_all | solution.py:370
  69.2 5.1 %inner.1 = (f32[256,512]{1,0:T(8,128)}, f32[256,512]{1,0:T(8,128)}) custom-call(bf16[256,512]{1,0:T(8,128)(2,1)} %get-tuple-element.45.q_r, bf16[256,512]{1,0:T(8,128)(2,1)} %get-tuple-element.46.g_r, bf16[256,512]{1,0:T(8,128)(2,1)} %get-tuple-element.40.v_h.v_r, bf16[256,512]{1,0:T(8,128)(2,1)} %copy-done.9, f32[256,512]{1,0:T(8,128)} %get-tuple-element.37._.beta_h.beta), custom_call_target="tpu_custom_call" | custom-call | tf_op jit(solution)/shard_map/inner/pallas_call | solution.py:413
  74.3 2.2 %all-to-all-done.3.recv = bf16[16,64,128]{2,1,0:T(8,128)(2,1)S(1)} async-done(((bf16[16,64,128]{2,1,0:T(8,128)(2,1)}), bf16[16,64,128]{2,1,0:T(8,128)(2,1)S(1)}, u32[]{:S(2)}, u32[]{:S(2)}) %all-to-all-start.3) | async-done | bytes 262176 | tf_op jit(solution)/shard_map/all_to_all | solution.py:370
  76.5 0.7 copy-done.16
  77.2 0.4 copy-done.15
  77.6 4.5 %gate.1 = (bf16[256,512]{1,0:T(8,128)(2,1)}, bf16[256,256]{1,0:T(8,128)(2,1)}, bf16[256,256]{1,0:T(8,128)(2,1)}, bf16[256,512]{1,0:T(8,128)(2,1)}, bf16[128,512]...) custom-call(bf16[16,64,128]{2,1,0:T(8,128)(2,1)} %copy-done.16, ...), custom_call_target="tpu_custom_call" | custom-call | tf_op jit(solution)/shard_map/gate/pallas_call | solution.py:415
  82.1 1.6 %collective-permute-start.12 = (bf16[256,256]{1,0:T(8,128)(2,1)}, bf16[256,256]{1,0:T(8,128)(2,1)S(1)}, u32[]{:S(2)}, u32[]{:S(2)}) collective-permute-start(bf16[256,256]{1,0:T(8,128)(2,1)} %get-tuple-element.53.kd_far), channel_id=1, source_target_pairs={{0,32},{32,0},{64,96},{96,64},{128,160},{160,128},{192,224},{224,1... | collective-permute-start | bytes 393224 | tf_op jit(solution)/shard_map/ppermute | solution.py:366
  83.7 6.1 %collective-permute-start.10 = (f32[256,16]{1,0:T(8,128)}, f32[256,16]{1,0:T(8,128)S(1)}, u32[]{:S(2)}, u32[]{:S(2)}) collective-permute-start(f32[256,16]{1,0:T(8,128)} %get-tuple-element.56.lat_a), channel_id=1, source_target_pairs={{0,1},{1,0},{2,3},{3,2},{4,5},{5,4},{6,7},{7,6},{8,9},{9,8},{10,11... | collective-permute-start | bytes 49160 | tf_op jit(solution)/shard_map/ppermute | solution.py:362
  89.8 1.2 collective-permute-done.10.lat_b
  91.0 0.9 copy-done.11
  91.9 0.8 copy-done.14
  92.7 0.2 down.4
  92.9 0.6 copy-done.12
  93.5 0.6 copy-done.13
  94.1 0.7 copy-done.27
  94.8 3.9 %weights.1 = bf16[16,112,512]{2,1,0:T(8,128)(2,1)} custom-call(bf16[256,2048]{1,0:T(8,128)(2,1)} %get-tuple-element.36.tok, bf16[256,256]{1,0:T(8,128)(2,1)} %get-tuple-element.52.kd.kd_r, bf16[128,2048]{1,0:T(8,128)(2,1)} %copy-done.5, bf16[128,2048]{1,0:T(8,128)(2,1)} %copy-done.7, bf16[256,256]{1,0:T(8,128)(2,1)} %copy-done.27, bf16[48,512]{1,0:T(8,128)(2,1)} %copy-done.12), custom_call_target="tpu_custom_call" | custom-call | tf_op jit(solution)/shard_map/weights/pallas_call | solution.py:426
  98.6 3.7 %all-to-all-start.4 = ((bf16[16,112,512]{2,1,0:T(8,128)(2,1)}), bf16[16,112,512]{2,1,0:T(8,128)(2,1)S(1)}, u32[]{:S(2)}, u32[]{:S(2)}) async-start(bf16[16,112,512]{2,1,0:T(8,128)(2,1)} %weights.1), calls=%async_computation.4 | async-start | bytes 3670016 | tf_op jit(solution)/shard_map/all_to_all | solution.py:370
  102.3 3.8 %through.1 = (f32[128,2048]{1,0:T(8,128)}, f32[128,2048]{1,0:T(8,128)}) custom-call(bf16[256,256]{1,0:T(8,128)(2,1)} %get-tuple-element.52.kd.kd_r, bf16[256,256]{1,0:T(8,128)(2,1)} %get-tuple-element.53.kd_far, bf16[2048,256]{1,0:T(8,128)(2,1)} %copy-done, bf16[2048,256]{1,0:T(8,128)(2,1)} %copy-done.15), custom_call_target="tpu_custom_call" | custom-call | tf_op jit(solution)/shard_map/through/pallas_call | solution.py:434
  106.1 0.5 collective-permute-start.9
  106.6 22.0 %all-to-all-done.4.recv = bf16[16,112,512]{2,1,0:T(8,128)(2,1)S(1)} async-done(((bf16[16,112,512]{2,1,0:T(8,128)(2,1)}), bf16[16,112,512]{2,1,0:T(8,128)(2,1)S(1)}, u32[]{:S(2)}, u32[]{:S(2)}) %all-to-all-start.4) | async-done | bytes 1835040 | tf_op jit(solution)/shard_map/all_to_all | solution.py:370
  128.6 1.0 plane.1
  129.7 3.5 %all-to-all-start.5 = ((bf16[8,64,512]{2,1,0:T(8,128)(2,1)}), bf16[8,64,512]{2,1,0:T(8,128)(2,1)S(1)}, u32[]{:S(2)}, u32[]{:S(2)}) async-start(bf16[8,64,512]{2,1,0:T(8,128)(2,1)} %plane.1), calls=%async_computation.5 | async-start | bytes 1048576 | tf_op jit(solution)/shard_map/all_to_all | solution.py:370
  133.2 2.1 %collective-permute-start.11 = (bf16[128,512]{1,0:T(8,128)(2,1)S(1)}, bf16[128,512]{1,0:T(8,128)(2,1)S(1)}, u32[]{:S(2)}, u32[]{:S(2)}) collective-permute-start(bf16[128,512]{1,0:T(8,128)(2,1)S(1)} %copy-done.28), channel_id=1, source_target_pairs={{0,1},{1,0},{2,3},{3,2},{4,5},{5,4},{6,7},{7,6},{8,9},{9,8},{10,11... | collective-permute-start | bytes 393224 | tf_op jit(solution)/shard_map/ppermute | solution.py:362
  135.3 1.0 collective-permute-done.11
  136.3 0.8 pad_maximum_fusion
  137.1 1.0 copy-done.17
  138.1 2.6 %input.1.a = bf16[128,2048]{1,0:T(8,128)(2,1)} custom-call(f32[128,2048]{1,0:T(8,128)} %get-tuple-element.54.keep, f32[128,2048]{1,0:T(8,128)} %copy-done.17, bf16[128,16]{1,0:T(8,128)(2,1)} %copy-done.13, bf16[16,2048]{1,0:T(8,128)(2,1)} %down.5), custom_call_target="tpu_custom_call" | custom-call | tf_op jit(solution)/shard_map/input/pallas_call | solution.py:437
  140.7 8.1 %all-to-all-done.5.recv = bf16[8,64,512]{2,1,0:T(8,128)(2,1)S(1)} async-done(((bf16[8,64,512]{2,1,0:T(8,128)(2,1)}), bf16[8,64,512]{2,1,0:T(8,128)(2,1)S(1)}, u32[]{:S(2)}, u32[]{:S(2)}) %all-to-all-start.5) | async-done | bytes 524320 | tf_op jit(solution)/shard_map/all_to_all | solution.py:370
  148.8 1.0 copy-done.4
  149.9 2.8 %collective-permute-start.13 = (f32[56,512]{1,0:T(8,128)S(1)}, f32[56,512]{1,0:T(8,128)S(1)}, u32[]{:S(2)}, u32[]{:S(2)}) collective-permute-start(f32[56,512]{1,0:T(8,128)S(1)} %get-tuple-element.63), channel_id=1, source_target_pairs={{0,1},{1,0},{2,3},{3,2},{4,5},{5,4},{6,7},{7,6},{8,9},{9,8},{10,11... | collective-permute-start | bytes 344072 | tf_op jit(solution)/shard_map/ppermute | solution.py:362
  152.7 1.0 collective-permute-done.13.theirs
  153.7 0.7 grads.1
  (55 shorter events, 0.8 us)
Async XLA Ops:
  0.6 28.0 %copy-start.18 = (bf16[1,128,2048]{2,1,0:T(8,128)(2,1)S(1)}, bf16[1,128,2048]{2,1,0:T(8,128)(2,1)}, u32[]{:S(2)}) copy-start(bf16[1,128,2048]{2,1,0:T(8,128)(2,1)} %param.8) | copy-start | bytes 1572868
  0.6 30.6 %copy-start.20 = (bf16[1,128,1024]{2,1,0:T(8,128)(2,1)S(1)}, bf16[1,128,1024]{2,1,0:T(8,128)(2,1)}, u32[]{:S(2)}) copy-start(bf16[1,128,1024]{2,1,0:T(8,128)(2,1)} %param.9) | copy-start | bytes 786436
  0.7 31.1 %copy-start.21 = (bf16[1,128,1024]{2,1,0:T(8,128)(2,1)S(1)}, bf16[1,128,1024]{2,1,0:T(8,128)(2,1)}, u32[]{:S(2)}) copy-start(bf16[1,128,1024]{2,1,0:T(8,128)(2,1)} %param.11) | copy-start | bytes 786436
  1.5 4.1 %collective-permute-start.4 = (bf16[8,512]{1,0:T(8,128)(2,1)S(1)}, bf16[8,512]{1,0:T(8,128)(2,1)S(1)}, u32[]{:S(2)}, u32[]{:S(2)}) collective-permute-start(bf16[8,512]{1,0:T(8,128)(2,1)S(1)} %broadcast_select_fusion.4), channel_id=1, source_target_pairs={{0,1},{1,0},{2,3},{3,2},{4,5},{5,4},{6,7},{7,6},{8,9},{9,8},{10,11... | collective-permute-start | bytes 24584 | tf_op jit(solution)/shard_map/ppermute | solution.py:362
  6.9 13.7 %all-to-all-start = ((bf16[8,16,256]{2,1,0:T(8,128)(2,1)}), bf16[8,16,256]{2,1,0:T(8,128)(2,1)S(1)}, u32[]{:S(2)}, u32[]{:S(2)}) async-start(bf16[8,16,256]{2,1,0:T(8,128)(2,1)} %bitcast.7), calls=%async_computation | async-start | bytes 131072 | tf_op jit(solution)/shard_map/all_to_all | solution.py:370
  13.4 17.7 %collective-permute-start.5 = (bf16[128,2048]{1,0:T(8,128)(2,1)}, bf16[128,2048]{1,0:T(8,128)(2,1)S(1)}, u32[]{:S(2)}, u32[]{:S(2)}) collective-permute-start(bf16[128,2048]{1,0:T(8,128)(2,1)} %bitcast.15), channel_id=1, source_target_pairs={{0,32},{32,0},{64,96},{96,64},{128,160},{160,128},{192,224},{224,1... | collective-permute-start | bytes 1572872 | tf_op jit(solution)/shard_map/ppermute | solution.py:366
  21.7 9.9 %copy-start.22 = (bf16[1,128,1024]{2,1,0:T(8,128)(2,1)S(1)}, bf16[1,128,1024]{2,1,0:T(8,128)(2,1)}, u32[]{:S(2)}) copy-start(bf16[1,128,1024]{2,1,0:T(8,128)(2,1)} %param.10) | copy-start | bytes 786436
  21.7 21.6 %all-to-all-start.1 = ((bf16[16,128,256]{2,1,0:T(8,128)(2,1)}), bf16[16,128,256]{2,1,0:T(8,128)(2,1)S(1)}, u32[]{:S(2)}, u32[]{:S(2)}) async-start(bf16[16,128,256]{2,1,0:T(8,128)(2,1)} %broadcast_in_dim.25), calls=%async_computation.1 | async-start | bytes 2097152 | tf_op jit(solution)/shard_map/all_to_all | solution.py:370
  28.6 5.9 %collective-permute-start = (bf16[128,2048]{1,0:T(8,128)(2,1)S(1)}, bf16[128,2048]{1,0:T(8,128)(2,1)S(1)}, u32[]{:S(2)}, u32[]{:S(2)}) collective-permute-start(bf16[128,2048]{1,0:T(8,128)(2,1)S(1)} %bitcast.17), channel_id=1, source_target_pairs={{0,1},{1,0},{2,3},{3,2},{4,5},{5,4},{6,7},{7,6},{8,9},{9,8},{10,11... | collective-permute-start | bytes 1572872 | tf_op jit(solution)/shard_map/ppermute | solution.py:362
  31.1 12.2 %copy-start.5 = (bf16[128,2048]{1,0:T(8,128)(2,1)}, bf16[128,2048]{1,0:T(8,128)(2,1)S(1)}, u32[]{:S(2)}) copy-start(bf16[128,2048]{1,0:T(8,128)(2,1)S(1)} %collective-permute-done.5.far) | copy-start | bytes 1572868
  31.1 9.4 %collective-permute-start.6 = (bf16[128,2048]{1,0:T(8,128)(2,1)S(1)}, bf16[128,2048]{1,0:T(8,128)(2,1)S(1)}, u32[]{:S(2)}, u32[]{:S(2)}) collective-permute-start(bf16[128,2048]{1,0:T(8,128)(2,1)S(1)} %collective-permute-done.5.far), channel_id=1, source_target_pairs={{0,1},{1,0},{2,3},{3,2},{4,5},{5,4},{6,7},{7,6},{8,9},{9,8},{10,11... | collective-permute-start | bytes 1572872 | tf_op jit(solution)/shard_map/ppermute | solution.py:362
  31.2 2.5 %collective-permute-start.1 = (bf16[128,1024]{1,0:T(8,128)(2,1)S(1)}, bf16[128,1024]{1,0:T(8,128)(2,1)S(1)}, u32[]{:S(2)}, u32[]{:S(2)}) collective-permute-start(bf16[128,1024]{1,0:T(8,128)(2,1)S(1)} %bitcast.20), channel_id=1, source_target_pairs={{0,1},{1,0},{2,3},{3,2},{4,5},{5,4},{6,7},{7,6},{8,9},{9,8},{10,11... | collective-permute-start | bytes 786440 | tf_op jit(solution)/shard_map/ppermute | solution.py:362
  31.6 2.5 %collective-permute-start.3 = (bf16[128,1024]{1,0:T(8,128)(2,1)S(1)}, bf16[128,1024]{1,0:T(8,128)(2,1)S(1)}, u32[]{:S(2)}, u32[]{:S(2)}) collective-permute-start(bf16[128,1024]{1,0:T(8,128)(2,1)S(1)} %bitcast.24), channel_id=1, source_target_pairs={{0,1},{1,0},{2,3},{3,2},{4,5},{5,4},{6,7},{7,6},{8,9},{9,8},{10,11... | collective-permute-start | bytes 786440 | tf_op jit(solution)/shard_map/ppermute | solution.py:362
  31.7 2.8 %collective-permute-start.2 = (bf16[128,1024]{1,0:T(8,128)(2,1)S(1)}, bf16[128,1024]{1,0:T(8,128)(2,1)S(1)}, u32[]{:S(2)}, u32[]{:S(2)}) collective-permute-start(bf16[128,1024]{1,0:T(8,128)(2,1)S(1)} %bitcast.22), channel_id=1, source_target_pairs={{0,1},{1,0},{2,3},{3,2},{4,5},{5,4},{6,7},{7,6},{8,9},{9,8},{10,11... | collective-permute-start | bytes 786440 | tf_op jit(solution)/shard_map/ppermute | solution.py:362
  33.7 0.8 copy-start.23
  34.1 0.7 copy-start.24
  34.5 0.7 copy-start.25
  34.5 0.9 copy-start.19
  40.5 6.8 %copy-start.1 = (bf16[256,2048]{1,0:T(8,128)(2,1)S(1)}, bf16[256,2048]{1,0:T(8,128)(2,1)}, u32[]{:S(2)}) copy-start(bf16[256,2048]{1,0:T(8,128)(2,1)} %get-tuple-element.36.tok) | copy-start | bytes 3145732
  40.5 0.8 copy-start.7
  43.3 1.0 copy-start.2
  44.3 1.0 copy-start.6
  45.4 1.0 copy-start.8
  46.4 4.5 %copy-start.3 = (bf16[256,512]{1,0:T(8,128)(2,1)S(1)}, bf16[256,512]{1,0:T(8,128)(2,1)}, u32[]{:S(2)}) copy-start(bf16[256,512]{1,0:T(8,128)(2,1)} %get-tuple-element.40.v_h.v_r) | copy-start | bytes 786436
  46.4 4.5 %copy-start.10 = (bf16[16,48,128]{2,1,0:T(8,128)(2,1)S(1)}, bf16[16,48,128]{2,1,0:T(8,128)(2,1)}, u32[]{:S(2)}) copy-start(bf16[16,48,128]{2,1,0:T(8,128)(2,1)} %get-tuple-element.41.start) | copy-start | bytes 589828
  47.0 3.9 %collective-permute-start.7 = (bf16[256,256]{1,0:T(8,128)(2,1)S(1)}, bf16[256,256]{1,0:T(8,128)(2,1)S(1)}, u32[]{:S(2)}, u32[]{:S(2)}) collective-permute-start(bf16[256,256]{1,0:T(8,128)(2,1)S(1)} %get-tuple-element.39), channel_id=1, source_target_pairs={{0,32},{32,0},{64,96},{96,64},{128,160},{160,128},{192,224},{224,1... | collective-permute-start | bytes 393224 | tf_op jit(solution)/shard_map/ppermute | solution.py:366
  51.6 0.7 copy-start.9
  52.3 29.8 %copy-start = (bf16[2048,256]{1,0:T(8,128)(2,1)}, bf16[2048,256]{1,0:T(8,128)(2,1)S(1)}, u32[]{:S(2)}) copy-start(bf16[2048,256]{1,0:T(8,128)(2,1)S(1)} %get-tuple-element.51.w) | copy-start | bytes 3145732
  52.3 24.2 %collective-permute-start.8 = (bf16[2048,256]{1,0:T(8,128)(2,1)S(1)}, bf16[2048,256]{1,0:T(8,128)(2,1)S(1)}, u32[]{:S(2)}, u32[]{:S(2)}) collective-permute-start(bf16[2048,256]{1,0:T(8,128)(2,1)S(1)} %get-tuple-element.51.w), channel_id=1, source_target_pairs={{0,32},{32,0},{64,96},{96,64},{128,160},{160,128},{192,224},{224,1... | collective-permute-start | bytes 3145736 | tf_op jit(solution)/shard_map/ppermute | solution.py:366
  65.7 10.8 %all-to-all-start.3 = ((bf16[16,64,128]{2,1,0:T(8,128)(2,1)}), bf16[16,64,128]{2,1,0:T(8,128)(2,1)S(1)}, u32[]{:S(2)}, u32[]{:S(2)}) async-start(bf16[16,64,128]{2,1,0:T(8,128)(2,1)} %scan.1), calls=%async_computation.3 | async-start | bytes 524288 | tf_op jit(solution)/shard_map/all_to_all | solution.py:370
  76.5 0.7 copy-start.16
  76.5 1.1 copy-start.15
  82.1 12.0 %collective-permute-start.12 = (bf16[256,256]{1,0:T(8,128)(2,1)}, bf16[256,256]{1,0:T(8,128)(2,1)S(1)}, u32[]{:S(2)}, u32[]{:S(2)}) collective-permute-start(bf16[256,256]{1,0:T(8,128)(2,1)} %get-tuple-element.53.kd_far), channel_id=1, source_target_pairs={{0,32},{32,0},{64,96},{96,64},{128,160},{160,128},{192,224},{224,1... | collective-permute-start | bytes 393224 | tf_op jit(solution)/shard_map/ppermute | solution.py:366
  83.7 7.3 %collective-permute-start.10 = (f32[256,16]{1,0:T(8,128)}, f32[256,16]{1,0:T(8,128)S(1)}, u32[]{:S(2)}, u32[]{:S(2)}) collective-permute-start(f32[256,16]{1,0:T(8,128)} %get-tuple-element.56.lat_a), channel_id=1, source_target_pairs={{0,1},{1,0},{2,3},{3,2},{4,5},{5,4},{6,7},{7,6},{8,9},{9,8},{10,11... | collective-permute-start | bytes 49160 | tf_op jit(solution)/shard_map/ppermute | solution.py:362
  91.0 0.9 copy-start.11
  91.9 0.8 copy-start.14
  92.9 0.6 copy-start.12
  93.5 0.6 copy-start.13
  94.1 0.7 copy-start.27
  98.6 30.0 %all-to-all-start.4 = ((bf16[16,112,512]{2,1,0:T(8,128)(2,1)}), bf16[16,112,512]{2,1,0:T(8,128)(2,1)S(1)}, u32[]{:S(2)}, u32[]{:S(2)}) async-start(bf16[16,112,512]{2,1,0:T(8,128)(2,1)} %weights.1), calls=%async_computation.4 | async-start | bytes 3670016 | tf_op jit(solution)/shard_map/all_to_all | solution.py:370
  106.1 27.1 %copy-start.28 = (bf16[128,512]{1,0:T(8,128)(2,1)S(1)}, bf16[128,512]{1,0:T(8,128)(2,1)}, u32[]{:S(2)}) copy-start(bf16[128,512]{1,0:T(8,128)(2,1)} %get-tuple-element.60) | copy-start | bytes 393220
  106.1 30.2 %copy-start.26 = (bf16[128,512]{1,0:T(8,128)(2,1)S(1)}, bf16[128,512]{1,0:T(8,128)(2,1)}, u32[]{:S(2)}) copy-start(bf16[128,512]{1,0:T(8,128)(2,1)} %get-tuple-element.59) | copy-start | bytes 393220
  106.1 31.0 %collective-permute-start.9 = (f32[128,2048]{1,0:T(8,128)}, f32[128,2048]{1,0:T(8,128)S(1)}, u32[]{:S(2)}, u32[]{:S(2)}) collective-permute-start(f32[128,2048]{1,0:T(8,128)} %get-tuple-element.55), channel_id=1, source_target_pairs={{0,1},{1,0},{2,3},{3,2},{4,5},{5,4},{6,7},{7,6},{8,9},{9,8},{10,11... | collective-permute-start | bytes 3145736 | tf_op jit(solution)/shard_map/ppermute | solution.py:362
  129.7 19.1 %all-to-all-start.5 = ((bf16[8,64,512]{2,1,0:T(8,128)(2,1)}), bf16[8,64,512]{2,1,0:T(8,128)(2,1)S(1)}, u32[]{:S(2)}, u32[]{:S(2)}) async-start(bf16[8,64,512]{2,1,0:T(8,128)(2,1)} %plane.1), calls=%async_computation.5 | async-start | bytes 1048576 | tf_op jit(solution)/shard_map/all_to_all | solution.py:370
  133.2 3.1 %collective-permute-start.11 = (bf16[128,512]{1,0:T(8,128)(2,1)S(1)}, bf16[128,512]{1,0:T(8,128)(2,1)S(1)}, u32[]{:S(2)}, u32[]{:S(2)}) collective-permute-start(bf16[128,512]{1,0:T(8,128)(2,1)S(1)} %copy-done.28), channel_id=1, source_target_pairs={{0,1},{1,0},{2,3},{3,2},{4,5},{5,4},{6,7},{7,6},{8,9},{9,8},{10,11... | collective-permute-start | bytes 393224 | tf_op jit(solution)/shard_map/ppermute | solution.py:362
  137.1 1.0 copy-start.17
  148.8 1.0 copy-start.4
  149.9 3.8 %collective-permute-start.13 = (f32[56,512]{1,0:T(8,128)S(1)}, f32[56,512]{1,0:T(8,128)S(1)}, u32[]{:S(2)}, u32[]{:S(2)}) collective-permute-start(f32[56,512]{1,0:T(8,128)S(1)} %get-tuple-element.63), channel_id=1, source_target_pairs={{0,1},{1,0},{2,3},{3,2},{4,5},{5,4},{6,7},{7,6},{8,9},{9,8},{10,11... | collective-permute-start | bytes 344072 | tf_op jit(solution)/shard_map/ppermute | solution.py:362

commit v5 on v4

--- a/solution.py
+++ b/solution.py
@@ -31,7 +31,7 @@
 
 
 BIG = 56
-KEYS = 16
+FAR = 16
 
 
 VM = pl.BlockSpec(memory_space=pltpu.VMEM)
@@ -239,7 +239,7 @@
 
 
 def gate_body(recv, adds, key_r, v_r, beta, q_r, g_r, kd_in, local, logit, lat, up, _,
-              kd_o, kd_keep, kd_give, gate_o, gate_keep, gate_give, up_part, lat_part, delta):
+              kd_keep, kd_give, gate_keep, gate_give, up_part, lat_part, delta, kd_o, gate_o):
     first = is_first()
     high = low_mask()[1].astype(BF16)
     back = [jnp.concatenate([recv[h * PER + i, :ROWS] for i in range(PER)], axis=0).astype(F32)
@@ -284,22 +284,18 @@
     lat_part[...] = dot(gate, up_half, NT)
 
 
-SMALL = 3 * RANK
-
-
-def down_body(lat_a, lat_b, tok, up_part, lat_o, both):
+SMALL = WIDTH + MODEL // 2
+
+
+def weight_body(lat_a, lat_b, up_part, tok, kd_r, far, far_peer, far_kd, lat_o, send):
     first = is_first()
     latent = (lat_a[...] + lat_b[...]).astype(BF16)
     lat_o[...] = pick(first, latent[:TOK], latent[TOK:])
     half = MODEL // 2
     down = dot(latent, pick(first, tok[:, :half], tok[:, half:]), TN)
-    both[...] = jnp.concatenate(
-        [up_part[...], down[:, :WIDTH], down[:, WIDTH:]], axis=0
-    ).astype(BF16)
-
-
-def weight_body(tok, kd_r, far, far_peer, far_kd, small, send):
-    first = is_first()
+    small = jnp.concatenate([up_part[...], down], axis=1).astype(BF16)
+    for p in range(PS):
+        send[p, :, :SMALL] = small
     kd, kd_far = kd_r[...], far_kd[...]
     kd_a = pick(first, kd_far[:TOK], kd_far[TOK:])
     kd_b = pick(first, kd_far[TOK:], kd_far[:TOK])
@@ -308,12 +304,9 @@
         block = dot(tok[:, cols], kd, TN)
         block = block + dot(far[:, cols], kd_a, TN) + dot(far_peer[:, cols], kd_b, TN)
         block = block.astype(BF16)
-        at, lane = SMALL + (z % 4) * 16, (z // 4) * QUART
+        lanes = slice(SMALL + z * QUART, SMALL + (z + 1) * QUART)
         for p in range(PS):
-            send[p, at : at + 16, lane : lane + QUART] = block[p * 16 : p * 16 + 16]
-    few = small[...]
-    for p in range(PS):
-        send[p, :SMALL] = few
+            send[p, :, lanes] = block[p * 16 : p * 16 + 16]
 
 
 def through_body(kd, kd_far, w, w_far, keep, give):
@@ -323,8 +316,12 @@
     keep[...] = pick(first, total[:TOK], total[TOK:])
 
 
-def input_body(keep, got, lat, down, out):
+def input_body(keep, got, lat, down, gate_m, gate_p, out, gate, flag):
+    first = is_first()
     out[...] = (keep[...] + got[...] + dot(lat[...], down[...])).astype(BF16)
+    gate[:, :WIDTH] = pick(first, gate_m[...], gate_p[...])
+    gate[:, WIDTH:] = pick(first, gate_p[...], gate_m[...])
+    flag[...] = jnp.zeros_like(flag)
 
 
 PER = DK // ROWS
@@ -333,29 +330,31 @@
 def plane_body(recv, send):
     total = jnp.sum(recv[...].astype(F32), axis=0).astype(BF16)
     for z in range(ZS):
-        at, lane = SMALL + (z % 4) * 16, (z // 4) * QUART
-        send[z, :SMALL] = total[:SMALL]
-        send[z, SMALL:, :QUART] = total[at : at + 16, lane : lane + QUART]
-        send[z, SMALL:, QUART:] = jnp.zeros((16, QUART), BF16)
-
-
-def total_body(recv, a, b, keep, give):
-    first = is_first()
-    small = jnp.sum(recv[:, :SMALL].astype(F32), axis=0)
-    parts = [recv[z, SMALL:, :QUART].astype(F32) for z in range(ZS)]
-    rows = jnp.concatenate([sum(parts[0::2]), sum(parts[1::2])], axis=1)
-    keep[...] = jnp.concatenate([small, pick(first, rows[:8], rows[8:])], axis=0)
-    give[...] = jnp.concatenate([small, pick(first, rows[8:], rows[:8])], axis=0)
+        send[z, :, :SMALL] = total[:, :SMALL]
+        send[z, :, SMALL:] = total[:, SMALL + z * QUART : SMALL + (z + 1) * QUART]
+
+
+def total_body(recv, _, keep, give):
+    first = is_first()
+    parts = [recv[z].astype(F32) for z in range(ZS)]
+    even, odd = sum(parts[0::2]), sum(parts[1::2])
+    small = even[:, :SMALL] + odd[:, :SMALL]
+    rows = jnp.concatenate([even[:, SMALL:], odd[:, SMALL:]], axis=1)
+    keep[:, :SMALL] = small
+    give[:, :SMALL] = small
+    pad = jnp.zeros((8, WIDTH), F32)
+    keep[:, SMALL:] = jnp.concatenate([pick(first, rows[:8], rows[8:]), pad], axis=0)
+    give[:, SMALL:] = jnp.concatenate([pick(first, rows[8:], rows[:8]), pad], axis=0)
 
 
 def out_body(mine, theirs, down_o, up_o, w_o):
     first = is_first()
     halves = (pick(first, mine[...], theirs[...]), pick(first, theirs[...], mine[...]))
+    wide = MODEL // 2
     for i, a in enumerate(halves):
-        up_o[:, i * WIDTH : (i + 1) * WIDTH] = a[:RANK]
-        down_o[:, 2 * i * WIDTH : (2 * i + 1) * WIDTH] = a[RANK : 2 * RANK]
-        down_o[:, (2 * i + 1) * WIDTH : (2 * i + 2) * WIDTH] = a[2 * RANK : 3 * RANK]
-        w_o[:, i * WIDTH : (i + 1) * WIDTH] = a[3 * RANK :]
+        up_o[:, i * WIDTH : (i + 1) * WIDTH] = a[:, :WIDTH]
+        down_o[:, i * wide : (i + 1) * wide] = a[:, WIDTH:SMALL]
+        w_o[:, i * WIDTH : (i + 1) * WIDTH] = a[:8, SMALL:]
 
 
 def swap(a):
@@ -379,12 +378,10 @@
     packed = shape((PS, ROWS + 16, DK), BF16)
     quarter = shape((PAIR, QUART), BF16)
 
-    lo, hi = key_weight[:, :WIDTH], key_weight[:, WIDTH:]
-    w_m, w_p = jnp.where(first, lo, hi), swap(jnp.where(first, hi, lo))
-    w_chip = jnp.concatenate([jnp.where(first, w_m, w_p), jnp.where(first, w_p, w_m)], axis=0)
-    w_two = jnp.stack([w_chip[:, :QUART], w_chip[:, QUART:]])
-    w_z = jnp.broadcast_to(w_two[None], (ZS // 2, 2, 16, QUART)).reshape(ZS, 16, QUART)
-    w_z = a2a(w_z, "z").reshape(ZS * 16, QUART)
+
+    w_z = key_weight.reshape(1, 8, 2, 2, QUART).transpose(0, 3, 2, 1, 4)
+    w_z = jnp.broadcast_to(w_z, (ZS // 2, 2, 2, 8, QUART))
+    w_z = a2a(w_z.reshape(2 * ZS, 8, QUART), ("z", "c")).reshape(ZS * 16, QUART)
     w_all = a2a(jnp.broadcast_to(w_z[None], (PS, ZS * 16, QUART)), XY)
 
     tok, lat, logit, beta, q, g, v, add_g, start = kernel(
@@ -397,10 +394,10 @@
     far_peer = swap(far)
     tok_sems = pltpu.SemaphoreType.DMA((2,))
     keys_far, w = kernel(
-        far_keys_body, (quarter, shape((MODEL, QUART), BF16)), "far_keys", 16,
+        far_keys_body, (quarter, shape((MODEL, QUART), BF16)), "far_keys", FAR,
         specs=[VM, HBM, HBM, HBM], out_specs=(VM, VM),
         scratch=[pltpu.VMEM((TOK, MODEL), BF16)] * 2 + [tok_sems],
-    )(w_all, far, far_peer, beta)
+    )(w_all, far, far_peer, lat)
     keys_mine = kernel(near_keys_body, quarter, "near_keys", 16)(tok, w)
     keys, send, w = kernel(
         keys_body,
@@ -412,40 +409,32 @@
     recv = a2a(send, XY)
     kd_local, local_part = kernel(inner_body, (half_f, half_f), "inner", BIG)(q, g, v, keys, beta)
     recv = a2a(kernel(scan_body, shape((PS, 2 * ROWS, DK), BF16), "scan", 8)(recv), XY)
-    kd, kd_keep, kd_give, gate, gate_m, gate_x, up_part, lat_part = kernel(
+    kd_keep, kd_give, gate_m, gate_x, up_part, lat_part = kernel(
         gate_body,
-        (half_bf, quarter, quarter, half_bf, shape((TOK, WIDTH), BF16),
-         shape((TOK, WIDTH), BF16), shape((RANK, WIDTH)), shape((PAIR, RANK))),
-        "gate", BIG, scratch=[pltpu.VMEM((PAIR, WIDTH), F32)],
-        specs=[VM] * 12 + [HBM], out_specs=(VM,) * 8,
+        (quarter, quarter, shape((TOK, WIDTH), BF16), shape((TOK, WIDTH), BF16),
+         shape((RANK, WIDTH)), shape((PAIR, RANK))),
+        "gate", BIG, specs=[VM] * 12 + [HBM], out_specs=(VM,) * 6,
+        scratch=[pltpu.VMEM((PAIR, WIDTH), F32)] + [pltpu.VMEM((PAIR, WIDTH), BF16)] * 2,
     )(recv, add_g, keys, v, beta, q, g, kd_local, local_part, logit, lat, gate_up, w_far)
     far_kd = across(kd_give)
-    lat_own, small = kernel(
-        down_body, (shape((TOK, RANK), BF16), shape((SMALL, WIDTH), BF16)), "down", 8
-    )(lat_part, swap(lat_part), tok, up_part)
-    send = kernel(
-        weight_body, shape((PS, SMALL + ZS * 8, WIDTH), BF16), "weights", BIG
-    )(tok, kd_keep, far, far_peer, far_kd, small)
-    send = kernel(plane_body, shape((ZS, SMALL + 16, WIDTH), BF16), "plane", 8)(a2a(send, XY))
-    gate_p = swap(gate_x)
-    gate_grad = jnp.concatenate(
-        [jnp.where(first, gate_m, gate_p), jnp.where(first, gate_p, gate_m)], axis=1
-    )
+    lat_own, send = kernel(
+        weight_body, (shape((TOK, RANK), BF16), shape((PS, 16, SMALL + ZS * QUART), BF16)),
+        "weights", BIG,
+    )(lat_part, swap(lat_part), up_part, tok, kd_keep, far, far_peer, far_kd)
+    send = kernel(plane_body, shape((ZS, 16, SMALL + QUART), BF16), "plane", 8)(a2a(send, XY))
     mine, other = kernel(
         through_body, (shape((TOK, MODEL)), shape((TOK, MODEL))), "through", BIG
     )(kd_keep, kd_give, w, w_far)
-    input_grad = kernel(input_body, shape((TOK, MODEL), BF16), "input", BIG)(
-        mine, swap(other), lat_own, gate_down
-    )
-    end = shape((SMALL + 8, WIDTH))
-    keep, give = kernel(
-        total_body, (end, end), "total", 8, specs=[VM, HBM, HBM], out_specs=(VM, VM)
-    )(a2a(send, "z"), input_grad, gate_grad)
+    input_grad, gate_grad, flag = kernel(
+        input_body, (shape((TOK, MODEL), BF16), shape((TOK, 2 * WIDTH), BF16), shape((8, DK))),
+        "input", 16,
+    )(mine, swap(other), lat_own, gate_down, gate_m, swap(gate_x))
+    end = shape((16, SMALL + WIDTH))
+    keep, give = kernel(total_body, (end, end), "total", 8)(a2a(send, "z"), flag)
     down_grad, up_grad, key_weight_grad = kernel(
         out_body,
         (shape((RANK, MODEL)), shape((RANK, 2 * WIDTH)), shape((8, 2 * WIDTH))), "grads", 8,
     )(keep, swap(give))
-
     return (input_grad[None], gate_grad[None], key_weight_grad, down_grad, up_grad)
 
 

time: 155 us -> 146 us (0.942)
  waiting for transfers between devices: 49.5 us -> 43.6 us
  starting transfers between devices: 45.9 us -> 51.2 us
  local copies, waits for them, and re-layouts: 13.9 us -> 8.72 us
  other arithmetic: 2.32 us -> 0 us
    unnamed x58 -> x54, local copies, waits for them, and re-layouts: 12.2 us -> 6.17 us
    all_to_all x5, waiting for transfers between devices: 40 us -> 34.7 us  [a2a(): return lax.all_to_all(a, axis, 0, 0)]
    all_to_all x5, starting transfers between devices: 24.1 us -> 27.5 us  [a2a(): return lax.all_to_all(a, axis, 0, 0)]
    ppermute x10 -> x9, starting transfers between devices: 18.3 us -> 20.7 us  [swap(): return lax.ppermute(a, 'c', SWAP)]
    ppermute x10 -> x9, waiting for transfers between devices: 6.36 us -> 5.63 us  [swap(): return lax.ppermute(a, 'c', SWAP)]
    pallas_call x6 -> x5, Pallas kernels: 12.3 us -> 12 us  [the longest x1 4.51 us: local(): kernel(gate_body, (quarter, quarter, shape((TOK, WIDTH), BF16), shape((TO...]
  transfers between devices with their start and end apart: 19 -> 18, of which waited for: 13 -> 12; matrix products, arithmetic and copies ran while one was open for 1% -> 1% of each run, Pallas kernels for 12% -> 13%
where the time goes in v5:
time: 146 us; the launch traced here: 145 us
  starting transfers between devices  51.2 us (35%)
  waiting for transfers between devices  43.6 us (30%)
  Pallas kernels  29.2 us (20%)
  blocking collectives  11.1 us (8%)
  local copies, waits for them, and re-layouts  8.72 us (6%)
    all_to_all x5, waiting for transfers between devices, a2a(): return lax.all_to_all(a, axis, 0, 0)  34.7 us
    all_to_all x5, starting transfers between devices, a2a(): return lax.all_to_all(a, axis, 0, 0)  27.5 us
    ppermute x9, starting transfers between devices, swap(): return lax.ppermute(a, 'c', SWAP)  20.7 us
    all_to_all x1, blocking collectives, a2a(): return lax.all_to_all(a, axis, 0, 0)  11.1 us
    unnamed x54, local copies, waits for them, and re-layouts  6.17 us
    ppermute x9, waiting for transfers between devices, swap(): return lax.ppermute(a, 'c', SWAP)  5.63 us
    pallas_call x1, Pallas kernels, local(): kernel(gates_body, (shape((PAIR, MODEL), BF16), shape((PAIR, RANK), BF16)...  5.14 us
    pallas_call x1, Pallas kernels, local(): kernel(inner_body, (half_f, half_f), 'inner', BIG)(q, g, v, keys, beta)  5.13 us
  transfers between devices with their start and end apart: 18, of which 12 were waited for; matrix products, arithmetic and copies ran while one was open for 1% of the time, Pallas kernels for 13%

profile of v5, /device:TPU:1, one launch (start us, length us, event | category | flops | bytes accessed | tf_op | source)
XLA Modules:
  0.0 144.8 jit_solution(12770931915533825199)
XLA Ops:
  0.6 0.0 copy-start.16
  0.6 0.0 copy-start.18
  0.7 0.0 copy-start.20
  0.7 0.0 copy-start.19
  0.7 0.8 copy.14
  1.5 0.6 broadcast_in_dim.25
  2.1 10.0 %all-to-all-start = ((bf16[16,8,256]{2,1,0:T(8,128)(2,1)}), bf16[16,8,256]{2,1,0:T(8,128)(2,1)S(1)}, u32[]{:S(2)}, u32[]{:S(2)}) async-start(bf16[16,8,256]{2,1,0:T(8,128)(2,1)} %bitcast.8), calls=%async_computation | async-start | bytes 131072 | tf_op jit(solution)/shard_map/all_to_all | solution.py:369
  12.1 1.4 collective-permute-start.4
  13.5 6.7 %all-to-all-done = bf16[16,8,256]{2,1,0:T(8,128)(2,1)S(1)} async-done(((bf16[16,8,256]{2,1,0:T(8,128)(2,1)}), bf16[16,8,256]{2,1,0:T(8,128)(2,1)S(1)}, u32[]{:S(2)}, u32[]{:S(2)}) %all-to-all-start) | async-done | bytes 65568 | tf_op jit(solution)/shard_map/all_to_all | solution.py:369
  20.2 1.1 broadcast_in_dim.27
  21.2 6.8 %all-to-all-start.1 = ((bf16[16,128,256]{2,1,0:T(8,128)(2,1)}), bf16[16,128,256]{2,1,0:T(8,128)(2,1)S(1)}, u32[]{:S(2)}, u32[]{:S(2)}) async-start(bf16[16,128,256]{2,1,0:T(8,128)(2,1)} %broadcast_in_dim.27), calls=%async_computation.1 | async-start | bytes 2097152 | tf_op jit(solution)/shard_map/all_to_all | solution.py:369
  28.0 0.4 collective-permute-start
  28.4 0.2 collective-permute-start.5
  28.6 0.3 collective-permute-start.1
  28.9 0.2 collective-permute-start.3
  29.1 0.3 collective-permute-start.2
  29.4 1.7 %collective-permute-done.1.q_p = bf16[128,1024]{1,0:T(8,128)(2,1)S(1)} collective-permute-done((bf16[128,1024]{1,0:T(8,128)(2,1)S(1)}, bf16[128,1024]{1,0:T(8,128)(2,1)S(1)}, u32[]{:S(2)}, u32[]{:S(2)}) %collective-permute-start.1) | collective-permute-done | bytes 262176 | tf_op jit(solution)/shard_map/ppermute | solution.py:361
  31.1 0.4 collective-permute-done.3.v_p
  31.5 0.4 collective-permute-done.2.g_p
  31.9 0.3 copy-done.22
  32.2 0.4 copy-done.23
  32.6 0.2 copy-done.17
  32.8 5.1 %gates.1 = (bf16[256,2048]{1,0:T(8,128)(2,1)}, bf16[256,16]{1,0:T(8,128)(2,1)}, f32[256,512]{1,0:T(8,128)}, f32[256,512]{1,0:T(8,128)}, bf16[256,512]{1,0:T(8,12...) custom-call(bf16[128,2048]{1,0:T(8,128)(2,1)} %bitcast.15, ...), custom_call_target="tpu_custom_call" | custom-call | tf_op jit(solution)/shard_map/gates/pallas_call | solution.py:387
  37.9 0.0 copy-start.5
  37.9 0.8 copy-done.5
  38.7 6.3 %all-to-all-done.1.recv = bf16[16,128,256]{2,1,0:T(8,128)(2,1)S(1)} async-done(((bf16[16,128,256]{2,1,0:T(8,128)(2,1)}), bf16[16,128,256]{2,1,0:T(8,128)(2,1)S(1)}, u32[]{:S(2)}, u32[]{:S(2)}) %all-to-all-start.1) | async-done | bytes 1048608 | tf_op jit(solution)/shard_map/all_to_all | solution.py:369
  45.0 1.1 copy-done.6
  46.1 0.8 copy-done.9
  47.0 0.6 far_keys.1
  47.6 0.1 collective-permute-start.6
  47.7 0.4 near_keys.1.mine
  48.2 3.4 %collective-permute-done.6.theirs = bf16[256,256]{1,0:T(8,128)(2,1)S(1)} collective-permute-done((bf16[256,256]{1,0:T(8,128)(2,1)S(1)}, bf16[256,256]{1,0:T(8,128)(2,1)S(1)}, u32[]{:S(2)}, u32[]{:S(2)}) %collective-permute-start.6) | collective-permute-done | bytes 131104 | tf_op jit(solution)/shard_map/ppermute | solution.py:365
  51.5 0.6 keys.1
  52.2 0.7 copy-done.8
  52.9 0.0 collective-permute-start.7
  52.9 11.1 %all_to_all.30.recv = bf16[16,80,128]{2,1,0:T(8,128)(2,1)S(1)} all-to-all(bf16[16,80,128]{2,1,0:T(8,128)(2,1)S(1)} %get-tuple-element.46), channel_id=1, replica_groups=mesh['z'=8,'x'=4,'y'=4,'c'=2] {'x','y'}, dimensions={0} | all-to-all | bytes 655360 | tf_op jit(solution)/shard_map/all_to_all | solution.py:369
  64.0 0.8 scan.1
  64.8 3.5 %all-to-all-start.3 = ((bf16[16,64,128]{2,1,0:T(8,128)(2,1)}), bf16[16,64,128]{2,1,0:T(8,128)(2,1)S(1)}, u32[]{:S(2)}, u32[]{:S(2)}) async-start(bf16[16,64,128]{2,1,0:T(8,128)(2,1)} %scan.1), calls=%async_computation.3 | async-start | bytes 524288 | tf_op jit(solution)/shard_map/all_to_all | solution.py:369
  68.3 5.1 %inner.1 = (f32[256,512]{1,0:T(8,128)}, f32[256,512]{1,0:T(8,128)}) custom-call(bf16[256,512]{1,0:T(8,128)(2,1)} %get-tuple-element.49.q_r, bf16[256,512]{1,0:T(8,128)(2,1)} %get-tuple-element.50.g_r, bf16[256,512]{1,0:T(8,128)(2,1)} %get-tuple-element.44.v_h.v_r, bf16[256,512]{1,0:T(8,128)(2,1)} %copy-done.8, f32[256,512]{1,0:T(8,128)} %get-tuple-element.43.beta_h.beta), custom_call_target="tpu_custom_call" | custom-call | tf_op jit(solution)/shard_map/inner/pallas_call | solution.py:410
  73.5 2.2 %all-to-all-done.3.recv = bf16[16,64,128]{2,1,0:T(8,128)(2,1)S(1)} async-done(((bf16[16,64,128]{2,1,0:T(8,128)(2,1)}), bf16[16,64,128]{2,1,0:T(8,128)(2,1)S(1)}, u32[]{:S(2)}, u32[]{:S(2)}) %all-to-all-start.3) | async-done | bytes 262176 | tf_op jit(solution)/shard_map/all_to_all | solution.py:369
  75.6 0.7 copy-done.15
  76.3 0.4 copy-done.14
  76.7 4.5 %gate.1 = (bf16[256,256]{1,0:T(8,128)(2,1)}, bf16[256,256]{1,0:T(8,128)(2,1)}, bf16[128,512]{1,0:T(8,128)(2,1)}, bf16[128,512]{1,0:T(8,128)(2,1)}, f32[16,512]{1,0:T(8,128)}, /*index=5*/f32[256,16]{1,0:T(8,128)}) custom-call(bf16[16,64,128]{2,1,0:T(8,128)(2,1)} %copy-done.15, f32[4,512,128]{2,1,0:T(8,128)} %get-tuple-element.47.adds, ...), custom_call_target="tpu_custom_call" | custom-call | tf_op jit(solution)/shard_map/gate/pallas_call | solution.py:412
  81.2 1.5 %collective-permute-start.10 = (bf16[256,256]{1,0:T(8,128)(2,1)}, bf16[256,256]{1,0:T(8,128)(2,1)S(1)}, u32[]{:S(2)}, u32[]{:S(2)}) collective-permute-start(bf16[256,256]{1,0:T(8,128)(2,1)} %get-tuple-element.56.kd_far), channel_id=1, source_target_pairs={{0,32},{32,0},{64,96},{96,64},{128,160},{160,128},{192,224},{224,1... | collective-permute-start | bytes 393224 | tf_op jit(solution)/shard_map/ppermute | solution.py:365
  82.8 5.8 %collective-permute-start.9 = (f32[256,16]{1,0:T(8,128)}, f32[256,16]{1,0:T(8,128)S(1)}, u32[]{:S(2)}, u32[]{:S(2)}) collective-permute-start(f32[256,16]{1,0:T(8,128)} %get-tuple-element.59.lat_a), channel_id=1, source_target_pairs={{0,1},{1,0},{2,3},{3,2},{4,5},{5,4},{6,7},{7,6},{8,9},{9,8},{10,11... | collective-permute-start | bytes 49160 | tf_op jit(solution)/shard_map/ppermute | solution.py:361
  88.6 1.2 collective-permute-done.9.lat_b
  89.8 0.6 copy-done.25
  90.4 0.0 copy-done.24
  90.5 4.1 %weights.1 = (bf16[128,16]{1,0:T(8,128)(2,1)}, bf16[16,16,3584]{2,1,0:T(8,128)(2,1)}) custom-call(f32[256,16]{1,0:T(8,128)} %get-tuple-element.59.lat_a, f32[256,16]{1,0:T(8,128)} %copy-done.25, f32[16,512]{1,0:T(8,128)} %get-tuple-element.60.up_part, bf16[256,2048]{1,0:T(8,128)(2,1)} %get-tuple-element.39.tok, bf16[256,256]{1,0:T(8,128)(2,1)} %get-tuple-element.55.kd.kd_r, ...), custom_call_target="tpu_custom_call" | custom-call | tf_op jit(solution)/shard_map/weights/pallas_call | solution.py:420
  94.5 3.7 %all-to-all-start.4 = ((bf16[16,16,3584]{2,1,0:T(8,128)(2,1)}), bf16[16,16,3584]{2,1,0:T(8,128)(2,1)S(1)}, u32[]{:S(2)}, u32[]{:S(2)}) async-start(bf16[16,16,3584]{2,1,0:T(8,128)(2,1)} %get-tuple-element.66), calls=%async_computation.4 | async-start | bytes 3670016 | tf_op jit(solution)/shard_map/all_to_all | solution.py:369
  98.3 3.8 %through.1 = (f32[128,2048]{1,0:T(8,128)}, f32[128,2048]{1,0:T(8,128)}) custom-call(bf16[256,256]{1,0:T(8,128)(2,1)} %get-tuple-element.55.kd.kd_r, bf16[256,256]{1,0:T(8,128)(2,1)} %get-tuple-element.56.kd_far, bf16[2048,256]{1,0:T(8,128)(2,1)} %copy-done, bf16[2048,256]{1,0:T(8,128)(2,1)} %copy-done.14), custom_call_target="tpu_custom_call" | custom-call | tf_op jit(solution)/shard_map/through/pallas_call | solution.py:425
  102.1 0.0 copy-start.13
  102.1 2.5 %collective-permute-start.8 = (f32[128,2048]{1,0:T(8,128)}, f32[128,2048]{1,0:T(8,128)}, u32[]{:S(2)}, u32[]{:S(2)}) collective-permute-start(f32[128,2048]{1,0:T(8,128)} %get-tuple-element.58), channel_id=1, source_target_pairs={{0,1},{1,0},{2,3},{3,2},{4,5},{5,4},{6,7},{7,6},{8,9},{9,8},{10,11... | collective-permute-start | bytes 3145736 | tf_op jit(solution)/shard_map/ppermute | solution.py:361
  104.6 16.5 %all-to-all-done.4.recv = bf16[16,16,3584]{2,1,0:T(8,128)(2,1)S(1)} async-done(((bf16[16,16,3584]{2,1,0:T(8,128)(2,1)}), bf16[16,16,3584]{2,1,0:T(8,128)(2,1)S(1)}, u32[]{:S(2)}, u32[]{:S(2)}) %all-to-all-start.4) | async-done | bytes 1835040 | tf_op jit(solution)/shard_map/all_to_all | solution.py:369
  121.1 1.0 plane.1
  122.1 3.5 %all-to-all-start.5 = ((bf16[8,16,1792]{2,1,0:T(8,128)(2,1)}), bf16[8,16,1792]{2,1,0:T(8,128)(2,1)S(1)}, u32[]{:S(2)}, u32[]{:S(2)}) async-start(bf16[8,16,1792]{2,1,0:T(8,128)(2,1)} %plane.1), calls=%async_computation.5 | async-start | bytes 917504 | tf_op jit(solution)/shard_map/all_to_all | solution.py:369
  125.6 5.0 %collective-permute-start.11 = (bf16[128,512]{1,0:T(8,128)(2,1)S(1)}, bf16[128,512]{1,0:T(8,128)(2,1)S(1)}, u32[]{:S(2)}, u32[]{:S(2)}) collective-permute-start(bf16[128,512]{1,0:T(8,128)(2,1)S(1)} %copy-done.26), channel_id=1, source_target_pairs={{0,1},{1,0},{2,3},{3,2},{4,5},{5,4},{6,7},{7,6},{8,9},{9,8},{10,11... | collective-permute-start | bytes 393224 | tf_op jit(solution)/shard_map/ppermute | solution.py:361
  130.5 1.0 collective-permute-done.11.gate_p
  131.5 2.3 %input.1 = (bf16[128,2048]{1,0:T(8,128)(2,1)}, bf16[128,1024]{1,0:T(8,128)(2,1)}, f32[8,128]{1,0:T(8,128)S(1)}) custom-call(f32[128,2048]{1,0:T(8,128)S(1)} %copy-done.7, f32[128,2048]{1,0:T(8,128)} %collective-permute-done.8.got, bf16[128,16]{1,0:T(8,128)(2,1)S(1)} %copy-done.13, bf16[16,2048]{1,0:T(8,128)(2,1)S(1)} %copy-done.10, ...), custom_call_target="tpu_custom_call" | custom-call | tf_op jit(solution)/shard_map/input/pallas_call | solution.py:428
  133.9 3.1 %all-to-all-done.5.recv = bf16[8,16,1792]{2,1,0:T(8,128)(2,1)S(1)} async-done(((bf16[8,16,1792]{2,1,0:T(8,128)(2,1)}), bf16[8,16,1792]{2,1,0:T(8,128)(2,1)S(1)}, u32[]{:S(2)}, u32[]{:S(2)}) %all-to-all-start.5) | async-done | bytes 458784 | tf_op jit(solution)/shard_map/all_to_all | solution.py:369
  137.0 0.1 total.1
  137.0 6.1 %collective-permute-start.12 = (f32[16,2048]{1,0:T(8,128)S(1)}, f32[16,2048]{1,0:T(8,128)S(1)}, u32[]{:S(2)}, u32[]{:S(2)}) collective-permute-start(f32[16,2048]{1,0:T(8,128)S(1)} %get-tuple-element.69), channel_id=1, source_target_pairs={{0,1},{1,0},{2,3},{3,2},{4,5},{5,4},{6,7},{7,6},{8,9},{9,8},{10,11... | collective-permute-start | bytes 393224 | tf_op jit(solution)/shard_map/ppermute | solution.py:361
  143.1 1.0 collective-permute-done.12.theirs
  144.1 0.7 grads.1
  (43 shorter events, 0.1 us)
Async XLA Ops:
  0.6 27.4 %copy-start.16 = (bf16[1,128,2048]{2,1,0:T(8,128)(2,1)S(1)}, bf16[1,128,2048]{2,1,0:T(8,128)(2,1)}, u32[]{:S(2)}) copy-start(bf16[1,128,2048]{2,1,0:T(8,128)(2,1)} %param.8) | copy-start | bytes 1572868
  0.6 28.0 %copy-start.18 = (bf16[1,128,1024]{2,1,0:T(8,128)(2,1)S(1)}, bf16[1,128,1024]{2,1,0:T(8,128)(2,1)}, u32[]{:S(2)}) copy-start(bf16[1,128,1024]{2,1,0:T(8,128)(2,1)} %param.9) | copy-start | bytes 786436
  0.7 28.3 %copy-start.20 = (bf16[1,128,1024]{2,1,0:T(8,128)(2,1)S(1)}, bf16[1,128,1024]{2,1,0:T(8,128)(2,1)}, u32[]{:S(2)}) copy-start(bf16[1,128,1024]{2,1,0:T(8,128)(2,1)} %param.10) | copy-start | bytes 786436
  0.7 28.5 %copy-start.19 = (bf16[1,128,1024]{2,1,0:T(8,128)(2,1)S(1)}, bf16[1,128,1024]{2,1,0:T(8,128)(2,1)}, u32[]{:S(2)}) copy-start(bf16[1,128,1024]{2,1,0:T(8,128)(2,1)} %param.11) | copy-start | bytes 786436
  2.1 18.0 %all-to-all-start = ((bf16[16,8,256]{2,1,0:T(8,128)(2,1)}), bf16[16,8,256]{2,1,0:T(8,128)(2,1)S(1)}, u32[]{:S(2)}, u32[]{:S(2)}) async-start(bf16[16,8,256]{2,1,0:T(8,128)(2,1)} %bitcast.8), calls=%async_computation | async-start | bytes 131072 | tf_op jit(solution)/shard_map/all_to_all | solution.py:369
  12.1 16.3 %collective-permute-start.4 = (bf16[128,2048]{1,0:T(8,128)(2,1)}, bf16[128,2048]{1,0:T(8,128)(2,1)S(1)}, u32[]{:S(2)}, u32[]{:S(2)}) collective-permute-start(bf16[128,2048]{1,0:T(8,128)(2,1)} %bitcast.14), channel_id=1, source_target_pairs={{0,32},{32,0},{64,96},{96,64},{128,160},{160,128},{192,224},{224,1... | collective-permute-start | bytes 1572872 | tf_op jit(solution)/shard_map/ppermute | solution.py:365
  21.2 23.7 %all-to-all-start.1 = ((bf16[16,128,256]{2,1,0:T(8,128)(2,1)}), bf16[16,128,256]{2,1,0:T(8,128)(2,1)S(1)}, u32[]{:S(2)}, u32[]{:S(2)}) async-start(bf16[16,128,256]{2,1,0:T(8,128)(2,1)} %broadcast_in_dim.27), calls=%async_computation.1 | async-start | bytes 2097152 | tf_op jit(solution)/shard_map/all_to_all | solution.py:369
  28.0 3.9 %collective-permute-start = (bf16[128,2048]{1,0:T(8,128)(2,1)S(1)}, bf16[128,2048]{1,0:T(8,128)(2,1)S(1)}, u32[]{:S(2)}, u32[]{:S(2)}) collective-permute-start(bf16[128,2048]{1,0:T(8,128)(2,1)S(1)} %bitcast.16), channel_id=1, source_target_pairs={{0,1},{1,0},{2,3},{3,2},{4,5},{5,4},{6,7},{7,6},{8,9},{9,8},{10,11... | collective-permute-start | bytes 1572872 | tf_op jit(solution)/shard_map/ppermute | solution.py:361
  28.4 19.2 %copy-start.4 = (bf16[128,2048]{1,0:T(8,128)(2,1)}, bf16[128,2048]{1,0:T(8,128)(2,1)S(1)}, u32[]{:S(2)}) copy-start(bf16[128,2048]{1,0:T(8,128)(2,1)S(1)} %collective-permute-done.4.far) | copy-start | bytes 1572868
  28.4 9.5 %collective-permute-start.5 = (bf16[128,2048]{1,0:T(8,128)(2,1)S(1)}, bf16[128,2048]{1,0:T(8,128)(2,1)S(1)}, u32[]{:S(2)}, u32[]{:S(2)}) collective-permute-start(bf16[128,2048]{1,0:T(8,128)(2,1)S(1)} %collective-permute-done.4.far), channel_id=1, source_target_pairs={{0,1},{1,0},{2,3},{3,2},{4,5},{5,4},{6,7},{7,6},{8,9},{9,8},{10,11... | collective-permute-start | bytes 1572872 | tf_op jit(solution)/shard_map/ppermute | solution.py:361
  28.6 2.5 %collective-permute-start.1 = (bf16[128,1024]{1,0:T(8,128)(2,1)S(1)}, bf16[128,1024]{1,0:T(8,128)(2,1)S(1)}, u32[]{:S(2)}, u32[]{:S(2)}) collective-permute-start(bf16[128,1024]{1,0:T(8,128)(2,1)S(1)} %bitcast.19), channel_id=1, source_target_pairs={{0,1},{1,0},{2,3},{3,2},{4,5},{5,4},{6,7},{7,6},{8,9},{9,8},{10,11... | collective-permute-start | bytes 786440 | tf_op jit(solution)/shard_map/ppermute | solution.py:361
  28.9 2.6 %collective-permute-start.3 = (bf16[128,1024]{1,0:T(8,128)(2,1)S(1)}, bf16[128,1024]{1,0:T(8,128)(2,1)S(1)}, u32[]{:S(2)}, u32[]{:S(2)}) collective-permute-start(bf16[128,1024]{1,0:T(8,128)(2,1)S(1)} %bitcast.23), channel_id=1, source_target_pairs={{0,1},{1,0},{2,3},{3,2},{4,5},{5,4},{6,7},{7,6},{8,9},{9,8},{10,11... | collective-permute-start | bytes 786440 | tf_op jit(solution)/shard_map/ppermute | solution.py:361
  29.1 2.7 %collective-permute-start.2 = (bf16[128,1024]{1,0:T(8,128)(2,1)S(1)}, bf16[128,1024]{1,0:T(8,128)(2,1)S(1)}, u32[]{:S(2)}, u32[]{:S(2)}) collective-permute-start(bf16[128,1024]{1,0:T(8,128)(2,1)S(1)} %bitcast.21), channel_id=1, source_target_pairs={{0,1},{1,0},{2,3},{3,2},{4,5},{5,4},{6,7},{7,6},{8,9},{9,8},{10,11... | collective-permute-start | bytes 786440 | tf_op jit(solution)/shard_map/ppermute | solution.py:361
  31.1 0.8 copy-start.21
  31.5 0.7 copy-start.22
  31.9 0.7 copy-start.23
  31.9 0.9 copy-start.17
  37.9 0.8 copy-start.5
  45.0 2.7 %copy-start.2 = (bf16[256,2048]{1,0:T(8,128)(2,1)S(1)}, bf16[256,2048]{1,0:T(8,128)(2,1)}, u32[]{:S(2)}) copy-start(bf16[256,2048]{1,0:T(8,128)(2,1)} %get-tuple-element.39.tok) | copy-start | bytes 3145732
  45.0 1.1 copy-start.6
  46.1 0.8 copy-start.9
  47.0 4.5 %copy-start.1 = (f32[256,512]{1,0:T(8,128)S(1)}, f32[256,512]{1,0:T(8,128)}, u32[]{:S(2)}) copy-start(f32[256,512]{1,0:T(8,128)} %get-tuple-element.43.beta_h.beta) | copy-start | bytes 1572868
  47.0 4.5 %copy-start.3 = (bf16[256,512]{1,0:T(8,128)(2,1)S(1)}, bf16[256,512]{1,0:T(8,128)(2,1)}, u32[]{:S(2)}) copy-start(bf16[256,512]{1,0:T(8,128)(2,1)} %get-tuple-element.44.v_h.v_r) | copy-start | bytes 786436
  47.0 4.5 %copy-start.11 = (bf16[16,48,128]{2,1,0:T(8,128)(2,1)S(1)}, bf16[16,48,128]{2,1,0:T(8,128)(2,1)}, u32[]{:S(2)}) copy-start(bf16[16,48,128]{2,1,0:T(8,128)(2,1)} %get-tuple-element.45.start) | copy-start | bytes 589828
  47.6 3.9 %collective-permute-start.6 = (bf16[256,256]{1,0:T(8,128)(2,1)S(1)}, bf16[256,256]{1,0:T(8,128)(2,1)S(1)}, u32[]{:S(2)}, u32[]{:S(2)}) collective-permute-start(bf16[256,256]{1,0:T(8,128)(2,1)S(1)} %get-tuple-element.42), channel_id=1, source_target_pairs={{0,32},{32,0},{64,96},{96,64},{128,160},{160,128},{192,224},{224,1... | collective-permute-start | bytes 393224 | tf_op jit(solution)/shard_map/ppermute | solution.py:365
  52.1 0.7 copy-start.8
  52.9 28.4 %copy-start = (bf16[2048,256]{1,0:T(8,128)(2,1)}, bf16[2048,256]{1,0:T(8,128)(2,1)S(1)}, u32[]{:S(2)}) copy-start(bf16[2048,256]{1,0:T(8,128)(2,1)S(1)} %get-tuple-element.54.w) | copy-start | bytes 3145732
  52.9 22.8 %collective-permute-start.7 = (bf16[2048,256]{1,0:T(8,128)(2,1)S(1)}, bf16[2048,256]{1,0:T(8,128)(2,1)S(1)}, u32[]{:S(2)}, u32[]{:S(2)}) collective-permute-start(bf16[2048,256]{1,0:T(8,128)(2,1)S(1)} %get-tuple-element.54.w), channel_id=1, source_target_pairs={{0,32},{32,0},{64,96},{96,64},{128,160},{160,128},{192,224},{224,1... | collective-permute-start | bytes 3145736 | tf_op jit(solution)/shard_map/ppermute | solution.py:365
  64.8 10.8 %all-to-all-start.3 = ((bf16[16,64,128]{2,1,0:T(8,128)(2,1)}), bf16[16,64,128]{2,1,0:T(8,128)(2,1)S(1)}, u32[]{:S(2)}, u32[]{:S(2)}) async-start(bf16[16,64,128]{2,1,0:T(8,128)(2,1)} %scan.1), calls=%async_computation.3 | async-start | bytes 524288 | tf_op jit(solution)/shard_map/all_to_all | solution.py:369
  75.6 0.7 copy-start.15
  75.6 1.1 copy-start.14
  81.2 8.6 %collective-permute-start.10 = (bf16[256,256]{1,0:T(8,128)(2,1)}, bf16[256,256]{1,0:T(8,128)(2,1)S(1)}, u32[]{:S(2)}, u32[]{:S(2)}) collective-permute-start(bf16[256,256]{1,0:T(8,128)(2,1)} %get-tuple-element.56.kd_far), channel_id=1, source_target_pairs={{0,32},{32,0},{64,96},{96,64},{128,160},{160,128},{192,224},{224,1... | collective-permute-start | bytes 393224 | tf_op jit(solution)/shard_map/ppermute | solution.py:365
  82.8 7.0 %collective-permute-start.9 = (f32[256,16]{1,0:T(8,128)}, f32[256,16]{1,0:T(8,128)S(1)}, u32[]{:S(2)}, u32[]{:S(2)}) collective-permute-start(f32[256,16]{1,0:T(8,128)} %get-tuple-element.59.lat_a), channel_id=1, source_target_pairs={{0,1},{1,0},{2,3},{3,2},{4,5},{5,4},{6,7},{7,6},{8,9},{9,8},{10,11... | collective-permute-start | bytes 49160 | tf_op jit(solution)/shard_map/ppermute | solution.py:361
  89.8 0.7 copy-start.25
  89.8 0.7 copy-start.24
  94.5 26.5 %all-to-all-start.4 = ((bf16[16,16,3584]{2,1,0:T(8,128)(2,1)}), bf16[16,16,3584]{2,1,0:T(8,128)(2,1)S(1)}, u32[]{:S(2)}, u32[]{:S(2)}) async-start(bf16[16,16,3584]{2,1,0:T(8,128)(2,1)} %get-tuple-element.66), calls=%async_computation.4 | async-start | bytes 3670016 | tf_op jit(solution)/shard_map/all_to_all | solution.py:369
  102.1 23.5 %copy-start.26 = (bf16[128,512]{1,0:T(8,128)(2,1)S(1)}, bf16[128,512]{1,0:T(8,128)(2,1)}, u32[]{:S(2)}) copy-start(bf16[128,512]{1,0:T(8,128)(2,1)} %get-tuple-element.63) | copy-start | bytes 393220
  102.1 29.5 %copy-start.7 = (f32[128,2048]{1,0:T(8,128)S(1)}, f32[128,2048]{1,0:T(8,128)}, u32[]{:S(2)}) copy-start(f32[128,2048]{1,0:T(8,128)} %get-tuple-element.57.keep) | copy-start | bytes 3145732
  102.1 29.5 %copy-start.10 = (bf16[16,2048]{1,0:T(8,128)(2,1)S(1)}, bf16[16,2048]{1,0:T(8,128)(2,1)}, u32[]{:S(2)}) copy-start(bf16[16,2048]{1,0:T(8,128)(2,1)} %down.3) | copy-start | bytes 196612
  102.1 29.5 %copy-start.12 = (bf16[128,512]{1,0:T(8,128)(2,1)S(1)}, bf16[128,512]{1,0:T(8,128)(2,1)}, u32[]{:S(2)}) copy-start(bf16[128,512]{1,0:T(8,128)(2,1)} %get-tuple-element.62.gate_m) | copy-start | bytes 393220
  102.1 29.5 %copy-start.13 = (bf16[128,16]{1,0:T(8,128)(2,1)S(1)}, bf16[128,16]{1,0:T(8,128)(2,1)}, u32[]{:S(2)}) copy-start(bf16[128,16]{1,0:T(8,128)(2,1)} %get-tuple-element.61.lat) | copy-start | bytes 12292
  102.1 29.4 %collective-permute-start.8 = (f32[128,2048]{1,0:T(8,128)}, f32[128,2048]{1,0:T(8,128)}, u32[]{:S(2)}, u32[]{:S(2)}) collective-permute-start(f32[128,2048]{1,0:T(8,128)} %get-tuple-element.58), channel_id=1, source_target_pairs={{0,1},{1,0},{2,3},{3,2},{4,5},{5,4},{6,7},{7,6},{8,9},{9,8},{10,11... | collective-permute-start | bytes 3145736 | tf_op jit(solution)/shard_map/ppermute | solution.py:361
  122.1 14.9 %all-to-all-start.5 = ((bf16[8,16,1792]{2,1,0:T(8,128)(2,1)}), bf16[8,16,1792]{2,1,0:T(8,128)(2,1)S(1)}, u32[]{:S(2)}, u32[]{:S(2)}) async-start(bf16[8,16,1792]{2,1,0:T(8,128)(2,1)} %plane.1), calls=%async_computation.5 | async-start | bytes 917504 | tf_op jit(solution)/shard_map/all_to_all | solution.py:369
  125.6 6.0 %collective-permute-start.11 = (bf16[128,512]{1,0:T(8,128)(2,1)S(1)}, bf16[128,512]{1,0:T(8,128)(2,1)S(1)}, u32[]{:S(2)}, u32[]{:S(2)}) collective-permute-start(bf16[128,512]{1,0:T(8,128)(2,1)S(1)} %copy-done.26), channel_id=1, source_target_pairs={{0,1},{1,0},{2,3},{3,2},{4,5},{5,4},{6,7},{7,6},{8,9},{9,8},{10,11... | collective-permute-start | bytes 393224 | tf_op jit(solution)/shard_map/ppermute | solution.py:361
  137.0 7.0 %collective-permute-start.12 = (f32[16,2048]{1,0:T(8,128)S(1)}, f32[16,2048]{1,0:T(8,128)S(1)}, u32[]{:S(2)}, u32[]{:S(2)}) collective-permute-start(f32[16,2048]{1,0:T(8,128)S(1)} %get-tuple-element.69), channel_id=1, source_target_pairs={{0,1},{1,0},{2,3},{3,2},{4,5},{5,4},{6,7},{7,6},{8,9},{9,8},{10,11... | collective-permute-start | bytes 393224 | tf_op jit(solution)/shard_map/ppermute | solution.py:361

commit v6 on v5

v6 whole, which is shorter than its diff:
```python
import jax
import jax.numpy as jnp
from jax import lax
from jax.experimental import pallas as pl
from jax.experimental.pallas import tpu as pltpu
from jax.sharding import Mesh, PartitionSpec as P

HEADS = 8
DK = 128
GROUP = 64
HALF = HEADS // 2
WIDTH = HALF * DK
QUART = WIDTH // 2
PER_SEQ = QUART // DK
TOK = 128
PAIR = 2 * TOK
QUAD = 2 * PAIR
BLOCKS = PAIR // GROUP
MODEL = 2048
WIDE = MODEL // 4
RANK = 16
ZS = 8
PS = 16
ROWS = HALF * DK // PS
F32 = jnp.float32
BF16 = jnp.bfloat16
XY = ("x", "y")
SWAP = ((0, 1), (1, 0))
MB = 1 << 20


def shape(dims, dtype=F32):
    return jax.ShapeDtypeStruct(dims, dtype)


BIG = 56


VM = pl.BlockSpec(memory_space=pltpu.VMEM)
HBM = pl.BlockSpec(memory_space=pltpu.HBM)


def kernel(body, outs, name, limit, scratch=(), specs=None, out_specs=None, alias=None):
    extra = {} if specs is None else {"in_specs": specs, "out_specs": out_specs}
    if alias:
        extra["input_output_aliases"] = alias
    return pl.pallas_call(
        body,
        out_shape=outs,
        name=name,
        scratch_shapes=scratch,
        compiler_params=pltpu.CompilerParams(vmem_limit_bytes=limit * MB),
        **extra,
    )


def split(a):
    hi = a.astype(BF16)
    return hi, (a - hi.astype(F32)).astype(BF16)


def dot(a, b, dims=((1,), (0,))):
    return lax.dot_general(a, b, (dims, ((), ())), preferred_element_type=F32)


NT = ((1,), (1,))
TN = ((0,), (0,))


def dot_hl(a, b, dims=((1,), (0,))):
    hi, lo = split(b)
    return dot(a, hi, dims) + dot(a, lo, dims)


def dot_ff(a, b, dims=((1,), (0,))):
    ah, al = split(a)
    bh, bl = split(b)
    return dot(ah, bh, dims) + dot(ah, bl, dims) + dot(al, bh, dims)


def dot_mask(mask, b):
    hi, lo = split(b)
    rest = (b - hi.astype(F32) - lo.astype(F32)).astype(BF16)
    return dot(mask, hi) + dot(mask, lo) + dot(mask, rest)


def is_first():
    return lax.axis_index("c") == 0


def pick(first, a, b):
    return jnp.where(first, a, b)


def low_mask():
    rows = lax.broadcasted_iota(jnp.int32, (GROUP, GROUP), 0)
    cols = lax.broadcasted_iota(jnp.int32, (GROUP, GROUP), 1)
    return rows >= cols, rows <= cols


def tok_of(n):
    return slice(n * GROUP, (n + 1) * GROUP)


def col_of(h):
    return slice(h * DK, (h + 1) * DK)


def span_of(beta, n):
    return beta[(n + 1) * GROUP - 1 : (n + 1) * GROUP]


def odd_z():
    return lax.rem(lax.axis_index("z"), 2) == 1


def quarter_of(ref, core, odd):
    lo = pick(odd, ref[:, QUART : 2 * QUART], ref[:, :QUART])
    hi = pick(odd, ref[:, 3 * QUART :], ref[:, 2 * QUART : 3 * QUART])
    return pick(core, lo, hi)


def prep_body(q, g, v, keep, to_c, to_z, to_cz):
    first, odd = is_first(), odd_z()
    other, even = jnp.logical_not(first), jnp.logical_not(odd)
    for i, ref in enumerate((q, g, v)):
        rows = slice(i * TOK, (i + 1) * TOK)
        keep[rows] = quarter_of(ref, first, odd)
        to_c[rows] = quarter_of(ref, other, odd)
        to_z[rows] = quarter_of(ref, first, even)
        to_cz[rows] = quarter_of(ref, other, even)


def rows_of(seq, n):
    at = seq * PAIR + n * GROUP
    return slice(at, at + GROUP)


def state_of(seq, h):
    return seq * PER_SEQ + h


def gates_body(own, peer, far, far_peer, down, up, bias, tok, lat, logit, beta):
    first, odd = is_first(), odd_z()
    tok[:TOK] = pick(first, own[...], peer[...])
    tok[TOK:PAIR] = pick(first, peer[...], own[...])
    tok[PAIR : PAIR + TOK] = pick(first, far[...], far_peer[...])
    tok[PAIR + TOK :] = pick(first, far_peer[...], far[...])
    latent = dot(tok[...], down[...], NT).astype(BF16)
    lat[...] = latent
    x = dot(latent, quarter_of(up, first, odd)) + quarter_of(bias, first, odd)
    logit[...] = x
    gamma = (jnp.minimum(x, 0.0) - jnp.log1p(jnp.exp(-jnp.abs(x)))) * (1.0 / 16.0)
    lower = low_mask()[0].astype(BF16)
    for n in range(QUAD // GROUP):
        beta[tok_of(n)] = dot_mask(lower, gamma[tok_of(n)])


def start_body(mine, from_c, from_z, from_cz, beta, q_o, g_o, v_o, adds, start):
    first = is_first()
    for i, out in enumerate((q_o, g_o, v_o)):
        rows = slice(i * TOK, (i + 1) * TOK)
        a, b, c, d = mine[rows], from_c[rows], from_z[rows], from_cz[rows]
        out[:TOK] = pick(first, a, b)
        out[TOK:PAIR] = pick(first, b, a)
        out[PAIR : PAIR + TOK] = pick(first, c, d)
        out[PAIR + TOK :] = pick(first, d, c)
    run = [jnp.zeros((DK, DK), F32)] * HALF
    decays = []
    for seq in range(2):
        total = jnp.zeros((1, QUART), F32)
        for n in reversed(range(BLOCKS)):
            r = rows_of(seq, n)
            b = beta[r]
            last = b[GROUP - 1 : GROUP]
            total = total + last
            decay = jnp.exp(last)
            scaled = q_o[r].astype(F32) * jnp.exp(b)
            grad = g_o[r]
            for h in range(PER_SEQ):
                s = state_of(seq, h)
                part = dot_hl(grad[:, col_of(h)], scaled[:, col_of(h)], TN)
                adds[n, col_of(s)] = part
                run[s] = decay[:, col_of(h)] * run[s] + part
        decays.append(jnp.exp(total))
    for p in range(PS):
        s, at = p // PER, (p % PER) * ROWS
        row = decays[s // PER_SEQ][:, col_of(s % PER_SEQ)]
        start[p, :ROWS] = run[s][at : at + ROWS].astype(BF16)
        top = row.astype(BF16).astype(F32)
        start[p, ROWS:] = jnp.concatenate(
            [jnp.broadcast_to(top, (8, DK)), jnp.broadcast_to(row - top, (8, DK))], axis=0
        ).astype(BF16)


def added_states(key, v, beta, seq, n):
    r = rows_of(seq, n)
    b = beta[r]
    last = b[GROUP - 1 : GROUP]
    tail = key[r].astype(F32) * jnp.exp(last - b)
    vals = v[r]
    return [dot_hl(vals[:, col_of(h)], tail[:, col_of(h)], TN) for h in range(PER_SEQ)], jnp.exp(last)


def load(pairs, sems):
    copies = [pltpu.make_async_copy(a, b, sems.at[i]) for i, (a, b) in enumerate(pairs)]
    for copy in copies:
        copy.start()
    return copies


def unpack(recv, w):
    for p in range(PS):
        for z in range(ZS):
            w[z * 256 + p * 16 : z * 256 + p * 16 + 16] = recv[p, z * 16 : z * 16 + 16]


def keys_body(recv_h, tok_h, beta_h, v_h, start_h, key_o, send, w_o,
              recv, tok, beta, v, start, w, sems):
    copies = load(
        ((recv_h, recv), (tok_h, tok), (beta_h, beta), (v_h, v), (start_h, start)), sems
    )
    copies[0].wait()
    unpack(recv, w)
    for copy in copies[1:]:
        copy.wait()
    key_o[...] = dot(tok[...], w[...]).astype(BF16)
    run = [jnp.zeros((DK, DK), F32)] * HALF
    for seq in range(2):
        for n in range(BLOCKS):
            parts, decay = added_states(key_o, v, beta, seq, n)
            for h in range(PER_SEQ):
                s = state_of(seq, h)
                run[s] = decay[:, col_of(h)] * run[s] + parts[h]
    for p in range(PS):
        s, at = p // PER, (p % PER) * ROWS
        send[p, : ROWS + 16] = start[p]
        send[p, ROWS + 16 :] = run[s][at : at + ROWS].astype(BF16)


def scan_body(recv, send):
    def decay(p):
        rows = recv[p, ROWS : ROWS + 16].astype(F32)
        return rows[:1] + rows[8:9]

    run = jnp.zeros((ROWS, DK), F32)
    for p in reversed(range(PS)):
        send[p, :ROWS] = run.astype(BF16)
        run = decay(p) * run + recv[p, :ROWS].astype(F32)
    run = jnp.zeros((ROWS, DK), F32)
    for p in range(PS):
        send[p, ROWS:] = run.astype(BF16)
        run = decay(p) * run + recv[p, ROWS + 16 :].astype(F32)


def inner_body(q_r, g_r, v_r, key_r, beta, kd_o, local):
    low, high = low_mask()
    for n in range(QUAD // GROUP):
        r = tok_of(n)
        b = beta[r]
        grow, shrink = jnp.exp(b), jnp.exp(-b)
        q = q_r[r].astype(F32)
        k = key_r[r].astype(F32)
        q_s, k_s = q * grow, k * shrink
        for h in range(PER_SEQ):
            c = col_of(h)
            g, v = g_r[r, c], v_r[r, c]
            pairs = jnp.where(low, dot(g, v, NT), 0.0)
            pairs_t = jnp.where(high, dot(v, g, NT), 0.0)
            kd = shrink[:, c] * dot_ff(pairs_t, q_s[:, c])
            qd = grow[:, c] * dot_ff(pairs, k_s[:, c])
            kd_o[r, c] = kd
            local[r, c] = q[:, c] * qd - k[:, c] * kd


def chip_rows(recv, at):
    return [
        jnp.concatenate([recv[s * PER + i, at : at + ROWS] for i in range(PER)], axis=0).astype(F32)
        for s in range(HALF)
    ]


def gate_body(recv, adds, key_r, v_r, beta, q_r, g_r, kd_in, local, logit, lat, up, _,
              kd_o, gate_o, up_part, lat_part, delta):
    first, odd = is_first(), odd_z()
    high = low_mask()[1].astype(BF16)
    back, run = chip_rows(recv, 0), chip_rows(recv, ROWS)
    grads = list(back)
    for seq in range(2):
        states = [state_of(seq, h) for h in range(PER_SEQ)]
        for n in reversed(range(BLOCKS)):
            r = rows_of(seq, n)
            b = beta[r]
            last = b[GROUP - 1 : GROUP]
            decay = jnp.exp(last)
            kd = jnp.concatenate(
                [dot_hl(v_r[r, col_of(h)], grads[s]) for h, s in enumerate(states)], axis=1
            ) * jnp.exp(last - b)
            kd_o[r] = (kd + kd_in[r]).astype(BF16)
            delta[r] = local[r] - key_r[r].astype(F32) * kd
            for h, s in enumerate(states):
                grads[s] = decay[:, col_of(h)] * grads[s] + adds[n, col_of(s)]
        for n in range(BLOCKS):
            r = rows_of(seq, n)
            parts, decay = added_states(key_r, v_r, beta, seq, n)
            qd = jnp.concatenate(
                [dot_hl(g_r[r, col_of(h)], run[s]) for h, s in enumerate(states)], axis=1
            ) * jnp.exp(beta[r])
            delta[r] += q_r[r].astype(F32) * qd
            for h, s in enumerate(states):
                run[s] = decay[:, col_of(h)] * run[s] + parts[h]
        beyond = jnp.concatenate(
            [jnp.sum(run[s] * back[s], axis=0, keepdims=True) for s in states], axis=1
        )
        for n in reversed(range(BLOCKS)):
            r = rows_of(seq, n)
            suffix = dot_mask(high, delta[r]) + beyond
            beyond = suffix[:1]
            x = logit[r]
            gate_o[r] = (suffix * (1.0 / (1.0 + jnp.exp(x))) * (1.0 / 16.0)).astype(BF16)
    gate = gate_o[...]
    up_part[...] = dot(lat[...], gate, TN)
    lat_part[...] = dot(quarter_of(up, first, odd), gate, NT)


SMALL = QUART + WIDE


def weight_body(lat_a, lat_c, lat_z, lat_cz, up_part, tok, kd_r, lat_o, send):
    first, odd = is_first(), odd_z()
    near = lat_a[...] + lat_c[...]
    far = lat_z[...] + lat_cz[...]
    latent = jnp.concatenate(
        [near[:, :PAIR] + far[:, PAIR:], near[:, PAIR:] + far[:, :PAIR]], axis=1
    ).astype(BF16)
    lat_o[...] = pick(first, latent[:, :TOK], latent[:, TOK:PAIR])
    lo = pick(odd, tok[:, WIDE : 2 * WIDE], tok[:, :WIDE])
    hi = pick(odd, tok[:, 3 * WIDE :], tok[:, 2 * WIDE : 3 * WIDE])
    down = dot(latent, pick(first, lo, hi))
    small = jnp.concatenate([up_part[...], down], axis=1).astype(BF16)
    for p in range(PS):
        send[p, :, :SMALL] = small
    kd = kd_r[...]
    for z in range(ZS):
        block = dot(tok[:, z * 256 : z * 256 + 256], kd, TN).astype(BF16)
        lanes = slice(SMALL + z * QUART, SMALL + (z + 1) * QUART)
        for p in range(PS):
            send[p, :, lanes] = block[p * 16 : p * 16 + 16]


def share_body(gate, keep, to_c, to_z, to_cz):
    first = is_first()
    keep[...] = pick(first, gate[:TOK], gate[TOK:PAIR])
    to_c[...] = pick(first, gate[TOK:PAIR], gate[:TOK])
    to_z[...] = pick(first, gate[PAIR : PAIR + TOK], gate[PAIR + TOK :])
    to_cz[...] = pick(first, gate[PAIR + TOK :], gate[PAIR : PAIR + TOK])


def through_body(kd, kd_far, w_all, far_all, keep, give, w, w_far):
    first = is_first()
    unpack(w_all, w)
    unpack(far_all, w_far)
    total = dot(kd[...], w[...], NT) + dot(kd_far[...], w_far[...], NT)
    give[...] = pick(first, total[TOK:], total[:TOK])
    keep[...] = pick(first, total[:TOK], total[TOK:])


def input_body(keep, got, lat, down, gate_m, gate_c, gate_z, gate_cz, out, gate, flag):
    first, odd = is_first(), odd_z()
    out[...] = (keep[...] + got[...] + dot(lat[...], down[...], TN)).astype(BF16)
    mine = jnp.concatenate(
        [pick(odd, gate_z[...], gate_m[...]), pick(odd, gate_m[...], gate_z[...])], axis=1
    )
    theirs = jnp.concatenate(
        [pick(odd, gate_cz[...], gate_c[...]), pick(odd, gate_c[...], gate_cz[...])], axis=1
    )
    gate[:, :WIDTH] = pick(first, mine, theirs)
    gate[:, WIDTH:] = pick(first, theirs, mine)
    flag[...] = jnp.zeros_like(flag)


PER = DK // ROWS


def plane_body(recv, _, send):
    total = jnp.sum(recv[...].astype(F32), axis=0).astype(BF16)
    for z in range(ZS):
        send[z, :, :SMALL] = total[:, :SMALL]
        send[z, :, SMALL:] = total[:, SMALL + z * QUART : SMALL + (z + 1) * QUART]


HALVES = WIDTH + MODEL // 2


def total_body(recv, keep, give):
    first = is_first()
    parts = [recv[z].astype(F32) for z in range(ZS)]
    even, odd = sum(parts[0::2]), sum(parts[1::2])
    small = jnp.concatenate(
        [even[:, :QUART], odd[:, :QUART], even[:, QUART:SMALL], odd[:, QUART:SMALL]], axis=1
    )
    rows = jnp.concatenate([even[:, SMALL:], odd[:, SMALL:]], axis=1)
    keep[:, :HALVES] = small
    give[:, :HALVES] = small
    pad = jnp.zeros((8, WIDTH), F32)
    keep[:, HALVES:] = jnp.concatenate([pick(first, rows[:8], rows[8:]), pad], axis=0)
    give[:, HALVES:] = jnp.concatenate([pick(first, rows[8:], rows[:8]), pad], axis=0)


def out_body(mine, theirs, down_o, up_o, w_o):
    first = is_first()
    halves = (pick(first, mine[...], theirs[...]), pick(first, theirs[...], mine[...]))
    wide = MODEL // 2
    for i, a in enumerate(halves):
        up_o[:, i * WIDTH : (i + 1) * WIDTH] = a[:, :WIDTH]
        down_o[:, i * wide : (i + 1) * wide] = a[:, WIDTH:HALVES]
        w_o[:, i * WIDTH : (i + 1) * WIDTH] = a[:8, HALVES:]


def swap(a):
    return lax.ppermute(a, "c", SWAP)


def cross(a):
    pairs = [(z * 2 + c, (z ^ 1) * 2 + (1 - c)) for z in range(ZS) for c in range(2)]
    return lax.ppermute(a, ("z", "c"), pairs)


def across(a):
    return lax.ppermute(a, "z", [(i, i ^ 1) for i in range(ZS)])


def a2a(a, axis):
    return lax.all_to_all(a, axis, 0, 0)


def local(inputs, queries, values, out_grad, key_weight, gate_down, gate_up, gate_bias):
    own = inputs[0]
    w_z = key_weight.reshape(1, 8, 2, 2, QUART).transpose(0, 3, 2, 1, 4)
    w_z = jnp.broadcast_to(w_z, (ZS // 2, 2, 2, 8, QUART))
    w_z = a2a(w_z.reshape(2 * ZS, 8, QUART), ("z", "c")).reshape(ZS * 16, QUART)
    w_all = a2a(jnp.broadcast_to(w_z[None], (PS, ZS * 16, QUART)), XY)

    third = shape((3 * TOK, QUART), BF16)
    mine, to_c, to_z, to_cz = kernel(prep_body, (third,) * 4, "prep", BIG)(
        queries[0], out_grad[0], values[0]
    )
    far = across(own)
    quad_bf = shape((QUAD, QUART), BF16)
    quad_f = shape((QUAD, QUART))
    tok, lat, logit, beta = kernel(
        gates_body,
        (shape((QUAD, MODEL), BF16), shape((QUAD, RANK), BF16), quad_f, quad_f), "gates", BIG,
    )(own, swap(own), far, swap(far), gate_down, gate_up, gate_bias[None])
    q, g, v, add_g, start = kernel(
        start_body,
        (quad_bf, quad_bf, quad_bf, shape((BLOCKS, WIDTH, DK)),
         shape((PS, ROWS + 16, DK), BF16)),
        "start", BIG,
    )(mine, swap(to_c), across(to_z), cross(to_cz), beta)
    keys, send, w_all = kernel(
        keys_body,
        (quad_bf, shape((PS, 2 * ROWS + 16, DK), BF16), shape((PS, ZS * 16, QUART), BF16)),
        "keys", BIG, specs=[HBM] * 5, out_specs=(VM, VM, HBM), alias={0: 2},
        scratch=[pltpu.VMEM((PS, ZS * 16, QUART), BF16), pltpu.VMEM((QUAD, MODEL), BF16),
                 pltpu.VMEM((QUAD, QUART), F32), pltpu.VMEM((QUAD, QUART), BF16),
                 pltpu.VMEM((PS, ROWS + 16, DK), BF16), pltpu.VMEM((MODEL, QUART), BF16),
                 pltpu.SemaphoreType.DMA((5,))],
    )(w_all, tok, beta, v, start)
    w_far = across(w_all)
    recv = a2a(send, XY)
    kd_local, local_part = kernel(inner_body, (quad_f, quad_f), "inner", BIG)(q, g, v, keys, beta)
    recv = a2a(kernel(scan_body, shape((PS, 2 * ROWS, DK), BF16), "scan", 8)(recv), XY)
    kd, gate, up_part, lat_part = kernel(
        gate_body,
        (quad_bf, quad_bf, shape((RANK, QUART)), shape((RANK, QUAD))),
        "gate", BIG, specs=[VM] * 12 + [HBM], out_specs=(VM,) * 4,
        scratch=[pltpu.VMEM((QUAD, QUART), F32)],
    )(recv, add_g, keys, v, beta, q, g, kd_local, local_part, logit, lat, gate_up, w_far)
    lat_own, send = kernel(
        weight_body, (shape((RANK, TOK), BF16), shape((PS, 16, SMALL + ZS * QUART), BF16)),
        "weights", BIG,
    )(lat_part, swap(lat_part), across(lat_part), cross(lat_part), up_part, tok, kd)
    keep, give = kernel(
        through_body, (shape((TOK, MODEL)), shape((TOK, MODEL))), "through", BIG,
        scratch=[pltpu.VMEM((MODEL, QUART), BF16)] * 2,
    )(kd[:PAIR], across(kd[PAIR:]), w_all, w_far)
    piece = shape((TOK, QUART), BF16)
    gate_m, gate_c, gate_z, gate_cz = kernel(share_body, (piece,) * 4, "share", 8)(gate)
    input_grad, gate_grad, flag = kernel(
        input_body, (shape((TOK, MODEL), BF16), shape((TOK, 2 * WIDTH), BF16), shape((8, DK))),
        "input", 16,
    )(keep, swap(give), lat_own, gate_down, gate_m, swap(gate_c), across(gate_z), cross(gate_cz))
    send = kernel(plane_body, shape((ZS, 16, SMALL + QUART), BF16), "plane", 8)(
        a2a(send, XY), flag
    )
    end = shape((16, HALVES + WIDTH))
    keep, give = kernel(total_body, (end, end), "total", 8)(a2a(send, "z"))
    down_grad, up_grad, key_weight_grad = kernel(
        out_body,
        (shape((RANK, MODEL)), shape((RANK, 2 * WIDTH)), shape((8, 2 * WIDTH))), "grads", 8,
    )(keep, swap(give))
    return (input_grad[None], gate_grad[None], key_weight_grad, down_grad, up_grad)


def solution(mesh):
    grid = Mesh(mesh.devices.reshape(8, 4, 4, 2), ("z", "x", "y", "c"))
    seq = ("x", "y", "c")
    tok = P("z", seq, None)
    row = P(("z",) + seq, None)
    return jax.shard_map(
        local,
        mesh=grid,
        in_specs=(tok, tok, tok, tok, row, P(), P(), P()),
        out_specs=(tok, tok, row, P(), P()),
        check_vma=False,
    )
```

time: 146 us -> 141 us (0.966)
  blocking collectives: 11.1 us -> 27.6 us
  waiting for transfers between devices: 43.6 us -> 27.7 us
  starting transfers between devices: 51.2 us -> 41.4 us
  Pallas kernels: 29.2 us -> 33.6 us
    all_to_all x5 -> x4, waiting for transfers between devices: 34.7 us -> 11.9 us  [a2a(): return lax.all_to_all(a, axis, 0, 0)]
    all_to_all x1 -> x2, blocking collectives: 11.1 us -> 27.6 us  [a2a(): return lax.all_to_all(a, axis, 0, 0)]
    ppermute x9 -> x7, starting transfers between devices: 20.7 us -> 6.11 us  [swap(): return lax.ppermute(a, 'c', SWAP)]
    ppermute x0 -> x3, waiting for transfers between devices: none -> 8.19 us  [cross(): return lax.ppermute(a, ('z', 'c'), pairs)]
    ppermute x0 -> x3, starting transfers between devices: none -> 7.17 us  [cross(): return lax.ppermute(a, ('z', 'c'), pairs)]
    pallas_call x8 -> x9, Pallas kernels: 20.6 us -> 27 us  [the longest x1 5.11 us: local(): kernel(inner_body, (quad_f, quad_f), 'inner', BIG)(q, g, v, keys, beta)]
    ppermute x9 -> x7, waiting for transfers between devices: 5.63 us -> 1 us  [swap(): return lax.ppermute(a, 'c', SWAP)]
    ppermute x4 -> x6, waiting for transfers between devices: 3.36 us -> 6.63 us  [across(): return lax.ppermute(a, 'z', [(i, i ^ 1) for i in range(ZS)])]
  transfers between devices with their start and end apart: 18 -> 20, of which waited for: 12 -> 10; matrix products, arithmetic and copies ran while one was open for 1% -> 1% of each run, Pallas kernels for 13% -> 14%
where the time goes in v6:
time: 141 us; the launch traced here: 140 us
  starting transfers between devices  41.4 us (29%)
  Pallas kernels  33.6 us (24%)
  waiting for transfers between devices  27.7 us (20%)
  blocking collectives  27.6 us (20%)
  local copies, waits for them, and re-layouts  9.3 us (7%)
    all_to_all x2, blocking collectives, a2a(): return lax.all_to_all(a, axis, 0, 0)  27.6 us
    all_to_all x4, starting transfers between devices, a2a(): return lax.all_to_all(a, axis, 0, 0)  24.6 us
    all_to_all x4, waiting for transfers between devices, a2a(): return lax.all_to_all(a, axis, 0, 0)  11.9 us
    ppermute x3, waiting for transfers between devices, cross(): return lax.ppermute(a, ('z', 'c'), pairs)  8.19 us
    ppermute x3, starting transfers between devices, cross(): return lax.ppermute(a, ('z', 'c'), pairs)  7.17 us
    ppermute x6, waiting for transfers between devices, across(): return lax.ppermute(a, 'z', [(i, i ^ 1) for i in range(ZS)])  6.63 us
    unnamed x38, local copies, waits for them, and re-layouts  6.19 us
    ppermute x7, starting transfers between devices, swap(): return lax.ppermute(a, 'c', SWAP)  6.11 us
  transfers between devices with their start and end apart: 20, of which 10 were waited for; matrix products, arithmetic and copies ran while one was open for 1% of the time, Pallas kernels for 14%

profile of v6, /device:TPU:1, one launch (start us, length us, event | category | flops | bytes accessed | tf_op | source)
XLA Modules:
  0.0 140.4 jit_solution(10841274245454821833)
XLA Ops:
  0.6 0.7 copy.14
  1.4 0.6 broadcast_in_dim.24
  2.0 10.0 %all-to-all-start = ((bf16[16,8,256]{2,1,0:T(8,128)(2,1)}), bf16[16,8,256]{2,1,0:T(8,128)(2,1)S(1)}, u32[]{:S(2)}, u32[]{:S(2)}) async-start(bf16[16,8,256]{2,1,0:T(8,128)(2,1)} %bitcast.3), calls=%async_computation | async-start | bytes 131072 | tf_op jit(solution)/shard_map/all_to_all | solution.py:434
  12.0 1.4 collective-permute-start.1
  13.4 6.7 %all-to-all-done = bf16[16,8,256]{2,1,0:T(8,128)(2,1)S(1)} async-done(((bf16[16,8,256]{2,1,0:T(8,128)(2,1)}), bf16[16,8,256]{2,1,0:T(8,128)(2,1)S(1)}, u32[]{:S(2)}, u32[]{:S(2)}) %all-to-all-start) | async-done | bytes 65568 | tf_op jit(solution)/shard_map/all_to_all | solution.py:434
  20.0 1.1 broadcast_in_dim.26
  21.1 6.8 %all-to-all-start.1 = ((bf16[16,128,256]{2,1,0:T(8,128)(2,1)}), bf16[16,128,256]{2,1,0:T(8,128)(2,1)S(1)}, u32[]{:S(2)}, u32[]{:S(2)}) async-start(bf16[16,128,256]{2,1,0:T(8,128)(2,1)} %broadcast_in_dim.26), calls=%async_computation.1 | async-start | bytes 2097152 | tf_op jit(solution)/shard_map/all_to_all | solution.py:434
  27.9 0.4 collective-permute-start
  28.2 0.0 collective-permute-done.1.far
  28.3 0.2 collective-permute-start.2
  28.5 2.0 %prep.1 = (bf16[384,256]{1,0:T(8,128)(2,1)}, bf16[384,256]{1,0:T(8,128)(2,1)}, bf16[384,256]{1,0:T(8,128)(2,1)}, bf16[384,256]{1,0:T(8,128)(2,1)}) custom-call(bf16[128,1024]{1,0:T(8,128)(2,1)} %bitcast.17, bf16[128,1024]{1,0:T(8,128)(2,1)} %bitcast.18, bf16[128,1024]{1,0:T(8,128)(2,1)} %bitcast.19), custom_call_target="tpu_custom_call" | custom-call | tf_op jit(solution)/shard_map/prep/pallas_call | solution.py:445
  30.5 0.3 collective-permute-start.3
  30.8 0.2 collective-permute-start.4
  31.0 1.6 %collective-permute-start.5 = (bf16[384,256]{1,0:T(8,128)(2,1)}, bf16[384,256]{1,0:T(8,128)(2,1)S(1)}, u32[]{:S(2)}, u32[]{:S(2)}) collective-permute-start(bf16[384,256]{1,0:T(8,128)(2,1)} %get-tuple-element.48), channel_id=1, source_target_pairs={{0,33},{1,32},{32,1},{33,0},{64,97},{65,96},{96,65},{97,64},{128,1... | collective-permute-start | bytes 589832 | tf_op jit(solution)/shard_map/ppermute | solution.py:426
  32.6 0.0 collective-permute-done.peer
  32.7 0.8 copy-done.10
  33.4 0.2 copy-done.11
  33.6 4.0 %gates.1 = (bf16[512,2048]{1,0:T(8,128)(2,1)}, bf16[512,16]{1,0:T(8,128)(2,1)}, f32[512,256]{1,0:T(8,128)}, f32[512,256]{1,0:T(8,128)}) custom-call(bf16[128,2048]{1,0:T(8,128)(2,1)} %bitcast.15, bf16[128,2048]{1,0:T(8,128)(2,1)} %copy-done.10, bf16[128,2048]{1,0:T(8,128)(2,1)} %copy-done.9, bf16[128,2048]{1,0:T(8,128)(2,1)} %copy-done.11, ...), custom_call_target="tpu_custom_call" | custom-call | tf_op jit(solution)/shard_map/gates/pallas_call | solution.py:451
  37.6 0.0 collective-permute-done.3.from_c
  37.6 0.0 collective-permute-done.4.from_z
  37.7 4.5 %collective-permute-done.5.from_cz = bf16[384,256]{1,0:T(8,128)(2,1)S(1)} collective-permute-done((bf16[384,256]{1,0:T(8,128)(2,1)}, bf16[384,256]{1,0:T(8,128)(2,1)S(1)}, u32[]{:S(2)}, u32[]{:S(2)}) %collective-permute-start.5) | collective-permute-done | bytes 196640 | tf_op jit(solution)/shard_map/ppermute | solution.py:426
  42.1 0.7 copy-done.14
  42.8 2.9 %start.1 = (bf16[512,256]{1,0:T(8,128)(2,1)}, bf16[512,256]{1,0:T(8,128)(2,1)}, bf16[512,256]{1,0:T(8,128)(2,1)}, f32[4,512,128]{2,1,0:T(8,128)}, bf16[16,48,128]{2,1,0:T(8,128)(2,1)}) custom-call(bf16[384,256]{1,0:T(8,128)(2,1)} %get-tuple-element.45.mine, bf16[384,256]{1,0:T(8,128)(2,1)} %copy-done.12, bf16[384,256]{1,0:T(8,128)(2,1)} %copy-done.13, ...), custom_call_target="tpu_custom_call" | custom-call | tf_op jit(solution)/shard_map/start/pallas_call | solution.py:455
  45.8 1.0 copy-done.4
  46.7 4.4 %keys.1 = (bf16[512,256]{1,0:T(8,128)(2,1)}, bf16[16,80,128]{2,1,0:T(8,128)(2,1)}, bf16[16,128,256]{2,1,0:T(8,128)(2,1)}) custom-call(bf16[16,128,256]{2,1,0:T(8,128)(2,1)} %copy-done.4, bf16[512,2048]{1,0:T(8,128)(2,1)} %get-tuple-element.43.tok_h.tok, f32[512,256]{1,0:T(8,128)} %get-tuple-element.44.beta.beta_h, ...), custom_call_target="tpu_custom_call", output_to_operand_aliasing={{2}: (0, {})} | custom-call | tf_op jit(solution)/shard_map/keys/pallas_call | solution.py:461
  51.2 0.3 collective-permute-start.6
  51.5 14.6 %all_to_all.30.recv = bf16[16,80,128]{2,1,0:T(8,128)(2,1)S(1)} all-to-all(bf16[16,80,128]{2,1,0:T(8,128)(2,1)} %get-tuple-element.51), channel_id=1, replica_groups=mesh['z'=8,'x'=4,'y'=4,'c'=2] {'x','y'}, dimensions={0} | all-to-all | bytes 655360 | tf_op jit(solution)/shard_map/all_to_all | solution.py:434
  66.1 0.8 scan.1
  66.9 4.0 %all-to-all-start.3 = ((bf16[16,64,128]{2,1,0:T(8,128)(2,1)}), bf16[16,64,128]{2,1,0:T(8,128)(2,1)S(1)}, u32[]{:S(2)}, u32[]{:S(2)}) async-start(bf16[16,64,128]{2,1,0:T(8,128)(2,1)} %scan.1), calls=%async_computation.3 | async-start | bytes 524288 | tf_op jit(solution)/shard_map/all_to_all | solution.py:434
  70.9 5.1 %inner.1 = (f32[512,256]{1,0:T(8,128)}, f32[512,256]{1,0:T(8,128)}) custom-call(bf16[512,256]{1,0:T(8,128)(2,1)} %get-tuple-element.54.q_r, bf16[512,256]{1,0:T(8,128)(2,1)} %get-tuple-element.55.g_r, bf16[512,256]{1,0:T(8,128)(2,1)} %get-tuple-element.49.v_h.v_r, bf16[512,256]{1,0:T(8,128)(2,1)} %get-tuple-element.53.key_r, ...), custom_call_target="tpu_custom_call" | custom-call | tf_op jit(solution)/shard_map/inner/pallas_call | solution.py:472
  76.0 2.2 %all-to-all-done.3.recv = bf16[16,64,128]{2,1,0:T(8,128)(2,1)S(1)} async-done(((bf16[16,64,128]{2,1,0:T(8,128)(2,1)}), bf16[16,64,128]{2,1,0:T(8,128)(2,1)S(1)}, u32[]{:S(2)}, u32[]{:S(2)}) %all-to-all-start.3) | async-done | bytes 262176 | tf_op jit(solution)/shard_map/all_to_all | solution.py:434
  78.2 0.0 collective-permute-done.6._.far_all
  78.2 0.7 copy-done.7
  78.9 0.4 copy-done.5
  79.3 4.7 %gate.1 = (bf16[512,256]{1,0:T(8,128)(2,1)}, bf16[512,256]{1,0:T(8,128)(2,1)}, f32[16,256]{1,0:T(8,128)}, f32[16,512]{1,0:T(8,128)}) custom-call(bf16[16,64,128]{2,1,0:T(8,128)(2,1)} %copy-done.7, f32[4,512,128]{2,1,0:T(8,128)} %get-tuple-element.52.adds, bf16[512,256]{1,0:T(8,128)(2,1)} %get-tuple-element.53.key_r, ...), custom_call_target="tpu_custom_call" | custom-call | tf_op jit(solution)/shard_map/gate/pallas_call | solution.py:474
  84.0 4.2 %collective-permute-start.11 = (f32[16,512]{1,0:T(8,128)}, f32[16,512]{1,0:T(8,128)S(1)}, u32[]{:S(2)}, u32[]{:S(2)}) collective-permute-start(f32[16,512]{1,0:T(8,128)} %get-tuple-element.64.lat_a), channel_id=1, source_target_pairs={{0,33},{1,32},{32,1},{33,0},{64,97},{65,96},{96,65},{97,64},{128,1... | collective-permute-start | bytes 98312 | tf_op jit(solution)/shard_map/ppermute | solution.py:426
  88.3 0.1 collective-permute-start.10
  88.3 0.4 collective-permute-start.9
  88.8 1.5 %collective-permute-done.11.lat_cz = f32[16,512]{1,0:T(8,128)S(1)} collective-permute-done((f32[16,512]{1,0:T(8,128)}, f32[16,512]{1,0:T(8,128)S(1)}, u32[]{:S(2)}, u32[]{:S(2)}) %collective-permute-start.11) | collective-permute-done | bytes 32800 | tf_op jit(solution)/shard_map/ppermute | solution.py:426
  90.2 1.0 collective-permute-done.10.lat_z
  91.2 0.0 collective-permute-done.9.lat_c
  91.3 0.6 copy-done.17
  91.9 0.0 copy-done.18
  91.9 3.6 %weights.1 = (bf16[16,128]{1,0:T(8,128)(2,1)}, bf16[16,16,2816]{2,1,0:T(8,128)(2,1)}) custom-call(f32[16,512]{1,0:T(8,128)} %get-tuple-element.64.lat_a, f32[16,512]{1,0:T(8,128)} %copy-done.18, f32[16,512]{1,0:T(8,128)} %copy-done.17, f32[16,512]{1,0:T(8,128)} %copy-done.16, f32[16,256]{1,0:T(8,128)} %get-tuple-element.65.up_part, ...), custom_call_target="tpu_custom_call" | custom-call | tf_op jit(solution)/shard_map/weights/pallas_call | solution.py:480
  95.5 3.8 %all-to-all-start.4 = ((bf16[16,16,2816]{2,1,0:T(8,128)(2,1)}), bf16[16,16,2816]{2,1,0:T(8,128)(2,1)S(1)}, u32[]{:S(2)}, u32[]{:S(2)}) async-start(bf16[16,16,2816]{2,1,0:T(8,128)(2,1)} %get-tuple-element.74), calls=%async_computation.4 | async-start | bytes 2883584 | tf_op jit(solution)/shard_map/all_to_all | solution.py:434
  99.4 0.7 fusion
  100.1 0.7 collective-permute-start.7
  100.8 4.2 %collective-permute-done.7.kd_far = bf16[256,256]{1,0:T(8,128)(2,1)S(1)} collective-permute-done((bf16[256,256]{1,0:T(8,128)(2,1)S(1)}, bf16[256,256]{1,0:T(8,128)(2,1)S(1)}, u32[]{:S(2)}, u32[]{:S(2)}) %collective-permute-start.7) | collective-permute-done | bytes 131104 | tf_op jit(solution)/shard_map/ppermute | solution.py:430
  105.0 0.7 copy-done.15
  105.7 3.8 %through.1 = (f32[128,2048]{1,0:T(8,128)}, f32[128,2048]{1,0:T(8,128)}) custom-call(bf16[256,256]{1,0:T(8,128)(2,1)} %get-tuple-element.82.kd, bf16[256,256]{1,0:T(8,128)(2,1)} %copy-done.15, bf16[16,128,256]{2,1,0:T(8,128)(2,1)} %get-tuple-element.60.w_all, bf16[16,128,256]{2,1,0:T(8,128)(2,1)} %copy-done.5), custom_call_target="tpu_custom_call" | custom-call | tf_op jit(solution)/shard_map/through/pallas_call | solution.py:484
  109.4 0.9 collective-permute-start.8
  110.4 0.1 collective-permute-start.12
  110.5 0.8 collective-permute-start.13
  111.3 1.3 collective-permute-start.14
  112.7 1.4 collective-permute-done.13.gate_z
  114.0 2.3 %collective-permute-done.14.gate_cz = bf16[128,256]{1,0:T(8,128)(2,1)S(1)} collective-permute-done((bf16[128,256]{1,0:T(8,128)(2,1)S(1)}, bf16[128,256]{1,0:T(8,128)(2,1)S(1)}, u32[]{:S(2)}, u32[]{:S(2)}) %collective-permute-start.14) | collective-permute-done | bytes 65568 | tf_op jit(solution)/shard_map/ppermute | solution.py:426
  116.3 1.2 copy-done
  117.5 1.2 input.1
  118.8 3.0 %all-to-all-done.4.recv = bf16[16,16,2816]{2,1,0:T(8,128)(2,1)S(1)} async-done(((bf16[16,16,2816]{2,1,0:T(8,128)(2,1)}), bf16[16,16,2816]{2,1,0:T(8,128)(2,1)S(1)}, u32[]{:S(2)}, u32[]{:S(2)}) %all-to-all-start.4) | async-done | bytes 1441824 | tf_op jit(solution)/shard_map/all_to_all | solution.py:434
  121.8 0.2 plane.1
  122.0 13.0 %all_to_all.31.recv = bf16[8,16,1024]{2,1,0:T(8,128)(2,1)S(1)} all-to-all(bf16[8,16,1024]{2,1,0:T(8,128)(2,1)S(1)} %plane.1), channel_id=1, replica_groups=mesh['z'=8,'x'=4,'y'=4,'c'=2] {'z'}, dimensions={0} | all-to-all | bytes 524288 | tf_op jit(solution)/shard_map/all_to_all | solution.py:434
  135.0 3.7 %collective-permute-start.15 = (f32[16,2048]{1,0:T(8,128)S(1)}, f32[16,2048]{1,0:T(8,128)S(1)}, u32[]{:S(2)}, u32[]{:S(2)}) collective-permute-start(f32[16,2048]{1,0:T(8,128)S(1)} %get-tuple-element.77), channel_id=1, source_target_pairs={{0,1},{1,0},{2,3},{3,2},{4,5},{5,4},{6,7},{7,6},{8,9},{9,8},{10,11... | collective-permute-start | bytes 393224 | tf_op jit(solution)/shard_map/ppermute | solution.py:421
  138.7 1.0 collective-permute-done.15.theirs
  139.7 0.7 grads.1
  (34 shorter events, 0.1 us)
Async XLA Ops:
  2.0 18.0 %all-to-all-start = ((bf16[16,8,256]{2,1,0:T(8,128)(2,1)}), bf16[16,8,256]{2,1,0:T(8,128)(2,1)S(1)}, u32[]{:S(2)}, u32[]{:S(2)}) async-start(bf16[16,8,256]{2,1,0:T(8,128)(2,1)} %bitcast.3), calls=%async_computation | async-start | bytes 131072 | tf_op jit(solution)/shard_map/all_to_all | solution.py:434
  12.0 16.3 %collective-permute-start.1 = (bf16[128,2048]{1,0:T(8,128)(2,1)}, bf16[128,2048]{1,0:T(8,128)(2,1)S(1)}, u32[]{:S(2)}, u32[]{:S(2)}) collective-permute-start(bf16[128,2048]{1,0:T(8,128)(2,1)} %bitcast.14), channel_id=1, source_target_pairs={{0,32},{32,0},{64,96},{96,64},{128,160},{160,128},{192,224},{224,1... | collective-permute-start | bytes 1572872 | tf_op jit(solution)/shard_map/ppermute | solution.py:430
  20.0 7.8 %copy-start.8 = (bf16[1,128,2048]{2,1,0:T(8,128)(2,1)S(1)}, bf16[1,128,2048]{2,1,0:T(8,128)(2,1)}, u32[]{:S(2)}) copy-start(bf16[1,128,2048]{2,1,0:T(8,128)(2,1)} %param.8) | copy-start | bytes 1572868
  21.1 24.7 %all-to-all-start.1 = ((bf16[16,128,256]{2,1,0:T(8,128)(2,1)}), bf16[16,128,256]{2,1,0:T(8,128)(2,1)S(1)}, u32[]{:S(2)}, u32[]{:S(2)}) async-start(bf16[16,128,256]{2,1,0:T(8,128)(2,1)} %broadcast_in_dim.26), calls=%async_computation.1 | async-start | bytes 2097152 | tf_op jit(solution)/shard_map/all_to_all | solution.py:434
  27.9 4.8 %collective-permute-start = (bf16[128,2048]{1,0:T(8,128)(2,1)S(1)}, bf16[128,2048]{1,0:T(8,128)(2,1)S(1)}, u32[]{:S(2)}, u32[]{:S(2)}) collective-permute-start(bf16[128,2048]{1,0:T(8,128)(2,1)S(1)} %bitcast.16), channel_id=1, source_target_pairs={{0,1},{1,0},{2,3},{3,2},{4,5},{5,4},{6,7},{7,6},{8,9},{9,8},{10,11... | collective-permute-start | bytes 1572872 | tf_op jit(solution)/shard_map/ppermute | solution.py:421
  28.2 4.4 %copy-start.9 = (bf16[128,2048]{1,0:T(8,128)(2,1)}, bf16[128,2048]{1,0:T(8,128)(2,1)S(1)}, u32[]{:S(2)}) copy-start(bf16[128,2048]{1,0:T(8,128)(2,1)S(1)} %collective-permute-done.1.far) | copy-start | bytes 1572868
  28.3 4.4 %collective-permute-start.2 = (bf16[128,2048]{1,0:T(8,128)(2,1)S(1)}, bf16[128,2048]{1,0:T(8,128)(2,1)S(1)}, u32[]{:S(2)}, u32[]{:S(2)}) collective-permute-start(bf16[128,2048]{1,0:T(8,128)(2,1)S(1)} %collective-permute-done.1.far), channel_id=1, source_target_pairs={{0,1},{1,0},{2,3},{3,2},{4,5},{5,4},{6,7},{7,6},{8,9},{9,8},{10,11... | collective-permute-start | bytes 1572872 | tf_op jit(solution)/shard_map/ppermute | solution.py:421
  30.5 7.2 %collective-permute-start.3 = (bf16[384,256]{1,0:T(8,128)(2,1)}, bf16[384,256]{1,0:T(8,128)(2,1)S(1)}, u32[]{:S(2)}, u32[]{:S(2)}) collective-permute-start(bf16[384,256]{1,0:T(8,128)(2,1)} %get-tuple-element.46), channel_id=1, source_target_pairs={{0,1},{1,0},{2,3},{3,2},{4,5},{5,4},{6,7},{7,6},{8,9},{9,8},{10,11... | collective-permute-start | bytes 589832 | tf_op jit(solution)/shard_map/ppermute | solution.py:421
  30.8 6.9 %collective-permute-start.4 = (bf16[384,256]{1,0:T(8,128)(2,1)}, bf16[384,256]{1,0:T(8,128)(2,1)S(1)}, u32[]{:S(2)}, u32[]{:S(2)}) collective-permute-start(bf16[384,256]{1,0:T(8,128)(2,1)} %get-tuple-element.47), channel_id=1, source_target_pairs={{0,32},{32,0},{64,96},{96,64},{128,160},{160,128},{192,224},{224,1... | collective-permute-start | bytes 589832 | tf_op jit(solution)/shard_map/ppermute | solution.py:430
  31.0 11.1 %collective-permute-start.5 = (bf16[384,256]{1,0:T(8,128)(2,1)}, bf16[384,256]{1,0:T(8,128)(2,1)S(1)}, u32[]{:S(2)}, u32[]{:S(2)}) collective-permute-start(bf16[384,256]{1,0:T(8,128)(2,1)} %get-tuple-element.48), channel_id=1, source_target_pairs={{0,33},{1,32},{32,1},{33,0},{64,97},{65,96},{96,65},{97,64},{128,1... | collective-permute-start | bytes 589832 | tf_op jit(solution)/shard_map/ppermute | solution.py:426
  32.6 0.8 copy-start.10
  32.6 1.0 copy-start.11
  37.6 4.5 %copy-start.12 = (bf16[384,256]{1,0:T(8,128)(2,1)}, bf16[384,256]{1,0:T(8,128)(2,1)S(1)}, u32[]{:S(2)}) copy-start(bf16[384,256]{1,0:T(8,128)(2,1)S(1)} %collective-permute-done.3.from_c) | copy-start | bytes 589828
  37.7 4.5 %copy-start.13 = (bf16[384,256]{1,0:T(8,128)(2,1)}, bf16[384,256]{1,0:T(8,128)(2,1)S(1)}, u32[]{:S(2)}) copy-start(bf16[384,256]{1,0:T(8,128)(2,1)S(1)} %collective-permute-done.4.from_z) | copy-start | bytes 589828
  42.1 0.7 copy-start.14
  45.8 1.0 copy-start.4
  51.2 27.1 %collective-permute-start.6 = (bf16[16,128,256]{2,1,0:T(8,128)(2,1)}, bf16[16,128,256]{2,1,0:T(8,128)(2,1)S(1)}, u32[]{:S(2)}, u32[]{:S(2)}) collective-permute-start(bf16[16,128,256]{2,1,0:T(8,128)(2,1)} %get-tuple-element.60.w_all), channel_id=1, source_target_pairs={{0,32},{32,0},{64,96},{96,64},{128,160},{160,128},{192,224},{224,1... | collective-permute-start | bytes 3145736 | tf_op jit(solution)/shard_map/ppermute | solution.py:430
  66.9 11.4 %all-to-all-start.3 = ((bf16[16,64,128]{2,1,0:T(8,128)(2,1)}), bf16[16,64,128]{2,1,0:T(8,128)(2,1)S(1)}, u32[]{:S(2)}, u32[]{:S(2)}) async-start(bf16[16,64,128]{2,1,0:T(8,128)(2,1)} %scan.1), calls=%async_computation.3 | async-start | bytes 524288 | tf_op jit(solution)/shard_map/all_to_all | solution.py:434
  78.2 0.7 copy-start.7
  78.2 1.1 copy-start.5
  84.0 6.2 %collective-permute-start.11 = (f32[16,512]{1,0:T(8,128)}, f32[16,512]{1,0:T(8,128)S(1)}, u32[]{:S(2)}, u32[]{:S(2)}) collective-permute-start(f32[16,512]{1,0:T(8,128)} %get-tuple-element.64.lat_a), channel_id=1, source_target_pairs={{0,33},{1,32},{32,1},{33,0},{64,97},{65,96},{96,65},{97,64},{128,1... | collective-permute-start | bytes 98312 | tf_op jit(solution)/shard_map/ppermute | solution.py:426
  88.3 3.0 %collective-permute-start.10 = (f32[16,512]{1,0:T(8,128)}, f32[16,512]{1,0:T(8,128)S(1)}, u32[]{:S(2)}, u32[]{:S(2)}) collective-permute-start(f32[16,512]{1,0:T(8,128)} %get-tuple-element.64.lat_a), channel_id=1, source_target_pairs={{0,32},{32,0},{64,96},{96,64},{128,160},{160,128},{192,224},{224,1... | collective-permute-start | bytes 98312 | tf_op jit(solution)/shard_map/ppermute | solution.py:430
  88.3 2.9 %collective-permute-start.9 = (f32[16,512]{1,0:T(8,128)}, f32[16,512]{1,0:T(8,128)S(1)}, u32[]{:S(2)}, u32[]{:S(2)}) collective-permute-start(f32[16,512]{1,0:T(8,128)} %get-tuple-element.64.lat_a), channel_id=1, source_target_pairs={{0,1},{1,0},{2,3},{3,2},{4,5},{5,4},{6,7},{7,6},{8,9},{9,8},{10,11... | collective-permute-start | bytes 98312 | tf_op jit(solution)/shard_map/ppermute | solution.py:421
  90.2 1.0 copy-start.16
  91.2 0.6 copy-start.17
  91.3 0.6 copy-start.18
  95.5 3.8 %copy-start.6 = (bf16[512,256]{1,0:T(8,128)(2,1)S(1)}, bf16[512,256]{1,0:T(8,128)(2,1)}, u32[]{:S(2)}) copy-start(bf16[512,256]{1,0:T(8,128)(2,1)} %get-tuple-element.61.kd_r) | copy-start | bytes 786436
  95.5 26.3 %all-to-all-start.4 = ((bf16[16,16,2816]{2,1,0:T(8,128)(2,1)}), bf16[16,16,2816]{2,1,0:T(8,128)(2,1)S(1)}, u32[]{:S(2)}, u32[]{:S(2)}) async-start(bf16[16,16,2816]{2,1,0:T(8,128)(2,1)} %get-tuple-element.74), calls=%async_computation.4 | async-start | bytes 2883584 | tf_op jit(solution)/shard_map/all_to_all | solution.py:434
  99.4 11.0 %copy-start.2 = (bf16[512,256]{1,0:T(8,128)(2,1)S(1)}, bf16[512,256]{1,0:T(8,128)(2,1)}, u32[]{:S(2)}) copy-start(bf16[512,256]{1,0:T(8,128)(2,1)} %get-tuple-element.67.gate) | copy-start | bytes 786436
  100.1 16.3 %copy-start.1 = (bf16[16,2048]{1,0:T(8,128)(2,1)S(1)}, bf16[16,2048]{1,0:T(8,128)(2,1)}, u32[]{:S(2)}) copy-start(bf16[16,2048]{1,0:T(8,128)(2,1)} %down.3) | copy-start | bytes 196612
  100.1 16.3 %copy-start.3 = (bf16[16,128]{1,0:T(8,128)(2,1)S(1)}, bf16[16,128]{1,0:T(8,128)(2,1)}, u32[]{:S(2)}) copy-start(bf16[16,128]{1,0:T(8,128)(2,1)} %get-tuple-element.66.lat) | copy-start | bytes 12292
  100.1 5.0 %collective-permute-start.7 = (bf16[256,256]{1,0:T(8,128)(2,1)S(1)}, bf16[256,256]{1,0:T(8,128)(2,1)S(1)}, u32[]{:S(2)}, u32[]{:S(2)}) collective-permute-start(bf16[256,256]{1,0:T(8,128)(2,1)S(1)} %get-tuple-element.81), channel_id=1, source_target_pairs={{0,32},{32,0},{64,96},{96,64},{128,160},{160,128},{192,224},{224,1... | collective-permute-start | bytes 393224 | tf_op jit(solution)/shard_map/ppermute | solution.py:430
  105.0 0.7 copy-start.15
  109.4 6.9 %collective-permute-start.8 = (f32[128,2048]{1,0:T(8,128)}, f32[128,2048]{1,0:T(8,128)S(1)}, u32[]{:S(2)}, u32[]{:S(2)}) collective-permute-start(f32[128,2048]{1,0:T(8,128)} %get-tuple-element.63), channel_id=1, source_target_pairs={{0,1},{1,0},{2,3},{3,2},{4,5},{5,4},{6,7},{7,6},{8,9},{9,8},{10,11... | collective-permute-start | bytes 3145736 | tf_op jit(solution)/shard_map/ppermute | solution.py:421
  110.4 2.2 %collective-permute-start.12 = (bf16[128,256]{1,0:T(8,128)(2,1)S(1)}, bf16[128,256]{1,0:T(8,128)(2,1)S(1)}, u32[]{:S(2)}, u32[]{:S(2)}) collective-permute-start(bf16[128,256]{1,0:T(8,128)(2,1)S(1)} %get-tuple-element.69), channel_id=1, source_target_pairs={{0,1},{1,0},{2,3},{3,2},{4,5},{5,4},{6,7},{7,6},{8,9},{9,8},{10,11... | collective-permute-start | bytes 196616 | tf_op jit(solution)/shard_map/ppermute | solution.py:421
  110.5 3.5 %collective-permute-start.13 = (bf16[128,256]{1,0:T(8,128)(2,1)S(1)}, bf16[128,256]{1,0:T(8,128)(2,1)S(1)}, u32[]{:S(2)}, u32[]{:S(2)}) collective-permute-start(bf16[128,256]{1,0:T(8,128)(2,1)S(1)} %get-tuple-element.70), channel_id=1, source_target_pairs={{0,32},{32,0},{64,96},{96,64},{128,160},{160,128},{192,224},{224,1... | collective-permute-start | bytes 196616 | tf_op jit(solution)/shard_map/ppermute | solution.py:430
  111.3 5.0 %collective-permute-start.14 = (bf16[128,256]{1,0:T(8,128)(2,1)S(1)}, bf16[128,256]{1,0:T(8,128)(2,1)S(1)}, u32[]{:S(2)}, u32[]{:S(2)}) collective-permute-start(bf16[128,256]{1,0:T(8,128)(2,1)S(1)} %get-tuple-element.71), channel_id=1, source_target_pairs={{0,33},{1,32},{32,1},{33,0},{64,97},{65,96},{96,65},{97,64},{128,1... | collective-permute-start | bytes 196616 | tf_op jit(solution)/shard_map/ppermute | solution.py:426
  116.3 1.2 copy-start
  135.0 4.7 %collective-permute-start.15 = (f32[16,2048]{1,0:T(8,128)S(1)}, f32[16,2048]{1,0:T(8,128)S(1)}, u32[]{:S(2)}, u32[]{:S(2)}) collective-permute-start(f32[16,2048]{1,0:T(8,128)S(1)} %get-tuple-element.77), channel_id=1, source_target_pairs={{0,1},{1,0},{2,3},{3,2},{4,5},{5,4},{6,7},{7,6},{8,9},{9,8},{10,11... | collective-permute-start | bytes 393224 | tf_op jit(solution)/shard_map/ppermute | solution.py:421

commit v7 on v6

--- a/solution.py
+++ b/solution.py
@@ -156,39 +156,41 @@
         beta[tok_of(n)] = dot_mask(lower, gamma[tok_of(n)])
 
 
-def start_body(mine, from_c, from_z, from_cz, beta, q_o, g_o, v_o, adds, start):
+def assemble(out, a, b, c, d):
     first = is_first()
-    for i, out in enumerate((q_o, g_o, v_o)):
-        rows = slice(i * TOK, (i + 1) * TOK)
-        a, b, c, d = mine[rows], from_c[rows], from_z[rows], from_cz[rows]
-        out[:TOK] = pick(first, a, b)
-        out[TOK:PAIR] = pick(first, b, a)
-        out[PAIR : PAIR + TOK] = pick(first, c, d)
-        out[PAIR + TOK :] = pick(first, d, c)
+    out[:TOK] = pick(first, a, b)
+    out[TOK:PAIR] = pick(first, b, a)
+    out[PAIR : PAIR + TOK] = pick(first, c, d)
+    out[PAIR + TOK :] = pick(first, d, c)
+
+
+def added_grads(q, g, beta, seq, n):
+    r = rows_of(seq, n)
+    b = beta[r]
+    scaled = q[r].astype(F32) * jnp.exp(b)
+    grad = g[r]
+    return [dot_hl(grad[:, col_of(h)], scaled[:, col_of(h)], TN) for h in range(PER_SEQ)], b[-1:]
+
+
+def start_states(q, g, beta, send):
     run = [jnp.zeros((DK, DK), F32)] * HALF
     decays = []
     for seq in range(2):
         total = jnp.zeros((1, QUART), F32)
         for n in reversed(range(BLOCKS)):
-            r = rows_of(seq, n)
-            b = beta[r]
-            last = b[GROUP - 1 : GROUP]
+            parts, last = added_grads(q, g, beta, seq, n)
             total = total + last
             decay = jnp.exp(last)
-            scaled = q_o[r].astype(F32) * jnp.exp(b)
-            grad = g_o[r]
             for h in range(PER_SEQ):
                 s = state_of(seq, h)
-                part = dot_hl(grad[:, col_of(h)], scaled[:, col_of(h)], TN)
-                adds[n, col_of(s)] = part
-                run[s] = decay[:, col_of(h)] * run[s] + part
+                run[s] = decay[:, col_of(h)] * run[s] + parts[h]
         decays.append(jnp.exp(total))
     for p in range(PS):
         s, at = p // PER, (p % PER) * ROWS
         row = decays[s // PER_SEQ][:, col_of(s % PER_SEQ)]
-        start[p, :ROWS] = run[s][at : at + ROWS].astype(BF16)
+        send[p, :ROWS] = run[s][at : at + ROWS].astype(BF16)
         top = row.astype(BF16).astype(F32)
-        start[p, ROWS:] = jnp.concatenate(
+        send[p, ROWS : ROWS + 16] = jnp.concatenate(
             [jnp.broadcast_to(top, (8, DK)), jnp.broadcast_to(row - top, (8, DK))], axis=0
         ).astype(BF16)
 
@@ -215,15 +217,22 @@
             w[z * 256 + p * 16 : z * 256 + p * 16 + 16] = recv[p, z * 16 : z * 16 + 16]
 
 
-def keys_body(recv_h, tok_h, beta_h, v_h, start_h, key_o, send, w_o,
-              recv, tok, beta, v, start, w, sems):
+def keys_body(recv_h, tok_h, beta_h, mine, from_c, from_z, from_cz, key_o, send, w_o,
+              recv, tok, beta, parts, q, g, v, w, sems):
     copies = load(
-        ((recv_h, recv), (tok_h, tok), (beta_h, beta), (v_h, v), (start_h, start)), sems
-    )
-    copies[0].wait()
+        [(beta_h, beta)]
+        + [(a, parts.at[i]) for i, a in enumerate((mine, from_c, from_z, from_cz))]
+        + [(recv_h, recv), (tok_h, tok)],
+        sems,
+    )
+    for copy in copies[:5]:
+        copy.wait()
+    for i, out in enumerate((q, g, v)):
+        assemble(out, *(parts[j, i * TOK : (i + 1) * TOK] for j in range(4)))
+    start_states(q, g, beta, send)
+    copies[5].wait()
     unpack(recv, w)
-    for copy in copies[1:]:
-        copy.wait()
+    copies[6].wait()
     key_o[...] = dot(tok[...], w[...]).astype(BF16)
     run = [jnp.zeros((DK, DK), F32)] * HALF
     for seq in range(2):
@@ -234,7 +243,6 @@
                 run[s] = decay[:, col_of(h)] * run[s] + parts[h]
     for p in range(PS):
         s, at = p // PER, (p % PER) * ROWS
-        send[p, : ROWS + 16] = start[p]
         send[p, ROWS + 16 :] = run[s][at : at + ROWS].astype(BF16)
 
 
@@ -253,8 +261,16 @@
         run = decay(p) * run + recv[p, ROWS + 16 :].astype(F32)
 
 
-def inner_body(q_r, g_r, v_r, key_r, beta, kd_o, local):
+def inner_body(mine, from_c, from_z, from_cz, key_r, beta, kd_o, local, q_r, g_r, v_r, adds):
     low, high = low_mask()
+    for i, out in enumerate((q_r, g_r, v_r)):
+        rows = slice(i * TOK, (i + 1) * TOK)
+        assemble(out, mine[rows], from_c[rows], from_z[rows], from_cz[rows])
+    for seq in range(2):
+        for n in range(BLOCKS):
+            parts, _ = added_grads(q_r, g_r, beta, seq, n)
+            for h in range(PER_SEQ):
+                adds[n, col_of(state_of(seq, h))] = parts[h]
     for n in range(QUAD // GROUP):
         r = tok_of(n)
         b = beta[r]
@@ -452,24 +468,22 @@
         gates_body,
         (shape((QUAD, MODEL), BF16), shape((QUAD, RANK), BF16), quad_f, quad_f), "gates", BIG,
     )(own, swap(own), far, swap(far), gate_down, gate_up, gate_bias[None])
-    q, g, v, add_g, start = kernel(
-        start_body,
-        (quad_bf, quad_bf, quad_bf, shape((BLOCKS, WIDTH, DK)),
-         shape((PS, ROWS + 16, DK), BF16)),
-        "start", BIG,
-    )(mine, swap(to_c), across(to_z), cross(to_cz), beta)
+    parts = (mine, swap(to_c), across(to_z), cross(to_cz))
     keys, send, w_all = kernel(
         keys_body,
         (quad_bf, shape((PS, 2 * ROWS + 16, DK), BF16), shape((PS, ZS * 16, QUART), BF16)),
-        "keys", BIG, specs=[HBM] * 5, out_specs=(VM, VM, HBM), alias={0: 2},
+        "keys", BIG, specs=[HBM] * 7, out_specs=(VM, VM, HBM), alias={0: 2},
         scratch=[pltpu.VMEM((PS, ZS * 16, QUART), BF16), pltpu.VMEM((QUAD, MODEL), BF16),
-                 pltpu.VMEM((QUAD, QUART), F32), pltpu.VMEM((QUAD, QUART), BF16),
-                 pltpu.VMEM((PS, ROWS + 16, DK), BF16), pltpu.VMEM((MODEL, QUART), BF16),
-                 pltpu.SemaphoreType.DMA((5,))],
-    )(w_all, tok, beta, v, start)
+                 pltpu.VMEM((QUAD, QUART), F32), pltpu.VMEM((4, 3 * TOK, QUART), BF16)]
+        + [pltpu.VMEM((QUAD, QUART), BF16)] * 3
+        + [pltpu.VMEM((MODEL, QUART), BF16), pltpu.SemaphoreType.DMA((7,))],
+    )(w_all, tok, beta, *parts)
     w_far = across(w_all)
     recv = a2a(send, XY)
-    kd_local, local_part = kernel(inner_body, (quad_f, quad_f), "inner", BIG)(q, g, v, keys, beta)
+    kd_local, local_part, q, g, v, add_g = kernel(
+        inner_body, (quad_f, quad_f, quad_bf, quad_bf, quad_bf, shape((BLOCKS, WIDTH, DK))),
+        "inner", BIG,
+    )(*parts, keys, beta)
     recv = a2a(kernel(scan_body, shape((PS, 2 * ROWS, DK), BF16), "scan", 8)(recv), XY)
     kd, gate, up_part, lat_part = kernel(
         gate_body,

time: 141 us -> 139 us (0.986)
  starting transfers between devices: 41.4 us -> 45 us
  waiting for transfers between devices: 27.7 us -> 24.6 us
  Pallas kernels: 33.6 us -> 31.5 us
    ppermute x6, waiting for transfers between devices: 6.63 us -> 3.73 us  [across(): return lax.ppermute(a, 'z', [(i, i ^ 1) for i in range(ZS)])]
    pallas_call x2 -> x1, Pallas kernels: 8.05 us -> 5.65 us  [local(): kernel(inner_body, (quad_f, quad_f, quad_bf, quad_bf, quad_bf, shape((BLO...]
    ppermute x7, starting transfers between devices: 6.11 us -> 8.29 us  [swap(): return lax.ppermute(a, 'c', SWAP)]
    ppermute x6, starting transfers between devices: 3.49 us -> 5.25 us  [across(): return lax.ppermute(a, 'z', [(i, i ^ 1) for i in range(ZS)])]
  transfers between devices with their start and end apart: 20 -> 20, of which waited for: 10 -> 9; matrix products, arithmetic and copies ran while one was open for 1% -> 1% of each run, Pallas kernels for 14% -> 13%
where the time goes in v7:
time: 139 us; the launch traced here: 138 us
  starting transfers between devices  45 us (32%)
  Pallas kernels  31.5 us (23%)
  blocking collectives  27.2 us (20%)
  waiting for transfers between devices  24.6 us (18%)
  local copies, waits for them, and re-layouts  8.62 us (6%)
    all_to_all x2, blocking collectives, a2a(): return lax.all_to_all(a, axis, 0, 0)  27.2 us
    all_to_all x4, starting transfers between devices, a2a(): return lax.all_to_all(a, axis, 0, 0)  24.5 us
    all_to_all x4, waiting for transfers between devices, a2a(): return lax.all_to_all(a, axis, 0, 0)  11.1 us
    ppermute x3, waiting for transfers between devices, cross(): return lax.ppermute(a, ('z', 'c'), pairs)  8.77 us
    ppermute x7, starting transfers between devices, swap(): return lax.ppermute(a, 'c', SWAP)  8.29 us
    ppermute x3, starting transfers between devices, cross(): return lax.ppermute(a, ('z', 'c'), pairs)  6.92 us
    pallas_call x1, Pallas kernels, local(): kernel(inner_body, (quad_f, quad_f, quad_bf, quad_bf, quad_bf, shape((BLO...  5.65 us
    unnamed x38, local copies, waits for them, and re-layouts  5.52 us
  transfers between devices with their start and end apart: 20, of which 9 were waited for; matrix products, arithmetic and copies ran while one was open for 1% of the time, Pallas kernels for 13%

profile of v7, /device:TPU:1, one launch (start us, length us, event | category | flops | bytes accessed | tf_op | source)
XLA Modules:
  0.0 137.8 jit_solution(14051591729765275900)
XLA Ops:
  0.6 0.7 copy.14
  1.4 0.6 broadcast_in_dim.24
  2.0 10.0 %all-to-all-start = ((bf16[16,8,256]{2,1,0:T(8,128)(2,1)}), bf16[16,8,256]{2,1,0:T(8,128)(2,1)S(1)}, u32[]{:S(2)}, u32[]{:S(2)}) async-start(bf16[16,8,256]{2,1,0:T(8,128)(2,1)} %bitcast.3), calls=%async_computation | async-start | bytes 131072 | tf_op jit(solution)/shard_map/all_to_all | solution.py:450
  12.0 1.4 %collective-permute-start.1 = (bf16[128,2048]{1,0:T(8,128)(2,1)}, bf16[128,2048]{1,0:T(8,128)(2,1)S(1)}, u32[]{:S(2)}, u32[]{:S(2)}) collective-permute-start(bf16[128,2048]{1,0:T(8,128)(2,1)} %bitcast.14), channel_id=1, source_target_pairs={{0,32},{32,0},{64,96},{96,64},{128,160},{160,128},{192,224},{224,1... | collective-permute-start | bytes 1572872 | tf_op jit(solution)/shard_map/ppermute | solution.py:446
  13.4 6.7 %all-to-all-done = bf16[16,8,256]{2,1,0:T(8,128)(2,1)S(1)} async-done(((bf16[16,8,256]{2,1,0:T(8,128)(2,1)}), bf16[16,8,256]{2,1,0:T(8,128)(2,1)S(1)}, u32[]{:S(2)}, u32[]{:S(2)}) %all-to-all-start) | async-done | bytes 65568 | tf_op jit(solution)/shard_map/all_to_all | solution.py:450
  20.0 1.1 broadcast_in_dim.26
  21.1 6.8 %all-to-all-start.1 = ((bf16[16,128,256]{2,1,0:T(8,128)(2,1)}), bf16[16,128,256]{2,1,0:T(8,128)(2,1)S(1)}, u32[]{:S(2)}, u32[]{:S(2)}) async-start(bf16[16,128,256]{2,1,0:T(8,128)(2,1)} %broadcast_in_dim.26), calls=%async_computation.1 | async-start | bytes 2097152 | tf_op jit(solution)/shard_map/all_to_all | solution.py:450
  27.9 0.4 collective-permute-start
  28.2 0.0 collective-permute-done.1.far
  28.2 0.2 collective-permute-start.2
  28.5 2.0 %prep.1 = (bf16[384,256]{1,0:T(8,128)(2,1)}, bf16[384,256]{1,0:T(8,128)(2,1)}, bf16[384,256]{1,0:T(8,128)(2,1)}, bf16[384,256]{1,0:T(8,128)(2,1)}) custom-call(bf16[128,1024]{1,0:T(8,128)(2,1)} %bitcast.17, bf16[128,1024]{1,0:T(8,128)(2,1)} %bitcast.18, bf16[128,1024]{1,0:T(8,128)(2,1)} %bitcast.19), custom_call_target="tpu_custom_call" | custom-call | tf_op jit(solution)/shard_map/prep/pallas_call | solution.py:461
  30.5 0.3 collective-permute-start.3
  30.8 0.2 collective-permute-start.4
  31.0 1.6 %collective-permute-start.5 = (bf16[384,256]{1,0:T(8,128)(2,1)}, bf16[384,256]{1,0:T(8,128)(2,1)S(1)}, u32[]{:S(2)}, u32[]{:S(2)}) collective-permute-start(bf16[384,256]{1,0:T(8,128)(2,1)} %get-tuple-element.47), channel_id=1, source_target_pairs={{0,33},{1,32},{32,1},{33,0},{64,97},{65,96},{96,65},{97,64},{128,1... | collective-permute-start | bytes 589832 | tf_op jit(solution)/shard_map/ppermute | solution.py:442
  32.6 0.0 collective-permute-done.peer
  32.6 0.0 collective-permute-done.2.far_peer
  32.7 0.8 copy-done.13
  33.4 0.2 copy-done.14
  33.6 4.1 %gates.1 = (bf16[512,2048]{1,0:T(8,128)(2,1)}, bf16[512,16]{1,0:T(8,128)(2,1)}, f32[512,256]{1,0:T(8,128)}, f32[512,256]{1,0:T(8,128)}) custom-call(bf16[128,2048]{1,0:T(8,128)(2,1)} %bitcast.15, bf16[128,2048]{1,0:T(8,128)(2,1)} %copy-done.13, bf16[128,2048]{1,0:T(8,128)(2,1)} %copy-done.12, bf16[128,2048]{1,0:T(8,128)(2,1)} %copy-done.14, ...), custom_call_target="tpu_custom_call" | custom-call | tf_op jit(solution)/shard_map/gates/pallas_call | solution.py:467
  37.7 0.0 collective-permute-done.3.from_c
  37.7 0.0 collective-permute-done.4.from_z
  37.7 4.4 %collective-permute-done.5.from_cz = bf16[384,256]{1,0:T(8,128)(2,1)S(1)} collective-permute-done((bf16[384,256]{1,0:T(8,128)(2,1)}, bf16[384,256]{1,0:T(8,128)(2,1)S(1)}, u32[]{:S(2)}, u32[]{:S(2)}) %collective-permute-start.5) | collective-permute-done | bytes 196640 | tf_op jit(solution)/shard_map/ppermute | solution.py:442
  42.1 2.7 %all-to-all-done.1.recv_h = bf16[16,128,256]{2,1,0:T(8,128)(2,1)S(1)} async-done(((bf16[16,128,256]{2,1,0:T(8,128)(2,1)}), bf16[16,128,256]{2,1,0:T(8,128)(2,1)S(1)}, u32[]{:S(2)}, u32[]{:S(2)}) %all-to-all-start.1) | async-done | bytes 1048608 | tf_op jit(solution)/shard_map/all_to_all | solution.py:450
  44.8 0.9 copy-done.4
  45.8 4.7 %keys.1 = (bf16[512,256]{1,0:T(8,128)(2,1)}, bf16[16,80,128]{2,1,0:T(8,128)(2,1)}, bf16[16,128,256]{2,1,0:T(8,128)(2,1)}) custom-call(bf16[16,128,256]{2,1,0:T(8,128)(2,1)} %copy-done.4, bf16[512,2048]{1,0:T(8,128)(2,1)} %get-tuple-element.42.tok_h.tok, f32[512,256]{1,0:T(8,128)} %get-tuple-element.43.beta_h.beta, ...), custom_call_target="tpu_custom_call", output_to_operand_aliasing={{2}: (0, {})} | custom-call | tf_op jit(solution)/shard_map/keys/pallas_call | solution.py:472
  50.4 0.1 collective-permute-start.6
  50.5 12.1 %all_to_all.30.recv = bf16[16,80,128]{2,1,0:T(8,128)(2,1)S(1)} all-to-all(bf16[16,80,128]{2,1,0:T(8,128)(2,1)} %get-tuple-element.48), channel_id=1, replica_groups=mesh['z'=8,'x'=4,'y'=4,'c'=2] {'x','y'}, dimensions={0} | all-to-all | bytes 655360 | tf_op jit(solution)/shard_map/all_to_all | solution.py:450
  62.6 0.8 scan.1
  63.4 3.5 %all-to-all-start.3 = ((bf16[16,64,128]{2,1,0:T(8,128)(2,1)}), bf16[16,64,128]{2,1,0:T(8,128)(2,1)S(1)}, u32[]{:S(2)}, u32[]{:S(2)}) async-start(bf16[16,64,128]{2,1,0:T(8,128)(2,1)} %scan.1), calls=%async_computation.3 | async-start | bytes 524288 | tf_op jit(solution)/shard_map/all_to_all | solution.py:450
  66.9 5.7 %inner.1 = (f32[512,256]{1,0:T(8,128)}, f32[512,256]{1,0:T(8,128)}, bf16[512,256]{1,0:T(8,128)(2,1)}, bf16[512,256]{1,0:T(8,128)(2,1)}, bf16[512,256]{1,0:T(8,128)(2,1)}, /*index=5*/f32[4,512,128]{2,1,0:T(8,128)}) custom-call(bf16[384,256]{1,0:T(8,128)(2,1)} %get-tuple-element.44.mine, bf16[384,256]{1,0:T(8,128)(2,1)} %copy-done.8, ...), custom_call_target="tpu_custom_call" | custom-call | tf_op jit(solution)/shard_map/inner/pallas_call | solution.py:483
  72.6 1.8 %all-to-all-done.3.recv = bf16[16,64,128]{2,1,0:T(8,128)(2,1)S(1)} async-done(((bf16[16,64,128]{2,1,0:T(8,128)(2,1)}), bf16[16,64,128]{2,1,0:T(8,128)(2,1)S(1)}, u32[]{:S(2)}, u32[]{:S(2)}) %all-to-all-start.3) | async-done | bytes 262176 | tf_op jit(solution)/shard_map/all_to_all | solution.py:450
  74.4 0.0 collective-permute-done.6._.far_all
  74.4 0.7 copy-done.7
  75.1 0.4 copy-done.5
  75.4 4.7 %gate.1 = (bf16[512,256]{1,0:T(8,128)(2,1)}, bf16[512,256]{1,0:T(8,128)(2,1)}, f32[16,256]{1,0:T(8,128)}, f32[16,512]{1,0:T(8,128)}) custom-call(bf16[16,64,128]{2,1,0:T(8,128)(2,1)} %copy-done.7, f32[4,512,128]{2,1,0:T(8,128)} %get-tuple-element.50.adds, bf16[512,256]{1,0:T(8,128)(2,1)} %get-tuple-element.49.key_r, bf16[512,256]{1,0:T(8,128)(2,1)} %get-tuple-element.51.v_r, ...), custom_call_target="tpu_custom_call" | custom-call | tf_op jit(solution)/shard_map/gate/pallas_call | solution.py:488
  80.2 1.2 collective-permute-start.10
  81.4 4.0 %collective-permute-start.11 = (f32[16,512]{1,0:T(8,128)}, f32[16,512]{1,0:T(8,128)S(1)}, u32[]{:S(2)}, u32[]{:S(2)}) collective-permute-start(f32[16,512]{1,0:T(8,128)} %get-tuple-element.62.lat_a), channel_id=1, source_target_pairs={{0,33},{1,32},{32,1},{33,0},{64,97},{65,96},{96,65},{97,64},{128,1... | collective-permute-start | bytes 98312 | tf_op jit(solution)/shard_map/ppermute | solution.py:442
  85.4 0.1 collective-permute-start.9
  85.5 0.0 collective-permute-done.10.lat_z
  85.5 2.1 %collective-permute-done.11.lat_cz = f32[16,512]{1,0:T(8,128)S(1)} collective-permute-done((f32[16,512]{1,0:T(8,128)}, f32[16,512]{1,0:T(8,128)S(1)}, u32[]{:S(2)}, u32[]{:S(2)}) %collective-permute-start.11) | collective-permute-done | bytes 32800 | tf_op jit(solution)/shard_map/ppermute | solution.py:442
  87.5 0.6 copy-done.17
  88.1 0.0 copy-done.18
  88.2 3.7 %weights.1 = (bf16[16,128]{1,0:T(8,128)(2,1)}, bf16[16,16,2816]{2,1,0:T(8,128)(2,1)}) custom-call(f32[16,512]{1,0:T(8,128)} %get-tuple-element.62.lat_a, f32[16,512]{1,0:T(8,128)} %copy-done.18, f32[16,512]{1,0:T(8,128)} %copy-done.16, f32[16,512]{1,0:T(8,128)} %copy-done.17, f32[16,256]{1,0:T(8,128)} %get-tuple-element.63.up_part, ...), custom_call_target="tpu_custom_call" | custom-call | tf_op jit(solution)/shard_map/weights/pallas_call | solution.py:494
  91.8 4.2 %all-to-all-start.4 = ((bf16[16,16,2816]{2,1,0:T(8,128)(2,1)}), bf16[16,16,2816]{2,1,0:T(8,128)(2,1)S(1)}, u32[]{:S(2)}, u32[]{:S(2)}) async-start(bf16[16,16,2816]{2,1,0:T(8,128)(2,1)} %get-tuple-element.72), calls=%async_computation.4 | async-start | bytes 2883584 | tf_op jit(solution)/shard_map/all_to_all | solution.py:450
  96.1 0.7 fusion
  96.8 1.5 %collective-permute-start.7 = (bf16[256,256]{1,0:T(8,128)(2,1)S(1)}, bf16[256,256]{1,0:T(8,128)(2,1)S(1)}, u32[]{:S(2)}, u32[]{:S(2)}) collective-permute-start(bf16[256,256]{1,0:T(8,128)(2,1)S(1)} %get-tuple-element.79), channel_id=1, source_target_pairs={{0,32},{32,0},{64,96},{96,64},{128,160},{160,128},{192,224},{224,1... | collective-permute-start | bytes 393224 | tf_op jit(solution)/shard_map/ppermute | solution.py:446
  98.3 2.4 %collective-permute-done.7.kd_far = bf16[256,256]{1,0:T(8,128)(2,1)S(1)} collective-permute-done((bf16[256,256]{1,0:T(8,128)(2,1)S(1)}, bf16[256,256]{1,0:T(8,128)(2,1)S(1)}, u32[]{:S(2)}, u32[]{:S(2)}) %collective-permute-start.7) | collective-permute-done | bytes 131104 | tf_op jit(solution)/shard_map/ppermute | solution.py:446
  100.7 0.7 copy-done.15
  101.3 3.8 %through.1 = (f32[128,2048]{1,0:T(8,128)}, f32[128,2048]{1,0:T(8,128)}) custom-call(bf16[256,256]{1,0:T(8,128)(2,1)} %get-tuple-element.80.kd, bf16[256,256]{1,0:T(8,128)(2,1)} %copy-done.15, bf16[16,128,256]{2,1,0:T(8,128)(2,1)} %get-tuple-element.58.w_all, bf16[16,128,256]{2,1,0:T(8,128)(2,1)} %copy-done.5), custom_call_target="tpu_custom_call" | custom-call | tf_op jit(solution)/shard_map/through/pallas_call | solution.py:498
  105.1 2.8 %collective-permute-start.8 = (f32[128,2048]{1,0:T(8,128)}, f32[128,2048]{1,0:T(8,128)S(1)}, u32[]{:S(2)}, u32[]{:S(2)}) collective-permute-start(f32[128,2048]{1,0:T(8,128)} %get-tuple-element.61), channel_id=1, source_target_pairs={{0,1},{1,0},{2,3},{3,2},{4,5},{5,4},{6,7},{7,6},{8,9},{9,8},{10,11... | collective-permute-start | bytes 3145736 | tf_op jit(solution)/shard_map/ppermute | solution.py:437
  108.0 0.1 collective-permute-start.12
  108.1 0.8 collective-permute-start.13
  108.9 1.3 collective-permute-start.14
  110.2 1.4 collective-permute-done.13.gate_z
  111.6 2.3 %collective-permute-done.14.gate_cz = bf16[128,256]{1,0:T(8,128)(2,1)S(1)} collective-permute-done((bf16[128,256]{1,0:T(8,128)(2,1)S(1)}, bf16[128,256]{1,0:T(8,128)(2,1)S(1)}, u32[]{:S(2)}, u32[]{:S(2)}) %collective-permute-start.14) | collective-permute-done | bytes 65568 | tf_op jit(solution)/shard_map/ppermute | solution.py:442
  113.8 0.0 collective-permute-done.8.got
  113.9 1.2 copy-done
  115.1 1.2 input.1
  116.3 0.0 all-to-all-done.4.recv
  116.3 0.2 plane.1
  116.5 15.1 %all_to_all.31.recv = bf16[8,16,1024]{2,1,0:T(8,128)(2,1)S(1)} all-to-all(bf16[8,16,1024]{2,1,0:T(8,128)(2,1)S(1)} %plane.1), channel_id=1, replica_groups=mesh['z'=8,'x'=4,'y'=4,'c'=2] {'z'}, dimensions={0} | all-to-all | bytes 524288 | tf_op jit(solution)/shard_map/all_to_all | solution.py:450
  131.7 4.4 %collective-permute-start.15 = (f32[16,2048]{1,0:T(8,128)S(1)}, f32[16,2048]{1,0:T(8,128)S(1)}, u32[]{:S(2)}, u32[]{:S(2)}) collective-permute-start(f32[16,2048]{1,0:T(8,128)S(1)} %get-tuple-element.75), channel_id=1, source_target_pairs={{0,1},{1,0},{2,3},{3,2},{4,5},{5,4},{6,7},{7,6},{8,9},{9,8},{10,11... | collective-permute-start | bytes 393224 | tf_op jit(solution)/shard_map/ppermute | solution.py:437
  136.1 1.0 collective-permute-done.15.theirs
  137.1 0.7 grads.1
  (33 shorter events, 0.1 us)
Async XLA Ops:
  2.0 18.0 %all-to-all-start = ((bf16[16,8,256]{2,1,0:T(8,128)(2,1)}), bf16[16,8,256]{2,1,0:T(8,128)(2,1)S(1)}, u32[]{:S(2)}, u32[]{:S(2)}) async-start(bf16[16,8,256]{2,1,0:T(8,128)(2,1)} %bitcast.3), calls=%async_computation | async-start | bytes 131072 | tf_op jit(solution)/shard_map/all_to_all | solution.py:450
  12.0 16.3 %collective-permute-start.1 = (bf16[128,2048]{1,0:T(8,128)(2,1)}, bf16[128,2048]{1,0:T(8,128)(2,1)S(1)}, u32[]{:S(2)}, u32[]{:S(2)}) collective-permute-start(bf16[128,2048]{1,0:T(8,128)(2,1)} %bitcast.14), channel_id=1, source_target_pairs={{0,32},{32,0},{64,96},{96,64},{128,160},{160,128},{192,224},{224,1... | collective-permute-start | bytes 1572872 | tf_op jit(solution)/shard_map/ppermute | solution.py:446
  20.0 7.8 %copy-start.11 = (bf16[1,128,2048]{2,1,0:T(8,128)(2,1)S(1)}, bf16[1,128,2048]{2,1,0:T(8,128)(2,1)}, u32[]{:S(2)}) copy-start(bf16[1,128,2048]{2,1,0:T(8,128)(2,1)} %param.8) | copy-start | bytes 1572868
  21.1 23.7 %all-to-all-start.1 = ((bf16[16,128,256]{2,1,0:T(8,128)(2,1)}), bf16[16,128,256]{2,1,0:T(8,128)(2,1)S(1)}, u32[]{:S(2)}, u32[]{:S(2)}) async-start(bf16[16,128,256]{2,1,0:T(8,128)(2,1)} %broadcast_in_dim.26), calls=%async_computation.1 | async-start | bytes 2097152 | tf_op jit(solution)/shard_map/all_to_all | solution.py:450
  27.9 4.8 %collective-permute-start = (bf16[128,2048]{1,0:T(8,128)(2,1)S(1)}, bf16[128,2048]{1,0:T(8,128)(2,1)S(1)}, u32[]{:S(2)}, u32[]{:S(2)}) collective-permute-start(bf16[128,2048]{1,0:T(8,128)(2,1)S(1)} %bitcast.16), channel_id=1, source_target_pairs={{0,1},{1,0},{2,3},{3,2},{4,5},{5,4},{6,7},{7,6},{8,9},{9,8},{10,11... | collective-permute-start | bytes 1572872 | tf_op jit(solution)/shard_map/ppermute | solution.py:437
  28.2 4.4 %copy-start.12 = (bf16[128,2048]{1,0:T(8,128)(2,1)}, bf16[128,2048]{1,0:T(8,128)(2,1)S(1)}, u32[]{:S(2)}) copy-start(bf16[128,2048]{1,0:T(8,128)(2,1)S(1)} %collective-permute-done.1.far) | copy-start | bytes 1572868
  28.2 4.4 %collective-permute-start.2 = (bf16[128,2048]{1,0:T(8,128)(2,1)S(1)}, bf16[128,2048]{1,0:T(8,128)(2,1)S(1)}, u32[]{:S(2)}, u32[]{:S(2)}) collective-permute-start(bf16[128,2048]{1,0:T(8,128)(2,1)S(1)} %collective-permute-done.1.far), channel_id=1, source_target_pairs={{0,1},{1,0},{2,3},{3,2},{4,5},{5,4},{6,7},{7,6},{8,9},{9,8},{10,11... | collective-permute-start | bytes 1572872 | tf_op jit(solution)/shard_map/ppermute | solution.py:437
  30.5 7.2 %collective-permute-start.3 = (bf16[384,256]{1,0:T(8,128)(2,1)}, bf16[384,256]{1,0:T(8,128)(2,1)S(1)}, u32[]{:S(2)}, u32[]{:S(2)}) collective-permute-start(bf16[384,256]{1,0:T(8,128)(2,1)} %get-tuple-element.45), channel_id=1, source_target_pairs={{0,1},{1,0},{2,3},{3,2},{4,5},{5,4},{6,7},{7,6},{8,9},{9,8},{10,11... | collective-permute-start | bytes 589832 | tf_op jit(solution)/shard_map/ppermute | solution.py:437
  30.8 6.9 %collective-permute-start.4 = (bf16[384,256]{1,0:T(8,128)(2,1)}, bf16[384,256]{1,0:T(8,128)(2,1)S(1)}, u32[]{:S(2)}, u32[]{:S(2)}) collective-permute-start(bf16[384,256]{1,0:T(8,128)(2,1)} %get-tuple-element.46), channel_id=1, source_target_pairs={{0,32},{32,0},{64,96},{96,64},{128,160},{160,128},{192,224},{224,1... | collective-permute-start | bytes 589832 | tf_op jit(solution)/shard_map/ppermute | solution.py:446
  31.0 11.1 %collective-permute-start.5 = (bf16[384,256]{1,0:T(8,128)(2,1)}, bf16[384,256]{1,0:T(8,128)(2,1)S(1)}, u32[]{:S(2)}, u32[]{:S(2)}) collective-permute-start(bf16[384,256]{1,0:T(8,128)(2,1)} %get-tuple-element.47), channel_id=1, source_target_pairs={{0,33},{1,32},{32,1},{33,0},{64,97},{65,96},{96,65},{97,64},{128,1... | collective-permute-start | bytes 589832 | tf_op jit(solution)/shard_map/ppermute | solution.py:442
  32.6 0.8 copy-start.13
  32.6 1.0 copy-start.14
  37.7 7.1 %copy-start.8 = (bf16[384,256]{1,0:T(8,128)(2,1)}, bf16[384,256]{1,0:T(8,128)(2,1)S(1)}, u32[]{:S(2)}) copy-start(bf16[384,256]{1,0:T(8,128)(2,1)S(1)} %collective-permute-done.3.from_c) | copy-start | bytes 589828
  37.7 7.1 %copy-start.9 = (bf16[384,256]{1,0:T(8,128)(2,1)}, bf16[384,256]{1,0:T(8,128)(2,1)S(1)}, u32[]{:S(2)}) copy-start(bf16[384,256]{1,0:T(8,128)(2,1)S(1)} %collective-permute-done.4.from_z) | copy-start | bytes 589828
  42.1 2.7 %copy-start.10 = (bf16[384,256]{1,0:T(8,128)(2,1)}, bf16[384,256]{1,0:T(8,128)(2,1)S(1)}, u32[]{:S(2)}) copy-start(bf16[384,256]{1,0:T(8,128)(2,1)S(1)} %collective-permute-done.5.from_cz) | copy-start | bytes 589828
  44.8 1.0 copy-start.4
  50.4 23.9 %collective-permute-start.6 = (bf16[16,128,256]{2,1,0:T(8,128)(2,1)}, bf16[16,128,256]{2,1,0:T(8,128)(2,1)S(1)}, u32[]{:S(2)}, u32[]{:S(2)}) collective-permute-start(bf16[16,128,256]{2,1,0:T(8,128)(2,1)} %get-tuple-element.58.w_all), channel_id=1, source_target_pairs={{0,32},{32,0},{64,96},{96,64},{128,160},{160,128},{192,224},{224,1... | collective-permute-start | bytes 3145736 | tf_op jit(solution)/shard_map/ppermute | solution.py:446
  63.4 10.9 %all-to-all-start.3 = ((bf16[16,64,128]{2,1,0:T(8,128)(2,1)}), bf16[16,64,128]{2,1,0:T(8,128)(2,1)S(1)}, u32[]{:S(2)}, u32[]{:S(2)}) async-start(bf16[16,64,128]{2,1,0:T(8,128)(2,1)} %scan.1), calls=%async_computation.3 | async-start | bytes 524288 | tf_op jit(solution)/shard_map/all_to_all | solution.py:450
  74.4 0.7 copy-start.7
  74.4 1.1 copy-start.5
  80.2 5.3 %collective-permute-start.10 = (f32[16,512]{1,0:T(8,128)}, f32[16,512]{1,0:T(8,128)S(1)}, u32[]{:S(2)}, u32[]{:S(2)}) collective-permute-start(f32[16,512]{1,0:T(8,128)} %get-tuple-element.62.lat_a), channel_id=1, source_target_pairs={{0,32},{32,0},{64,96},{96,64},{128,160},{160,128},{192,224},{224,1... | collective-permute-start | bytes 98312 | tf_op jit(solution)/shard_map/ppermute | solution.py:446
  81.4 6.1 %collective-permute-start.11 = (f32[16,512]{1,0:T(8,128)}, f32[16,512]{1,0:T(8,128)S(1)}, u32[]{:S(2)}, u32[]{:S(2)}) collective-permute-start(f32[16,512]{1,0:T(8,128)} %get-tuple-element.62.lat_a), channel_id=1, source_target_pairs={{0,33},{1,32},{32,1},{33,0},{64,97},{65,96},{96,65},{97,64},{128,1... | collective-permute-start | bytes 98312 | tf_op jit(solution)/shard_map/ppermute | solution.py:442
  85.4 2.2 %collective-permute-start.9 = (f32[16,512]{1,0:T(8,128)}, f32[16,512]{1,0:T(8,128)S(1)}, u32[]{:S(2)}, u32[]{:S(2)}) collective-permute-start(f32[16,512]{1,0:T(8,128)} %get-tuple-element.62.lat_a), channel_id=1, source_target_pairs={{0,1},{1,0},{2,3},{3,2},{4,5},{5,4},{6,7},{7,6},{8,9},{9,8},{10,11... | collective-permute-start | bytes 98312 | tf_op jit(solution)/shard_map/ppermute | solution.py:437
  85.5 2.1 %copy-start.16 = (f32[16,512]{1,0:T(8,128)}, f32[16,512]{1,0:T(8,128)S(1)}, u32[]{:S(2)}) copy-start(f32[16,512]{1,0:T(8,128)S(1)} %collective-permute-done.10.lat_z) | copy-start | bytes 98308
  87.5 0.6 copy-start.17
  87.5 0.6 copy-start.18
  91.8 4.3 %copy-start.6 = (bf16[512,256]{1,0:T(8,128)(2,1)S(1)}, bf16[512,256]{1,0:T(8,128)(2,1)}, u32[]{:S(2)}) copy-start(bf16[512,256]{1,0:T(8,128)(2,1)} %get-tuple-element.59.kd_r) | copy-start | bytes 786436
  91.8 24.5 %all-to-all-start.4 = ((bf16[16,16,2816]{2,1,0:T(8,128)(2,1)}), bf16[16,16,2816]{2,1,0:T(8,128)(2,1)S(1)}, u32[]{:S(2)}, u32[]{:S(2)}) async-start(bf16[16,16,2816]{2,1,0:T(8,128)(2,1)} %get-tuple-element.72), calls=%async_computation.4 | async-start | bytes 2883584 | tf_op jit(solution)/shard_map/all_to_all | solution.py:450
  96.1 11.9 %copy-start.2 = (bf16[512,256]{1,0:T(8,128)(2,1)S(1)}, bf16[512,256]{1,0:T(8,128)(2,1)}, u32[]{:S(2)}) copy-start(bf16[512,256]{1,0:T(8,128)(2,1)} %get-tuple-element.65.gate) | copy-start | bytes 786436
  96.8 17.1 %copy-start.1 = (bf16[16,2048]{1,0:T(8,128)(2,1)S(1)}, bf16[16,2048]{1,0:T(8,128)(2,1)}, u32[]{:S(2)}) copy-start(bf16[16,2048]{1,0:T(8,128)(2,1)} %down.3) | copy-start | bytes 196612
  96.8 17.1 %copy-start.3 = (bf16[16,128]{1,0:T(8,128)(2,1)S(1)}, bf16[16,128]{1,0:T(8,128)(2,1)}, u32[]{:S(2)}) copy-start(bf16[16,128]{1,0:T(8,128)(2,1)} %get-tuple-element.64.lat) | copy-start | bytes 12292
  96.8 3.9 %collective-permute-start.7 = (bf16[256,256]{1,0:T(8,128)(2,1)S(1)}, bf16[256,256]{1,0:T(8,128)(2,1)S(1)}, u32[]{:S(2)}, u32[]{:S(2)}) collective-permute-start(bf16[256,256]{1,0:T(8,128)(2,1)S(1)} %get-tuple-element.79), channel_id=1, source_target_pairs={{0,32},{32,0},{64,96},{96,64},{128,160},{160,128},{192,224},{224,1... | collective-permute-start | bytes 393224 | tf_op jit(solution)/shard_map/ppermute | solution.py:446
  100.7 0.7 copy-start.15
  105.1 8.8 %collective-permute-start.8 = (f32[128,2048]{1,0:T(8,128)}, f32[128,2048]{1,0:T(8,128)S(1)}, u32[]{:S(2)}, u32[]{:S(2)}) collective-permute-start(f32[128,2048]{1,0:T(8,128)} %get-tuple-element.61), channel_id=1, source_target_pairs={{0,1},{1,0},{2,3},{3,2},{4,5},{5,4},{6,7},{7,6},{8,9},{9,8},{10,11... | collective-permute-start | bytes 3145736 | tf_op jit(solution)/shard_map/ppermute | solution.py:437
  108.0 2.2 %collective-permute-start.12 = (bf16[128,256]{1,0:T(8,128)(2,1)S(1)}, bf16[128,256]{1,0:T(8,128)(2,1)S(1)}, u32[]{:S(2)}, u32[]{:S(2)}) collective-permute-start(bf16[128,256]{1,0:T(8,128)(2,1)S(1)} %get-tuple-element.67), channel_id=1, source_target_pairs={{0,1},{1,0},{2,3},{3,2},{4,5},{5,4},{6,7},{7,6},{8,9},{9,8},{10,11... | collective-permute-start | bytes 196616 | tf_op jit(solution)/shard_map/ppermute | solution.py:437
  108.1 3.5 %collective-permute-start.13 = (bf16[128,256]{1,0:T(8,128)(2,1)S(1)}, bf16[128,256]{1,0:T(8,128)(2,1)S(1)}, u32[]{:S(2)}, u32[]{:S(2)}) collective-permute-start(bf16[128,256]{1,0:T(8,128)(2,1)S(1)} %get-tuple-element.68), channel_id=1, source_target_pairs={{0,32},{32,0},{64,96},{96,64},{128,160},{160,128},{192,224},{224,1... | collective-permute-start | bytes 196616 | tf_op jit(solution)/shard_map/ppermute | solution.py:446
  108.9 5.0 %collective-permute-start.14 = (bf16[128,256]{1,0:T(8,128)(2,1)S(1)}, bf16[128,256]{1,0:T(8,128)(2,1)S(1)}, u32[]{:S(2)}, u32[]{:S(2)}) collective-permute-start(bf16[128,256]{1,0:T(8,128)(2,1)S(1)} %get-tuple-element.69), channel_id=1, source_target_pairs={{0,33},{1,32},{32,1},{33,0},{64,97},{65,96},{96,65},{97,64},{128,1... | collective-permute-start | bytes 196616 | tf_op jit(solution)/shard_map/ppermute | solution.py:442
  113.8 1.2 copy-start
  131.7 5.4 %collective-permute-start.15 = (f32[16,2048]{1,0:T(8,128)S(1)}, f32[16,2048]{1,0:T(8,128)S(1)}, u32[]{:S(2)}, u32[]{:S(2)}) collective-permute-start(f32[16,2048]{1,0:T(8,128)S(1)} %get-tuple-element.75), channel_id=1, source_target_pairs={{0,1},{1,0},{2,3},{3,2},{4,5},{5,4},{6,7},{7,6},{8,9},{9,8},{10,11... | collective-permute-start | bytes 393224 | tf_op jit(solution)/shard_map/ppermute | solution.py:437

commit v8 on v7

--- a/solution.py
+++ b/solution.py
@@ -261,7 +261,9 @@
         run = decay(p) * run + recv[p, ROWS + 16 :].astype(F32)
 
 
-def inner_body(mine, from_c, from_z, from_cz, key_r, beta, kd_o, local, q_r, g_r, v_r, adds):
+def inner_body(mine, from_c, from_z, from_cz, key_r, beta, logit,
+               kd_o, local, q_r, g_r, v_r, adds, slope):
+    slope[...] = 1.0 / (1.0 + jnp.exp(logit[...])) * (1.0 / 16.0)
     low, high = low_mask()
     for i, out in enumerate((q_r, g_r, v_r)):
         rows = slice(i * TOK, (i + 1) * TOK)
@@ -296,7 +298,7 @@
     ]
 
 
-def gate_body(recv, adds, key_r, v_r, beta, q_r, g_r, kd_in, local, logit, lat, up, _,
+def gate_body(recv, adds, key_r, v_r, beta, q_r, g_r, kd_in, local, slope, lat, up, _,
               kd_o, gate_o, up_part, lat_part, delta):
     first, odd = is_first(), odd_z()
     high = low_mask()[1].astype(BF16)
@@ -332,8 +334,7 @@
             r = rows_of(seq, n)
             suffix = dot_mask(high, delta[r]) + beyond
             beyond = suffix[:1]
-            x = logit[r]
-            gate_o[r] = (suffix * (1.0 / (1.0 + jnp.exp(x))) * (1.0 / 16.0)).astype(BF16)
+            gate_o[r] = (suffix * slope[r]).astype(BF16)
     gate = gate_o[...]
     up_part[...] = dot(lat[...], gate, TN)
     lat_part[...] = dot(quarter_of(up, first, odd), gate, NT)
@@ -480,17 +481,17 @@
     )(w_all, tok, beta, *parts)
     w_far = across(w_all)
     recv = a2a(send, XY)
-    kd_local, local_part, q, g, v, add_g = kernel(
-        inner_body, (quad_f, quad_f, quad_bf, quad_bf, quad_bf, shape((BLOCKS, WIDTH, DK))),
+    kd_local, local_part, q, g, v, add_g, slope = kernel(
+        inner_body, (quad_f, quad_f, quad_bf, quad_bf, quad_bf, shape((BLOCKS, WIDTH, DK)), quad_f),
         "inner", BIG,
-    )(*parts, keys, beta)
+    )(*parts, keys, beta, logit)
     recv = a2a(kernel(scan_body, shape((PS, 2 * ROWS, DK), BF16), "scan", 8)(recv), XY)
     kd, gate, up_part, lat_part = kernel(
         gate_body,
         (quad_bf, quad_bf, shape((RANK, QUART)), shape((RANK, QUAD))),
         "gate", BIG, specs=[VM] * 12 + [HBM], out_specs=(VM,) * 4,
         scratch=[pltpu.VMEM((QUAD, QUART), F32)],
-    )(recv, add_g, keys, v, beta, q, g, kd_local, local_part, logit, lat, gate_up, w_far)
+    )(recv, add_g, keys, v, beta, q, g, kd_local, local_part, slope, lat, gate_up, w_far)
     lat_own, send = kernel(
         weight_body, (shape((RANK, TOK), BF16), shape((PS, 16, SMALL + ZS * QUART), BF16)),
         "weights", BIG,

time: 139 us -> 139 us (level)
  no operation moved by 1% of the time
where the time goes in v8:
time: 139 us; the launch traced here: 138 us
  starting transfers between devices  45.3 us (33%)
  Pallas kernels  31.8 us (23%)
  blocking collectives  27.3 us (20%)
  waiting for transfers between devices  24.3 us (17%)
  local copies, waits for them, and re-layouts  8.64 us (6%)
    all_to_all x2, blocking collectives, a2a(): return lax.all_to_all(a, axis, 0, 0)  27.3 us
    all_to_all x4, starting transfers between devices, a2a(): return lax.all_to_all(a, axis, 0, 0)  24.8 us
    all_to_all x4, waiting for transfers between devices, a2a(): return lax.all_to_all(a, axis, 0, 0)  10.8 us
    ppermute x3, waiting for transfers between devices, cross(): return lax.ppermute(a, ('z', 'c'), pairs)  8.78 us
    ppermute x7, starting transfers between devices, swap(): return lax.ppermute(a, 'c', SWAP)  8.31 us
    ppermute x3, starting transfers between devices, cross(): return lax.ppermute(a, ('z', 'c'), pairs)  6.87 us
    pallas_call x1, Pallas kernels, local(): kernel(inner_body, (quad_f, quad_f, quad_bf, quad_bf, quad_bf, shape((BLO...  5.96 us
    unnamed x38, local copies, waits for them, and re-layouts  5.54 us
  transfers between devices with their start and end apart: 20, of which 9 were waited for; matrix products, arithmetic and copies ran while one was open for 1% of the time, Pallas kernels for 13%

profile of v8, /device:TPU:1, one launch (start us, length us, event | category | flops | bytes accessed | tf_op | source)
XLA Modules:
  0.0 138.1 jit_solution(5709220654874461901)
XLA Ops:
  0.6 0.7 copy.14
  1.4 0.6 broadcast_in_dim.24
  2.0 10.0 %all-to-all-start = ((bf16[16,8,256]{2,1,0:T(8,128)(2,1)}), bf16[16,8,256]{2,1,0:T(8,128)(2,1)S(1)}, u32[]{:S(2)}, u32[]{:S(2)}) async-start(bf16[16,8,256]{2,1,0:T(8,128)(2,1)} %bitcast.3), calls=%async_computation | async-start | bytes 131072 | tf_op jit(solution)/shard_map/all_to_all | solution.py:451
  12.0 1.4 %collective-permute-start.1 = (bf16[128,2048]{1,0:T(8,128)(2,1)}, bf16[128,2048]{1,0:T(8,128)(2,1)S(1)}, u32[]{:S(2)}, u32[]{:S(2)}) collective-permute-start(bf16[128,2048]{1,0:T(8,128)(2,1)} %bitcast.14), channel_id=1, source_target_pairs={{0,32},{32,0},{64,96},{96,64},{128,160},{160,128},{192,224},{224,1... | collective-permute-start | bytes 1572872 | tf_op jit(solution)/shard_map/ppermute | solution.py:447
  13.4 6.7 %all-to-all-done = bf16[16,8,256]{2,1,0:T(8,128)(2,1)S(1)} async-done(((bf16[16,8,256]{2,1,0:T(8,128)(2,1)}), bf16[16,8,256]{2,1,0:T(8,128)(2,1)S(1)}, u32[]{:S(2)}, u32[]{:S(2)}) %all-to-all-start) | async-done | bytes 65568 | tf_op jit(solution)/shard_map/all_to_all | solution.py:451
  20.0 1.1 broadcast_in_dim.26
  21.1 6.8 %all-to-all-start.1 = ((bf16[16,128,256]{2,1,0:T(8,128)(2,1)}), bf16[16,128,256]{2,1,0:T(8,128)(2,1)S(1)}, u32[]{:S(2)}, u32[]{:S(2)}) async-start(bf16[16,128,256]{2,1,0:T(8,128)(2,1)} %broadcast_in_dim.26), calls=%async_computation.1 | async-start | bytes 2097152 | tf_op jit(solution)/shard_map/all_to_all | solution.py:451
  27.9 0.4 collective-permute-start
  28.2 0.0 collective-permute-done.1.far
  28.2 0.2 collective-permute-start.2
  28.5 2.0 %prep.1 = (bf16[384,256]{1,0:T(8,128)(2,1)}, bf16[384,256]{1,0:T(8,128)(2,1)}, bf16[384,256]{1,0:T(8,128)(2,1)}, bf16[384,256]{1,0:T(8,128)(2,1)}) custom-call(bf16[128,1024]{1,0:T(8,128)(2,1)} %bitcast.17, bf16[128,1024]{1,0:T(8,128)(2,1)} %bitcast.18, bf16[128,1024]{1,0:T(8,128)(2,1)} %bitcast.19), custom_call_target="tpu_custom_call" | custom-call | tf_op jit(solution)/shard_map/prep/pallas_call | solution.py:462
  30.5 0.3 collective-permute-start.3
  30.8 0.2 collective-permute-start.4
  31.0 1.6 %collective-permute-start.5 = (bf16[384,256]{1,0:T(8,128)(2,1)}, bf16[384,256]{1,0:T(8,128)(2,1)S(1)}, u32[]{:S(2)}, u32[]{:S(2)}) collective-permute-start(bf16[384,256]{1,0:T(8,128)(2,1)} %get-tuple-element.48), channel_id=1, source_target_pairs={{0,33},{1,32},{32,1},{33,0},{64,97},{65,96},{96,65},{97,64},{128,1... | collective-permute-start | bytes 589832 | tf_op jit(solution)/shard_map/ppermute | solution.py:443
  32.6 0.0 collective-permute-done.peer
  32.6 0.0 collective-permute-done.2.far_peer
  32.7 0.8 copy-done.13
  33.4 0.2 copy-done.14
  33.6 4.0 %gates.1 = (bf16[512,2048]{1,0:T(8,128)(2,1)}, bf16[512,16]{1,0:T(8,128)(2,1)}, f32[512,256]{1,0:T(8,128)}, f32[512,256]{1,0:T(8,128)}) custom-call(bf16[128,2048]{1,0:T(8,128)(2,1)} %bitcast.15, bf16[128,2048]{1,0:T(8,128)(2,1)} %copy-done.13, bf16[128,2048]{1,0:T(8,128)(2,1)} %copy-done.12, bf16[128,2048]{1,0:T(8,128)(2,1)} %copy-done.14, ...), custom_call_target="tpu_custom_call" | custom-call | tf_op jit(solution)/shard_map/gates/pallas_call | solution.py:468
  37.7 0.0 collective-permute-done.3.from_c
  37.7 0.0 collective-permute-done.4.from_z
  37.7 4.4 %collective-permute-done.5.from_cz = bf16[384,256]{1,0:T(8,128)(2,1)S(1)} collective-permute-done((bf16[384,256]{1,0:T(8,128)(2,1)}, bf16[384,256]{1,0:T(8,128)(2,1)S(1)}, u32[]{:S(2)}, u32[]{:S(2)}) %collective-permute-start.5) | collective-permute-done | bytes 196640 | tf_op jit(solution)/shard_map/ppermute | solution.py:443
  42.1 2.7 %all-to-all-done.1.recv_h = bf16[16,128,256]{2,1,0:T(8,128)(2,1)S(1)} async-done(((bf16[16,128,256]{2,1,0:T(8,128)(2,1)}), bf16[16,128,256]{2,1,0:T(8,128)(2,1)S(1)}, u32[]{:S(2)}, u32[]{:S(2)}) %all-to-all-start.1) | async-done | bytes 1048608 | tf_op jit(solution)/shard_map/all_to_all | solution.py:451
  44.8 0.9 copy-done.4
  45.8 4.7 %keys.1 = (bf16[512,256]{1,0:T(8,128)(2,1)}, bf16[16,80,128]{2,1,0:T(8,128)(2,1)}, bf16[16,128,256]{2,1,0:T(8,128)(2,1)}) custom-call(bf16[16,128,256]{2,1,0:T(8,128)(2,1)} %copy-done.4, bf16[512,2048]{1,0:T(8,128)(2,1)} %get-tuple-element.43.tok_h.tok, f32[512,256]{1,0:T(8,128)} %get-tuple-element.44.beta_h.beta, ...), custom_call_target="tpu_custom_call", output_to_operand_aliasing={{2}: (0, {})} | custom-call | tf_op jit(solution)/shard_map/keys/pallas_call | solution.py:473
  50.4 0.1 collective-permute-start.6
  50.5 12.1 %all_to_all.30.recv = bf16[16,80,128]{2,1,0:T(8,128)(2,1)S(1)} all-to-all(bf16[16,80,128]{2,1,0:T(8,128)(2,1)} %get-tuple-element.49), channel_id=1, replica_groups=mesh['z'=8,'x'=4,'y'=4,'c'=2] {'x','y'}, dimensions={0} | all-to-all | bytes 655360 | tf_op jit(solution)/shard_map/all_to_all | solution.py:451
  62.7 0.8 scan.1
  63.5 3.5 %all-to-all-start.3 = ((bf16[16,64,128]{2,1,0:T(8,128)(2,1)}), bf16[16,64,128]{2,1,0:T(8,128)(2,1)S(1)}, u32[]{:S(2)}, u32[]{:S(2)}) async-start(bf16[16,64,128]{2,1,0:T(8,128)(2,1)} %scan.1), calls=%async_computation.3 | async-start | bytes 524288 | tf_op jit(solution)/shard_map/all_to_all | solution.py:451
  67.0 6.0 %inner.1 = (f32[512,256]{1,0:T(8,128)}, f32[512,256]{1,0:T(8,128)}, bf16[512,256]{1,0:T(8,128)(2,1)}, bf16[512,256]{1,0:T(8,128)(2,1)}, bf16[512,256]{1,0:T(8,12...) custom-call(bf16[384,256]{1,0:T(8,128)(2,1)} %get-tuple-element.45.mine, bf16[384,256]{1,0:T(8,128)(2,1)} %copy-done.8, ...), custom_call_target="tpu_custom_call" | custom-call | tf_op jit(solution)/shard_map/inner/pallas_call | solution.py:484
  73.0 1.5 %all-to-all-done.3.recv = bf16[16,64,128]{2,1,0:T(8,128)(2,1)S(1)} async-done(((bf16[16,64,128]{2,1,0:T(8,128)(2,1)}), bf16[16,64,128]{2,1,0:T(8,128)(2,1)S(1)}, u32[]{:S(2)}, u32[]{:S(2)}) %all-to-all-start.3) | async-done | bytes 262176 | tf_op jit(solution)/shard_map/all_to_all | solution.py:451
  74.4 0.0 collective-permute-done.6._.far_all
  74.4 0.7 copy-done.7
  75.2 0.4 copy-done.5
  75.5 4.7 %gate.1 = (bf16[512,256]{1,0:T(8,128)(2,1)}, bf16[512,256]{1,0:T(8,128)(2,1)}, f32[16,256]{1,0:T(8,128)}, f32[16,512]{1,0:T(8,128)}) custom-call(bf16[16,64,128]{2,1,0:T(8,128)(2,1)} %copy-done.7, f32[4,512,128]{2,1,0:T(8,128)} %get-tuple-element.52.adds, bf16[512,256]{1,0:T(8,128)(2,1)} %get-tuple-element.50.key_r, bf16[512,256]{1,0:T(8,128)(2,1)} %get-tuple-element.53.v_r, ...), custom_call_target="tpu_custom_call" | custom-call | tf_op jit(solution)/shard_map/gate/pallas_call | solution.py:489
  80.3 1.2 collective-permute-start.10
  81.5 3.9 %collective-permute-start.11 = (f32[16,512]{1,0:T(8,128)}, f32[16,512]{1,0:T(8,128)S(1)}, u32[]{:S(2)}, u32[]{:S(2)}) collective-permute-start(f32[16,512]{1,0:T(8,128)} %get-tuple-element.64.lat_a), channel_id=1, source_target_pairs={{0,33},{1,32},{32,1},{33,0},{64,97},{65,96},{96,65},{97,64},{128,1... | collective-permute-start | bytes 98312 | tf_op jit(solution)/shard_map/ppermute | solution.py:443
  85.4 0.1 collective-permute-start.9
  85.5 0.0 collective-permute-done.10.lat_z
  85.5 2.1 %collective-permute-done.11.lat_cz = f32[16,512]{1,0:T(8,128)S(1)} collective-permute-done((f32[16,512]{1,0:T(8,128)}, f32[16,512]{1,0:T(8,128)S(1)}, u32[]{:S(2)}, u32[]{:S(2)}) %collective-permute-start.11) | collective-permute-done | bytes 32800 | tf_op jit(solution)/shard_map/ppermute | solution.py:443
  87.6 0.0 collective-permute-done.9.lat_c
  87.6 0.6 copy-done.17
  88.2 0.0 copy-done.18
  88.2 3.7 %weights.1 = (bf16[16,128]{1,0:T(8,128)(2,1)}, bf16[16,16,2816]{2,1,0:T(8,128)(2,1)}) custom-call(f32[16,512]{1,0:T(8,128)} %get-tuple-element.64.lat_a, f32[16,512]{1,0:T(8,128)} %copy-done.18, f32[16,512]{1,0:T(8,128)} %copy-done.16, f32[16,512]{1,0:T(8,128)} %copy-done.17, f32[16,256]{1,0:T(8,128)} %get-tuple-element.65.up_part, ...), custom_call_target="tpu_custom_call" | custom-call | tf_op jit(solution)/shard_map/weights/pallas_call | solution.py:495
  91.9 4.6 %all-to-all-start.4 = ((bf16[16,16,2816]{2,1,0:T(8,128)(2,1)}), bf16[16,16,2816]{2,1,0:T(8,128)(2,1)S(1)}, u32[]{:S(2)}, u32[]{:S(2)}) async-start(bf16[16,16,2816]{2,1,0:T(8,128)(2,1)} %get-tuple-element.74), calls=%async_computation.4 | async-start | bytes 2883584 | tf_op jit(solution)/shard_map/all_to_all | solution.py:451
  96.4 0.7 fusion
  97.1 1.5 %collective-permute-start.7 = (bf16[256,256]{1,0:T(8,128)(2,1)S(1)}, bf16[256,256]{1,0:T(8,128)(2,1)S(1)}, u32[]{:S(2)}, u32[]{:S(2)}) collective-permute-start(bf16[256,256]{1,0:T(8,128)(2,1)S(1)} %get-tuple-element.81), channel_id=1, source_target_pairs={{0,32},{32,0},{64,96},{96,64},{128,160},{160,128},{192,224},{224,1... | collective-permute-start | bytes 393224 | tf_op jit(solution)/shard_map/ppermute | solution.py:447
  98.6 2.4 %collective-permute-done.7.kd_far = bf16[256,256]{1,0:T(8,128)(2,1)S(1)} collective-permute-done((bf16[256,256]{1,0:T(8,128)(2,1)S(1)}, bf16[256,256]{1,0:T(8,128)(2,1)S(1)}, u32[]{:S(2)}, u32[]{:S(2)}) %collective-permute-start.7) | collective-permute-done | bytes 131104 | tf_op jit(solution)/shard_map/ppermute | solution.py:447
  101.0 0.7 copy-done.15
  101.7 3.8 %through.1 = (f32[128,2048]{1,0:T(8,128)}, f32[128,2048]{1,0:T(8,128)}) custom-call(bf16[256,256]{1,0:T(8,128)(2,1)} %get-tuple-element.82.kd, bf16[256,256]{1,0:T(8,128)(2,1)} %copy-done.15, bf16[16,128,256]{2,1,0:T(8,128)(2,1)} %get-tuple-element.60.w_all, bf16[16,128,256]{2,1,0:T(8,128)(2,1)} %copy-done.5), custom_call_target="tpu_custom_call" | custom-call | tf_op jit(solution)/shard_map/through/pallas_call | solution.py:499
  105.4 2.8 %collective-permute-start.8 = (f32[128,2048]{1,0:T(8,128)}, f32[128,2048]{1,0:T(8,128)S(1)}, u32[]{:S(2)}, u32[]{:S(2)}) collective-permute-start(f32[128,2048]{1,0:T(8,128)} %get-tuple-element.63), channel_id=1, source_target_pairs={{0,1},{1,0},{2,3},{3,2},{4,5},{5,4},{6,7},{7,6},{8,9},{9,8},{10,11... | collective-permute-start | bytes 3145736 | tf_op jit(solution)/shard_map/ppermute | solution.py:438
  108.3 0.1 collective-permute-start.12
  108.4 0.8 collective-permute-start.13
  109.2 1.3 collective-permute-start.14
  110.5 1.4 collective-permute-done.13.gate_z
  111.9 2.3 %collective-permute-done.14.gate_cz = bf16[128,256]{1,0:T(8,128)(2,1)S(1)} collective-permute-done((bf16[128,256]{1,0:T(8,128)(2,1)S(1)}, bf16[128,256]{1,0:T(8,128)(2,1)S(1)}, u32[]{:S(2)}, u32[]{:S(2)}) %collective-permute-start.14) | collective-permute-done | bytes 65568 | tf_op jit(solution)/shard_map/ppermute | solution.py:443
  114.2 0.0 collective-permute-done.8.got
  114.2 1.2 copy-done
  115.4 1.2 input.1
  116.7 0.2 plane.1
  116.8 15.1 %all_to_all.31.recv = bf16[8,16,1024]{2,1,0:T(8,128)(2,1)S(1)} all-to-all(bf16[8,16,1024]{2,1,0:T(8,128)(2,1)S(1)} %plane.1), channel_id=1, replica_groups=mesh['z'=8,'x'=4,'y'=4,'c'=2] {'z'}, dimensions={0} | all-to-all | bytes 524288 | tf_op jit(solution)/shard_map/all_to_all | solution.py:451
  132.0 4.4 %collective-permute-start.15 = (f32[16,2048]{1,0:T(8,128)S(1)}, f32[16,2048]{1,0:T(8,128)S(1)}, u32[]{:S(2)}, u32[]{:S(2)}) collective-permute-start(f32[16,2048]{1,0:T(8,128)S(1)} %get-tuple-element.77), channel_id=1, source_target_pairs={{0,1},{1,0},{2,3},{3,2},{4,5},{5,4},{6,7},{7,6},{8,9},{9,8},{10,11... | collective-permute-start | bytes 393224 | tf_op jit(solution)/shard_map/ppermute | solution.py:438
  136.4 1.0 collective-permute-done.15.theirs
  137.4 0.7 grads.1
  (33 shorter events, 0.1 us)
Async XLA Ops:
  2.0 18.0 %all-to-all-start = ((bf16[16,8,256]{2,1,0:T(8,128)(2,1)}), bf16[16,8,256]{2,1,0:T(8,128)(2,1)S(1)}, u32[]{:S(2)}, u32[]{:S(2)}) async-start(bf16[16,8,256]{2,1,0:T(8,128)(2,1)} %bitcast.3), calls=%async_computation | async-start | bytes 131072 | tf_op jit(solution)/shard_map/all_to_all | solution.py:451
  12.0 16.3 %collective-permute-start.1 = (bf16[128,2048]{1,0:T(8,128)(2,1)}, bf16[128,2048]{1,0:T(8,128)(2,1)S(1)}, u32[]{:S(2)}, u32[]{:S(2)}) collective-permute-start(bf16[128,2048]{1,0:T(8,128)(2,1)} %bitcast.14), channel_id=1, source_target_pairs={{0,32},{32,0},{64,96},{96,64},{128,160},{160,128},{192,224},{224,1... | collective-permute-start | bytes 1572872 | tf_op jit(solution)/shard_map/ppermute | solution.py:447
  20.0 7.8 %copy-start.11 = (bf16[1,128,2048]{2,1,0:T(8,128)(2,1)S(1)}, bf16[1,128,2048]{2,1,0:T(8,128)(2,1)}, u32[]{:S(2)}) copy-start(bf16[1,128,2048]{2,1,0:T(8,128)(2,1)} %param.8) | copy-start | bytes 1572868
  21.1 23.7 %all-to-all-start.1 = ((bf16[16,128,256]{2,1,0:T(8,128)(2,1)}), bf16[16,128,256]{2,1,0:T(8,128)(2,1)S(1)}, u32[]{:S(2)}, u32[]{:S(2)}) async-start(bf16[16,128,256]{2,1,0:T(8,128)(2,1)} %broadcast_in_dim.26), calls=%async_computation.1 | async-start | bytes 2097152 | tf_op jit(solution)/shard_map/all_to_all | solution.py:451
  27.9 4.8 %collective-permute-start = (bf16[128,2048]{1,0:T(8,128)(2,1)S(1)}, bf16[128,2048]{1,0:T(8,128)(2,1)S(1)}, u32[]{:S(2)}, u32[]{:S(2)}) collective-permute-start(bf16[128,2048]{1,0:T(8,128)(2,1)S(1)} %bitcast.16), channel_id=1, source_target_pairs={{0,1},{1,0},{2,3},{3,2},{4,5},{5,4},{6,7},{7,6},{8,9},{9,8},{10,11... | collective-permute-start | bytes 1572872 | tf_op jit(solution)/shard_map/ppermute | solution.py:438
  28.2 4.4 %copy-start.12 = (bf16[128,2048]{1,0:T(8,128)(2,1)}, bf16[128,2048]{1,0:T(8,128)(2,1)S(1)}, u32[]{:S(2)}) copy-start(bf16[128,2048]{1,0:T(8,128)(2,1)S(1)} %collective-permute-done.1.far) | copy-start | bytes 1572868
  28.2 4.4 %collective-permute-start.2 = (bf16[128,2048]{1,0:T(8,128)(2,1)S(1)}, bf16[128,2048]{1,0:T(8,128)(2,1)S(1)}, u32[]{:S(2)}, u32[]{:S(2)}) collective-permute-start(bf16[128,2048]{1,0:T(8,128)(2,1)S(1)} %collective-permute-done.1.far), channel_id=1, source_target_pairs={{0,1},{1,0},{2,3},{3,2},{4,5},{5,4},{6,7},{7,6},{8,9},{9,8},{10,11... | collective-permute-start | bytes 1572872 | tf_op jit(solution)/shard_map/ppermute | solution.py:438
  30.5 7.2 %collective-permute-start.3 = (bf16[384,256]{1,0:T(8,128)(2,1)}, bf16[384,256]{1,0:T(8,128)(2,1)S(1)}, u32[]{:S(2)}, u32[]{:S(2)}) collective-permute-start(bf16[384,256]{1,0:T(8,128)(2,1)} %get-tuple-element.46), channel_id=1, source_target_pairs={{0,1},{1,0},{2,3},{3,2},{4,5},{5,4},{6,7},{7,6},{8,9},{9,8},{10,11... | collective-permute-start | bytes 589832 | tf_op jit(solution)/shard_map/ppermute | solution.py:438
  30.8 6.9 %collective-permute-start.4 = (bf16[384,256]{1,0:T(8,128)(2,1)}, bf16[384,256]{1,0:T(8,128)(2,1)S(1)}, u32[]{:S(2)}, u32[]{:S(2)}) collective-permute-start(bf16[384,256]{1,0:T(8,128)(2,1)} %get-tuple-element.47), channel_id=1, source_target_pairs={{0,32},{32,0},{64,96},{96,64},{128,160},{160,128},{192,224},{224,1... | collective-permute-start | bytes 589832 | tf_op jit(solution)/shard_map/ppermute | solution.py:447
  31.0 11.1 %collective-permute-start.5 = (bf16[384,256]{1,0:T(8,128)(2,1)}, bf16[384,256]{1,0:T(8,128)(2,1)S(1)}, u32[]{:S(2)}, u32[]{:S(2)}) collective-permute-start(bf16[384,256]{1,0:T(8,128)(2,1)} %get-tuple-element.48), channel_id=1, source_target_pairs={{0,33},{1,32},{32,1},{33,0},{64,97},{65,96},{96,65},{97,64},{128,1... | collective-permute-start | bytes 589832 | tf_op jit(solution)/shard_map/ppermute | solution.py:443
  32.6 0.8 copy-start.13
  32.6 1.0 copy-start.14
  37.7 7.1 %copy-start.8 = (bf16[384,256]{1,0:T(8,128)(2,1)}, bf16[384,256]{1,0:T(8,128)(2,1)S(1)}, u32[]{:S(2)}) copy-start(bf16[384,256]{1,0:T(8,128)(2,1)S(1)} %collective-permute-done.3.from_c) | copy-start | bytes 589828
  37.7 7.1 %copy-start.9 = (bf16[384,256]{1,0:T(8,128)(2,1)}, bf16[384,256]{1,0:T(8,128)(2,1)S(1)}, u32[]{:S(2)}) copy-start(bf16[384,256]{1,0:T(8,128)(2,1)S(1)} %collective-permute-done.4.from_z) | copy-start | bytes 589828
  42.1 2.7 %copy-start.10 = (bf16[384,256]{1,0:T(8,128)(2,1)}, bf16[384,256]{1,0:T(8,128)(2,1)S(1)}, u32[]{:S(2)}) copy-start(bf16[384,256]{1,0:T(8,128)(2,1)S(1)} %collective-permute-done.5.from_cz) | copy-start | bytes 589828
  44.8 1.0 copy-start.4
  50.4 24.0 %collective-permute-start.6 = (bf16[16,128,256]{2,1,0:T(8,128)(2,1)}, bf16[16,128,256]{2,1,0:T(8,128)(2,1)S(1)}, u32[]{:S(2)}, u32[]{:S(2)}) collective-permute-start(bf16[16,128,256]{2,1,0:T(8,128)(2,1)} %get-tuple-element.60.w_all), channel_id=1, source_target_pairs={{0,32},{32,0},{64,96},{96,64},{128,160},{160,128},{192,224},{224,1... | collective-permute-start | bytes 3145736 | tf_op jit(solution)/shard_map/ppermute | solution.py:447
  63.5 11.0 %all-to-all-start.3 = ((bf16[16,64,128]{2,1,0:T(8,128)(2,1)}), bf16[16,64,128]{2,1,0:T(8,128)(2,1)S(1)}, u32[]{:S(2)}, u32[]{:S(2)}) async-start(bf16[16,64,128]{2,1,0:T(8,128)(2,1)} %scan.1), calls=%async_computation.3 | async-start | bytes 524288 | tf_op jit(solution)/shard_map/all_to_all | solution.py:451
  74.4 0.7 copy-start.7
  74.4 1.1 copy-start.5
  80.3 5.2 %collective-permute-start.10 = (f32[16,512]{1,0:T(8,128)}, f32[16,512]{1,0:T(8,128)S(1)}, u32[]{:S(2)}, u32[]{:S(2)}) collective-permute-start(f32[16,512]{1,0:T(8,128)} %get-tuple-element.64.lat_a), channel_id=1, source_target_pairs={{0,32},{32,0},{64,96},{96,64},{128,160},{160,128},{192,224},{224,1... | collective-permute-start | bytes 98312 | tf_op jit(solution)/shard_map/ppermute | solution.py:447
  81.5 6.1 %collective-permute-start.11 = (f32[16,512]{1,0:T(8,128)}, f32[16,512]{1,0:T(8,128)S(1)}, u32[]{:S(2)}, u32[]{:S(2)}) collective-permute-start(f32[16,512]{1,0:T(8,128)} %get-tuple-element.64.lat_a), channel_id=1, source_target_pairs={{0,33},{1,32},{32,1},{33,0},{64,97},{65,96},{96,65},{97,64},{128,1... | collective-permute-start | bytes 98312 | tf_op jit(solution)/shard_map/ppermute | solution.py:443
  85.4 2.2 %collective-permute-start.9 = (f32[16,512]{1,0:T(8,128)}, f32[16,512]{1,0:T(8,128)S(1)}, u32[]{:S(2)}, u32[]{:S(2)}) collective-permute-start(f32[16,512]{1,0:T(8,128)} %get-tuple-element.64.lat_a), channel_id=1, source_target_pairs={{0,1},{1,0},{2,3},{3,2},{4,5},{5,4},{6,7},{7,6},{8,9},{9,8},{10,11... | collective-permute-start | bytes 98312 | tf_op jit(solution)/shard_map/ppermute | solution.py:438
  85.5 2.1 %copy-start.16 = (f32[16,512]{1,0:T(8,128)}, f32[16,512]{1,0:T(8,128)S(1)}, u32[]{:S(2)}) copy-start(f32[16,512]{1,0:T(8,128)S(1)} %collective-permute-done.10.lat_z) | copy-start | bytes 98308
  87.6 0.6 copy-start.17
  87.6 0.6 copy-start.18
  91.9 4.6 %copy-start.6 = (bf16[512,256]{1,0:T(8,128)(2,1)S(1)}, bf16[512,256]{1,0:T(8,128)(2,1)}, u32[]{:S(2)}) copy-start(bf16[512,256]{1,0:T(8,128)(2,1)} %get-tuple-element.61.kd_r) | copy-start | bytes 786436
  91.9 24.8 %all-to-all-start.4 = ((bf16[16,16,2816]{2,1,0:T(8,128)(2,1)}), bf16[16,16,2816]{2,1,0:T(8,128)(2,1)S(1)}, u32[]{:S(2)}, u32[]{:S(2)}) async-start(bf16[16,16,2816]{2,1,0:T(8,128)(2,1)} %get-tuple-element.74), calls=%async_computation.4 | async-start | bytes 2883584 | tf_op jit(solution)/shard_map/all_to_all | solution.py:451
  96.4 11.8 %copy-start.2 = (bf16[512,256]{1,0:T(8,128)(2,1)S(1)}, bf16[512,256]{1,0:T(8,128)(2,1)}, u32[]{:S(2)}) copy-start(bf16[512,256]{1,0:T(8,128)(2,1)} %get-tuple-element.67.gate) | copy-start | bytes 786436
  97.1 17.1 %copy-start.1 = (bf16[16,2048]{1,0:T(8,128)(2,1)S(1)}, bf16[16,2048]{1,0:T(8,128)(2,1)}, u32[]{:S(2)}) copy-start(bf16[16,2048]{1,0:T(8,128)(2,1)} %down.3) | copy-start | bytes 196612
  97.1 17.1 %copy-start.3 = (bf16[16,128]{1,0:T(8,128)(2,1)S(1)}, bf16[16,128]{1,0:T(8,128)(2,1)}, u32[]{:S(2)}) copy-start(bf16[16,128]{1,0:T(8,128)(2,1)} %get-tuple-element.66.lat) | copy-start | bytes 12292
  97.1 3.9 %collective-permute-start.7 = (bf16[256,256]{1,0:T(8,128)(2,1)S(1)}, bf16[256,256]{1,0:T(8,128)(2,1)S(1)}, u32[]{:S(2)}, u32[]{:S(2)}) collective-permute-start(bf16[256,256]{1,0:T(8,128)(2,1)S(1)} %get-tuple-element.81), channel_id=1, source_target_pairs={{0,32},{32,0},{64,96},{96,64},{128,160},{160,128},{192,224},{224,1... | collective-permute-start | bytes 393224 | tf_op jit(solution)/shard_map/ppermute | solution.py:447
  101.0 0.7 copy-start.15
  105.4 8.7 %collective-permute-start.8 = (f32[128,2048]{1,0:T(8,128)}, f32[128,2048]{1,0:T(8,128)S(1)}, u32[]{:S(2)}, u32[]{:S(2)}) collective-permute-start(f32[128,2048]{1,0:T(8,128)} %get-tuple-element.63), channel_id=1, source_target_pairs={{0,1},{1,0},{2,3},{3,2},{4,5},{5,4},{6,7},{7,6},{8,9},{9,8},{10,11... | collective-permute-start | bytes 3145736 | tf_op jit(solution)/shard_map/ppermute | solution.py:438
  108.3 2.2 %collective-permute-start.12 = (bf16[128,256]{1,0:T(8,128)(2,1)S(1)}, bf16[128,256]{1,0:T(8,128)(2,1)S(1)}, u32[]{:S(2)}, u32[]{:S(2)}) collective-permute-start(bf16[128,256]{1,0:T(8,128)(2,1)S(1)} %get-tuple-element.69), channel_id=1, source_target_pairs={{0,1},{1,0},{2,3},{3,2},{4,5},{5,4},{6,7},{7,6},{8,9},{9,8},{10,11... | collective-permute-start | bytes 196616 | tf_op jit(solution)/shard_map/ppermute | solution.py:438
  108.4 3.5 %collective-permute-start.13 = (bf16[128,256]{1,0:T(8,128)(2,1)S(1)}, bf16[128,256]{1,0:T(8,128)(2,1)S(1)}, u32[]{:S(2)}, u32[]{:S(2)}) collective-permute-start(bf16[128,256]{1,0:T(8,128)(2,1)S(1)} %get-tuple-element.70), channel_id=1, source_target_pairs={{0,32},{32,0},{64,96},{96,64},{128,160},{160,128},{192,224},{224,1... | collective-permute-start | bytes 196616 | tf_op jit(solution)/shard_map/ppermute | solution.py:447
  109.2 5.0 %collective-permute-start.14 = (bf16[128,256]{1,0:T(8,128)(2,1)S(1)}, bf16[128,256]{1,0:T(8,128)(2,1)S(1)}, u32[]{:S(2)}, u32[]{:S(2)}) collective-permute-start(bf16[128,256]{1,0:T(8,128)(2,1)S(1)} %get-tuple-element.71), channel_id=1, source_target_pairs={{0,33},{1,32},{32,1},{33,0},{64,97},{65,96},{96,65},{97,64},{128,1... | collective-permute-start | bytes 196616 | tf_op jit(solution)/shard_map/ppermute | solution.py:443
  114.2 1.2 copy-start
  132.0 5.4 %collective-permute-start.15 = (f32[16,2048]{1,0:T(8,128)S(1)}, f32[16,2048]{1,0:T(8,128)S(1)}, u32[]{:S(2)}, u32[]{:S(2)}) collective-permute-start(f32[16,2048]{1,0:T(8,128)S(1)} %get-tuple-element.77), channel_id=1, source_target_pairs={{0,1},{1,0},{2,3},{3,2},{4,5},{5,4},{6,7},{7,6},{8,9},{9,8},{10,11... | collective-permute-start | bytes 393224 | tf_op jit(solution)/shard_map/ppermute | solution.py:438
